TPU v7x, 32 devices: a whole 2x2x4 slice. The times are simulated.
32 devices in a mesh: groups: 2 (over x), rows: 16 (over z, y, core).
Axes of the slice: x: 2, y: 2, z: 4, core: 2. Of those that a mesh axis runs over, the one named last changes fastest.
Arguments:
- frame_maps: bfloat16 [64, 2, 48, 64, 128], P(('groups', 'rows')), parts along dimension 0, may hold values from -6 to 6
- net_state: bfloat16 [128, 48, 64, 128], P(('groups', 'rows')), parts along dimension 0, may hold values from -3 to 3
- edges: int32 [128, 2], P('groups'), parts along dimension 0, may hold values from 0 to 31, as said below
- offsets: int32 [128, 2], P(('groups', 'rows')), parts along dimension 0, may hold values from -8 to 8
- w_motion: bfloat16 [81, 128], replicated, may hold values from -0.625 to 0.625
- w_input: bfloat16 [256, 384], replicated, may hold values from -0.375 to 0.375
- w_gates: bfloat16 [1152, 256], replicated, may hold values from -0.1875 to 0.1875
- w_candidate: bfloat16 [1152, 128], replicated, may hold values from -0.1875 to 0.1875
- w_aggregate: bfloat16 [1152, 128], replicated, may hold values from -0.1875 to 0.1875
Outputs:
- new_state: bfloat16 [128, 48, 64, 128], P(('groups', 'rows')), parts along dimension 0
- frame_update: bfloat16 [64, 48, 64, 128], P(('groups', 'rows')), parts along dimension 0
There are 2 independent parts, one for each index of `groups`. A program takes and returns all parts, laid end to end along the dimension named above; an argument that names none is the same for every part. Nothing has to cross between parts.
Inputs may be any that keep to these rules, and one draw needn't show every extreme that they name: `edges`: edge e lies with the frames of index k = e // 4 of rows (frames k * 2 to (k + 1) * 2 - 1); its source and target are frames of indices k - 1, k or k + 1, and differ.
All inputs are finite; a program needn't handle non-finite values.
Results may differ from a plain program's by a relative error of at most 0.006.
Values may be sent and summed in bfloat16 or wider, within the bound.
No kernel may reach another device: no remote copies, remote signals or barrier semaphores. Data moves between devices by JAX's collectives and lax.ppermute only.
A program may use at most 128 MiB of HBM per device.

v0:
```python
import jax
import jax.numpy as jnp
from jax import lax
from jax.sharding import PartitionSpec as P

RADIUS = 4
SHIFT = 8


def with_halo(cells, sides, width):
    for axis, dim in sides:
        count = lax.axis_size(axis)
        ends = count - 1
        head = lax.slice_in_dim(cells, 0, width, axis=dim)
        tail = lax.slice_in_dim(cells, cells.shape[dim] - width, cells.shape[dim], axis=dim)
        cells = jnp.concatenate(
            [
                lax.ppermute(tail, axis, [(i, (i + 1) % count) for i in range(ends)]),
                cells,
                lax.ppermute(head, axis, [((i + 1) % count, i) for i in range(ends)]),
            ],
            axis=dim,
        )
    return cells


def from_behind(block, axis, distance):
    devices = range(lax.axis_size(axis))
    route = [(i - distance, i) for i in devices if i - distance in devices]
    return lax.ppermute(block, axis, route)


def conv_columns(field):
    height, width_px, chans = field.shape
    padded = jnp.pad(field, ((1, 1), (1, 1), (0, 0)))
    pieces = [
        padded[row_step : row_step + height, col_step : col_step + width_px, :]
        for row_step in range(3)
        for col_step in range(3)
    ]
    return jnp.concatenate(pieces, axis=-1).reshape(height * width_px, 9 * chans)


def correlate(source_feat, target_feat, offset_pair):
    height, width_px, chans = source_feat.shape
    margin = SHIFT + RADIUS
    span = 2 * RADIUS + 1
    wide = width_px + span - 1
    padded = jnp.pad(target_feat, ((margin, margin), (margin, margin), (0, 0)))
    start_row = SHIFT + offset_pair[0]
    start_col = SHIFT + offset_pair[1]
    window = lax.dynamic_slice(
        padded, (start_row, start_col, jnp.int32(0)), (height + span - 1, wide, chans)
    )
    stacked = jnp.stack([window[row_step : row_step + height] for row_step in range(span)], axis=1)
    scores = jnp.einsum("hwc,havc->hawv", source_feat, stacked, preferred_element_type=jnp.float32)
    flat = scores.reshape(height, span, width_px * wide)
    flat = jnp.pad(flat, ((0, 0), (0, 0), (0, width_px)))
    band = flat.reshape(height, span, width_px, wide + 1)[:, :, :, :span]
    volume = jnp.transpose(band, (1, 3, 0, 2))
    return (volume.reshape(span * span, height * width_px) * chans ** (-0.5)).astype(jnp.bfloat16)


def edge_update(
    source_feat, target_feat, context, state, offset_pair, w_motion, w_input, w_gates, w_candidate
):
    height, width_px, chans = state.shape
    volume = correlate(source_feat, target_feat, offset_pair)
    motion = jax.nn.relu(
        jnp.einsum("kp,kc->pc", volume, w_motion, preferred_element_type=jnp.float32)
    ).astype(jnp.bfloat16)
    flat_ctx = context.reshape(height * width_px, chans)
    flat_state = state.reshape(height * width_px, chans).astype(jnp.float32)
    inputs = jnp.dot(motion, w_input[:chans], preferred_element_type=jnp.float32) + jnp.dot(
        flat_ctx, w_input[chans:], preferred_element_type=jnp.float32
    )
    gates = jnp.dot(conv_columns(state), w_gates, preferred_element_type=jnp.float32)
    update_gate = jax.nn.sigmoid(gates[:, :chans] + inputs[:, :chans])
    reset_gate = jax.nn.sigmoid(gates[:, chans:] + inputs[:, chans : 2 * chans])
    reset_state = (reset_gate * flat_state).astype(jnp.bfloat16).reshape(height, width_px, chans)
    candidate = jnp.tanh(
        jnp.dot(conv_columns(reset_state), w_candidate, preferred_element_type=jnp.float32)
        + inputs[:, 2 * chans :]
    )
    fresh = (1.0 - update_gate) * flat_state + update_gate * candidate
    return fresh.astype(jnp.bfloat16).reshape(height, width_px, chans)


def aggregate(mean_map, w_aggregate):
    height, width_px, chans = mean_map.shape
    return (
        jnp.dot(conv_columns(mean_map), w_aggregate, preferred_element_type=jnp.float32)
        .astype(jnp.bfloat16)
        .reshape(height, width_px, chans)
    )


def per_device(
    frame_maps, net_state, edges, offsets, w_motion, w_input, w_gates, w_candidate, w_aggregate
):
    frame_count = frame_maps.shape[0]
    edge_count = net_state.shape[0]
    my_position = lax.axis_index("rows")
    window = with_halo(frame_maps, (("rows", 0),), frame_count)
    first_frame = (my_position - 1) * frame_count
    my_edges = lax.dynamic_slice_in_dim(edges, my_position * edge_count, edge_count, 0)
    source_local = my_edges[:, 0] - first_frame
    target_local = my_edges[:, 1] - first_frame

    def one_edge(item):
        source_id, target_id, shift_pair, state = item
        source_pair = lax.dynamic_index_in_dim(window, source_id, 0, keepdims=False)
        target_pair = lax.dynamic_index_in_dim(window, target_id, 0, keepdims=False)
        return edge_update(
            source_pair[0],
            target_pair[0],
            source_pair[1],
            state,
            shift_pair,
            w_motion,
            w_input,
            w_gates,
            w_candidate,
        )

    new_state = lax.map(one_edge, (source_local, target_local, offsets, net_state))
    filler = jnp.full((edge_count,), -1, jnp.int32)
    padded_sources = jnp.concatenate([filler, edges[:, 0], filler])
    nearby_sources = lax.dynamic_slice_in_dim(
        padded_sources, my_position * edge_count, 3 * edge_count, 0
    )
    relative = nearby_sources - my_position * frame_count
    frame_slots = jnp.arange(frame_count, dtype=jnp.int32)
    selector = relative[None, :] == frame_slots[:, None]
    counts = jnp.sum(selector.astype(jnp.float32), axis=1)
    window_slots = jnp.arange(3 * frame_count, dtype=jnp.int32)
    window_selector = (window_slots[:, None] == source_local[None, :]).astype(jnp.bfloat16)
    window_sums = jnp.einsum(
        "fe,ehwc->fhwc", window_selector, new_state, preferred_element_type=jnp.float32
    ).astype(jnp.bfloat16)
    from_below = from_behind(window_sums[2 * frame_count :], "rows", 1)
    from_above = from_behind(window_sums[:frame_count], "rows", -1)
    sums = (
        window_sums[frame_count : 2 * frame_count].astype(jnp.float32)
        + from_below.astype(jnp.float32)
        + from_above.astype(jnp.float32)
    )
    mean_state = (sums / jnp.maximum(counts, 1.0)[:, None, None, None]).astype(jnp.bfloat16)

    def one_frame(mean_map):
        return aggregate(mean_map, w_aggregate)

    frame_update = lax.map(one_frame, mean_state)
    return (new_state, frame_update)


def solution(mesh):
    in_specs = (
        P(("groups", "rows"), None, None, None, None),
        P(("groups", "rows"), None, None, None),
        P("groups", None),
        P(("groups", "rows"), None),
        P(),
        P(),
        P(),
        P(),
        P(),
    )
    out_specs = (P(("groups", "rows"), None, None, None), P(("groups", "rows"), None, None, None))
    return jax.shard_map(
        per_device, mesh=mesh, in_specs=in_specs, out_specs=out_specs, check_vma=False
    )
```

profile of v0, /device:TPU:1, one launch (start us, length us, event | category | flops | bytes accessed | tf_op | source)
XLA Modules:
  0.0 696.3 jit_solution(2461550109323962633)
XLA Ops:
  7.9 65.5 %collective-permute-done = bf16[2,2,48,64,128]{4,3,2,1,0:T(8,128)(2,1)} collective-permute-done((bf16[2,2,48,64,128]{4,3,2,1,0:T(8,128)(2,1)}, bf16[2,2,48,64,128]{4,3,2,1,0:T(8,128)(2,1)}, u32[]{:S(2)}, u32[]{:S(2)}) %collective-permute-start) | collective-permute-done | bytes 3145760 | tf_op jit(solution)/shard_map/ppermute | solution.py:18
  82.5 541.6 %while.24 = (s32[]{:T(128)}, bf16[4,48,64,128]{3,2,1,0:T(8,128)(2,1)}, bf16[4,48,64,128]{3,2,1,0:T(8,128)(2,1)}, bf16[1152,256]{1,0:T(8,128)(2,1)S(1)}, s32[4]{0...) while((s32[]{:T(128)}, ...), condition=%wide.region_1.2_spmd, body=%wide.region_0.1_spmd.sunk | while | flops 3904739328 | bytes 207082672 | solution.py:126
  107.2 14.8 %convolution_bitcast_fusion.2 = f32[48,9,64,72]{3,2,1,0:T(8,128)} fusion(bf16[48,9,72,128]{3,2,1,0:T(8,128)(2,1)} %fusion.109, bf16[6,2,48,64,128]{4,3,2,1,0:T(8,128)(2,1)} %get-tuple-element.476, s32[]{:T(128)S(6)} %select_n.39), kind=kOutput, calls=%fused_computation.2.clone.1 | convolution fusion | flops 509607936 | bytes 16711684 | tf_op jit(solution)/shard_map/while/body/eval_jaxpr/hwc,havc->hawv/dot_general | solution.py:56
  122.1 18.2 %reshape.183 = f32[48,9,4608]{2,1,0:T(8,128)} reshape(f32[48,9,64,72]{3,2,1,0:T(8,128)} %convolution_bitcast_fusion.2) | data formatting | bytes 15925248 | tf_op jit(solution)/shard_map/while/body/eval_jaxpr/reshape | solution.py:57
  140.3 9.6 %copy.52 = f32[48,9,4608]{2,0,1:T(8,128)S(1)} copy(f32[48,9,4608]{2,1,0:T(8,128)} %reshape.183) | data formatting | bytes 15925248 | tf_op jit(solution)/shard_map/while/body/eval_jaxpr/reshape | solution.py:57
  153.7 24.8 %reshape.184 = f32[48,9,64,73]{3,2,0,1:T(8,128)} reshape(f32[48,9,4672]{2,0,1:T(8,128)} %pad.138) | data formatting | bytes 16146432 | tf_op jit(solution)/shard_map/while/body/eval_jaxpr/reshape | solution.py:59
  178.5 10.0 %fusion.110 = bf16[9,9,48,64]{1,3,2,0:T(8,128)(2,1)} fusion(f32[48,9,64,73]{3,2,0,1:T(8,128)} %reshape.184), kind=kLoop, calls=%fused_computation.3.clone.1 | loop fusion | flops 497664 | bytes 1492992 | tf_op jit(solution)/shard_map/while/body/eval_jaxpr/convert_element_type | solution.py:61
  240.9 14.8 %convolution_bitcast_fusion.2 = f32[48,9,64,72]{3,2,1,0:T(8,128)} fusion(bf16[48,9,72,128]{3,2,1,0:T(8,128)(2,1)} %fusion.109, bf16[6,2,48,64,128]{4,3,2,1,0:T(8,128)(2,1)} %get-tuple-element.476, s32[]{:T(128)S(6)} %select_n.39), kind=kOutput, calls=%fused_computation.2.clone.1 | convolution fusion | flops 509607936 | bytes 16711684 | tf_op jit(solution)/shard_map/while/body/eval_jaxpr/hwc,havc->hawv/dot_general | solution.py:56
  255.8 18.2 %reshape.183 = f32[48,9,4608]{2,1,0:T(8,128)} reshape(f32[48,9,64,72]{3,2,1,0:T(8,128)} %convolution_bitcast_fusion.2) | data formatting | bytes 15925248 | tf_op jit(solution)/shard_map/while/body/eval_jaxpr/reshape | solution.py:57
  274.0 9.6 %copy.52 = f32[48,9,4608]{2,0,1:T(8,128)S(1)} copy(f32[48,9,4608]{2,1,0:T(8,128)} %reshape.183) | data formatting | bytes 15925248 | tf_op jit(solution)/shard_map/while/body/eval_jaxpr/reshape | solution.py:57
  287.4 24.8 %reshape.184 = f32[48,9,64,73]{3,2,0,1:T(8,128)} reshape(f32[48,9,4672]{2,0,1:T(8,128)} %pad.138) | data formatting | bytes 16146432 | tf_op jit(solution)/shard_map/while/body/eval_jaxpr/reshape | solution.py:59
  312.2 10.0 %fusion.110 = bf16[9,9,48,64]{1,3,2,0:T(8,128)(2,1)} fusion(f32[48,9,64,73]{3,2,0,1:T(8,128)} %reshape.184), kind=kLoop, calls=%fused_computation.3.clone.1 | loop fusion | flops 497664 | bytes 1492992 | tf_op jit(solution)/shard_map/while/body/eval_jaxpr/convert_element_type | solution.py:61
  374.6 14.8 %convolution_bitcast_fusion.2 = f32[48,9,64,72]{3,2,1,0:T(8,128)} fusion(bf16[48,9,72,128]{3,2,1,0:T(8,128)(2,1)} %fusion.109, bf16[6,2,48,64,128]{4,3,2,1,0:T(8,128)(2,1)} %get-tuple-element.476, s32[]{:T(128)S(6)} %select_n.39), kind=kOutput, calls=%fused_computation.2.clone.1 | convolution fusion | flops 509607936 | bytes 16711684 | tf_op jit(solution)/shard_map/while/body/eval_jaxpr/hwc,havc->hawv/dot_general | solution.py:56
  389.5 18.2 %reshape.183 = f32[48,9,4608]{2,1,0:T(8,128)} reshape(f32[48,9,64,72]{3,2,1,0:T(8,128)} %convolution_bitcast_fusion.2) | data formatting | bytes 15925248 | tf_op jit(solution)/shard_map/while/body/eval_jaxpr/reshape | solution.py:57
  407.7 9.6 %copy.52 = f32[48,9,4608]{2,0,1:T(8,128)S(1)} copy(f32[48,9,4608]{2,1,0:T(8,128)} %reshape.183) | data formatting | bytes 15925248 | tf_op jit(solution)/shard_map/while/body/eval_jaxpr/reshape | solution.py:57
  421.1 24.8 %reshape.184 = f32[48,9,64,73]{3,2,0,1:T(8,128)} reshape(f32[48,9,4672]{2,0,1:T(8,128)} %pad.138) | data formatting | bytes 16146432 | tf_op jit(solution)/shard_map/while/body/eval_jaxpr/reshape | solution.py:59
  445.9 10.0 %fusion.110 = bf16[9,9,48,64]{1,3,2,0:T(8,128)(2,1)} fusion(f32[48,9,64,73]{3,2,0,1:T(8,128)} %reshape.184), kind=kLoop, calls=%fused_computation.3.clone.1 | loop fusion | flops 497664 | bytes 1492992 | tf_op jit(solution)/shard_map/while/body/eval_jaxpr/convert_element_type | solution.py:61
  508.3 14.9 %convolution_bitcast_fusion.2 = f32[48,9,64,72]{3,2,1,0:T(8,128)} fusion(bf16[48,9,72,128]{3,2,1,0:T(8,128)(2,1)} %fusion.109, bf16[6,2,48,64,128]{4,3,2,1,0:T(8,128)(2,1)} %get-tuple-element.476, s32[]{:T(128)S(6)} %select_n.39), kind=kOutput, calls=%fused_computation.2.clone.1 | convolution fusion | flops 509607936 | bytes 16711684 | tf_op jit(solution)/shard_map/while/body/eval_jaxpr/hwc,havc->hawv/dot_general | solution.py:56
  523.2 18.2 %reshape.183 = f32[48,9,4608]{2,1,0:T(8,128)} reshape(f32[48,9,64,72]{3,2,1,0:T(8,128)} %convolution_bitcast_fusion.2) | data formatting | bytes 15925248 | tf_op jit(solution)/shard_map/while/body/eval_jaxpr/reshape | solution.py:57
  541.4 9.6 %copy.52 = f32[48,9,4608]{2,0,1:T(8,128)S(1)} copy(f32[48,9,4608]{2,1,0:T(8,128)} %reshape.183) | data formatting | bytes 15925248 | tf_op jit(solution)/shard_map/while/body/eval_jaxpr/reshape | solution.py:57
  554.8 24.8 %reshape.184 = f32[48,9,64,73]{3,2,0,1:T(8,128)} reshape(f32[48,9,4672]{2,0,1:T(8,128)} %pad.138) | data formatting | bytes 16146432 | tf_op jit(solution)/shard_map/while/body/eval_jaxpr/reshape | solution.py:59
  579.6 10.0 %fusion.110 = bf16[9,9,48,64]{1,3,2,0:T(8,128)(2,1)} fusion(f32[48,9,64,73]{3,2,0,1:T(8,128)} %reshape.184), kind=kLoop, calls=%fused_computation.3.clone.1 | loop fusion | flops 497664 | bytes 1492992 | tf_op jit(solution)/shard_map/while/body/eval_jaxpr/convert_element_type | solution.py:61
  642.7 32.3 %collective-permute-done.2 = bf16[2,48,64,128]{3,0,2,1:T(2,128)(2,1)S(1)} collective-permute-done((bf16[2,48,64,128]{3,0,2,1:T(2,128)(2,1)}, bf16[2,48,64,128]{3,0,2,1:T(2,128)(2,1)S(1)}, u32[]{:S(2)}, u32[]{:S(2)}) %collective-permute-start.2) | collective-permute-done | bytes 1572896 | tf_op jit(solution)/shard_map/ppermute | solution.py:30
  681.6 13.3 %while.25 = (s32[]{:T(128)}, bf16[2,48,64,128]{3,2,1,0:T(8,128)(2,1)S(1)}, bf16[2,48,64,128]{3,2,1,0:T(8,128)(2,1)S(1)}, bf16[1152,128]{1,0:T(8,128)(2,1)S(1)}, s32[]{:T(128)}) while((s32[]{:T(128)}, bf16[2,48,64,128]{3,2,1,0:T(8,128)(2,1)S(1)}, bf16[2,48,64,128]{3,2,1,0:T(8,128)(2,1)S(1)}, bf16[1152,128]{1,0:T(8,128)(2,1)S(1)}, ...), condition=%wide.region_4.5_spmd, body=%wide.region_3.4_spmd.sunk | while | flops 906362880 | bytes 34111560 | solution.py:153
  (257 shorter events, 255.0 us)
Async XLA Ops:
  0.6 72.8 %collective-permute-start = (bf16[2,2,48,64,128]{4,3,2,1,0:T(8,128)(2,1)}, bf16[2,2,48,64,128]{4,3,2,1,0:T(8,128)(2,1)}, u32[]{:S(2)}, u32[]{:S(2)}) collective-permute-start(bf16[2,2,48,64,128]{4,3,2,1,0:T(8,128)(2,1)} %param.13), channel_id=1, source_target_pairs={{0,1},{1,2},{2,3},{3,4},{4,5},{5,6},{6,7},{7,8},{8,9},{9,10},{10,1... | collective-permute-start | bytes 9437192 | tf_op jit(solution)/shard_map/ppermute | solution.py:18
  5.2 68.2 %collective-permute-start.1 = (bf16[2,2,48,64,128]{4,3,2,1,0:T(8,128)(2,1)}, bf16[2,2,48,64,128]{4,3,2,1,0:T(8,128)(2,1)}, u32[]{:S(2)}, u32[]{:S(2)}) collective-permute-start(bf16[2,2,48,64,128]{4,3,2,1,0:T(8,128)(2,1)} %param.13), channel_id=1, source_target_pairs={{1,0},{2,1},{3,2},{4,3},{5,4},{6,5},{7,6},{8,7},{9,8},{10,9},{11,1... | collective-permute-start | bytes 9437192 | tf_op jit(solution)/shard_map/ppermute | solution.py:20
  7.9 74.6 %copy-start.2 = (bf16[256,384]{1,0:T(8,128)(2,1)S(1)}, bf16[256,384]{1,0:T(8,128)(2,1)}, u32[]{:S(2)}) copy-start(bf16[256,384]{1,0:T(8,128)(2,1)} %param.18) | copy-start | bytes 589828
  7.9 74.6 %copy-start.3 = (bf16[81,128]{1,0:T(8,128)(2,1)S(1)}, bf16[81,128]{1,0:T(8,128)(2,1)}, u32[]{:S(2)}) copy-start(bf16[81,128]{1,0:T(8,128)(2,1)} %param.17) | copy-start | bytes 62212
  7.9 74.6 %copy-start.4 = (s32[4,2]{0,1:T(2,128)S(1)}, s32[4,2]{0,1:T(2,128)}, u32[]{:S(2)}) copy-start(s32[4,2]{0,1:T(2,128)} %param.16) | copy-start | bytes 100
  7.9 74.6 %copy-start.8 = (bf16[1152,256]{1,0:T(8,128)(2,1)S(1)}, bf16[1152,256]{1,0:T(8,128)(2,1)}, u32[]{:S(2)}) copy-start(bf16[1152,256]{1,0:T(8,128)(2,1)} %param.19) | copy-start | bytes 1769476
  7.9 74.6 %copy-start.9 = (bf16[1152,128]{1,0:T(8,128)(2,1)S(1)}, bf16[1152,128]{1,0:T(8,128)(2,1)}, u32[]{:S(2)}) copy-start(bf16[1152,128]{1,0:T(8,128)(2,1)} %param.20) | copy-start | bytes 884740
  198.5 3.3 copy-start
  332.2 3.3 copy-start
  465.9 3.3 copy-start
  599.6 3.3 copy-start
  624.1 18.4 %copy-start.5 = (s32[64,2]{0,1:T(2,128)S(1)}, s32[64,2]{0,1:T(2,128)}, u32[]{:S(2)}) copy-start(s32[64,2]{0,1:T(2,128)} %param.15) | copy-start | bytes 1540
  629.3 2.7 copy-start.1
  631.9 49.6 %copy-start.10 = (bf16[1152,128]{1,0:T(8,128)(2,1)S(1)}, bf16[1152,128]{1,0:T(8,128)(2,1)}, u32[]{:S(2)}) copy-start(bf16[1152,128]{1,0:T(8,128)(2,1)} %param.21) | copy-start | bytes 884740
  636.1 38.9 %collective-permute-start.2 = (bf16[2,48,64,128]{3,0,2,1:T(2,128)(2,1)}, bf16[2,48,64,128]{3,0,2,1:T(2,128)(2,1)S(1)}, u32[]{:S(2)}, u32[]{:S(2)}) collective-permute-start(bf16[2,48,64,128]{3,0,2,1:T(2,128)(2,1)} %get-tuple-element.267), channel_id=1, source_target_pairs={{0,1},{1,2},{2,3},{3,4},{4,5},{5,6},{6,7},{7,8},{8,9},{9,10},{10,1... | collective-permute-start | bytes 4718600 | tf_op jit(solution)/shard_map/ppermute | solution.py:30
  640.5 34.5 %collective-permute-start.3 = (bf16[2,48,64,128]{3,0,2,1:T(2,128)(2,1)S(1)}, bf16[2,48,64,128]{3,0,2,1:T(2,128)(2,1)}, u32[]{:S(2)}, u32[]{:S(2)}) collective-permute-start(bf16[2,48,64,128]{3,0,2,1:T(2,128)(2,1)S(1)} %get-tuple-element.268), channel_id=1, source_target_pairs={{1,0},{2,1},{3,2},{4,3},{5,4},{6,5},{7,6},{8,7},{9,8},{10,9},{11,1... | collective-permute-start | bytes 4718600 | tf_op jit(solution)/shard_map/ppermute | solution.py:30
  675.0 6.6 copy-start.6
  694.9 1.1 copy-start.7
where the time goes:
time: 700 us; the launch traced here: 696 us
  local copies, waits for them, and re-layouts  381 us (54%)
  matrix products  113 us (16%)
  waiting for transfers between devices  97.7 us (14%)
  other arithmetic  57.2 us (8%)
  loops' own time  33 us (5%)
  starting transfers between devices  12.8 us (2%)
    reshape x8, local copies, waits for them, and re-layouts, correlate(): flat = scores.reshape(height, span, width_px * wide)  111 us
    reshape x4, local copies, waits for them, and re-layouts, correlate(): band = flat.reshape(height, span, width_px, wide + 1)[:, :, :, :span]  99 us
    while x120, local copies, waits for them, and re-layouts  68.4 us
    ppermute x1, waiting for transfers between devices, with_halo(): lax.ppermute(tail, axis, [(i, (i + 1) % count) for i in range(ends)])  65.5 us
    dot_general x4, matrix products, correlate(): jnp.einsum('hwc,havc->hawv', source_feat, stacked, preferred_element_type...  59.4 us
    convert_element_type x4, other arithmetic, correlate(): (volume.reshape(span * span, height * width_px) * chans ** (-0.5)).astype...  39.8 us
    another operation x1, loops' own time, per_device(): lax.map(one_edge, (source_local, target_local, offsets, net_state))  32.8 us
    ppermute x2, waiting for transfers between devices, from_behind(): return lax.ppermute(block, axis, route)  32.3 us
  transfers between devices with their start and end apart: 4, of which 2 were waited for; matrix products, arithmetic and copies ran while one was open for 0% of the time, Pallas kernels for 0%

commit v1 on v0

v1 whole, which is shorter than its diff:
```python
import functools

import jax
import jax.numpy as jnp
from jax import lax
from jax.experimental import pallas as pl
from jax.experimental.pallas import tpu as pltpu
from jax.sharding import PartitionSpec as P

RADIUS = 4
SHIFT = 8
SPAN = 2 * RADIUS + 1
MARGIN = SHIFT + RADIUS
F32 = jnp.float32
BF16 = jnp.bfloat16
VMEM_LIMIT = 56 << 20


def any_spec():
    return pl.BlockSpec(memory_space=pl.ANY)


def whole(array):
    return pl.BlockSpec(array.shape, lambda *_: (0,) * array.ndim)


def fetch(cases, dst, sem):
    for condition, src in cases:

        @pl.when(condition)
        def _(src=src):
            pltpu.make_async_copy(src, dst, sem).start()


def await_copy(dst, sem):
    pltpu.make_async_copy(dst, dst, sem).wait()


def neighbours(block):
    rows, width, chans = block.shape
    flat = block.reshape(rows * width, chans)
    x = lax.broadcasted_iota(jnp.int32, (rows, width, chans), 1).reshape(rows * width, chans)
    left = jnp.where(x == 0, 0.0, pltpu.roll(flat, 1, 0)).astype(BF16)
    right = jnp.where(x == width - 1, 0.0, pltpu.roll(flat, rows * width - 1, 0)).astype(BF16)
    return [side.reshape(rows, width, chans) for side in (left, flat.astype(BF16), right)]


def put_columns(columns, start, block):
    chans = block.shape[-1]
    rows = block.shape[0]
    for i, side in enumerate(neighbours(block)):
        columns[pl.ds(start, rows), :, i * chans : (i + 1) * chans] = side


def conv_rows(columns, start, rows, weights):
    width, depth = columns.shape[1:]
    taps = [columns[pl.ds(start + step, rows)].reshape(rows * width, depth) for step in range(3)]
    return jnp.dot(jnp.concatenate(taps, axis=1), weights, preferred_element_type=F32)


def sigmoid(v):
    return 0.5 * jnp.tanh(0.5 * v) + 0.5


def gates_kernel(state_ref, weights_ref, out_ref, columns):
    height, width, chans = state_ref.shape[1:]
    edge_row = jnp.zeros((1,) + columns.shape[1:], BF16)
    columns[0:1] = edge_row
    columns[height + 1 :] = edge_row
    step = 8
    for y in range(0, height, step):
        put_columns(columns, y + 1, state_ref[0, y : y + step].astype(F32))
    weights = weights_ref[...]
    for y in range(0, height, step):
        gates = conv_rows(columns, y, step, weights)
        out_ref[0, y : y + step] = gates.astype(BF16).reshape(step, width, weights.shape[1])


def gates_of(state, weights):
    edges, height, width, chans = state.shape
    outs = weights.shape[1]
    return pl.pallas_call(
        gates_kernel,
        grid=(edges,),
        in_specs=[pl.BlockSpec((1, height, width, chans), lambda e: (e, 0, 0, 0)), whole(weights)],
        out_specs=pl.BlockSpec((1, height, width, outs), lambda e: (e, 0, 0, 0)),
        out_shape=jax.ShapeDtypeStruct((edges, height, width, outs), BF16),
        scratch_shapes=[pltpu.VMEM((height + 2, width, 3 * chans), BF16)],
        compiler_params=pltpu.CompilerParams(vmem_limit_bytes=VMEM_LIMIT),
        cost_estimate=pl.CostEstimate(
            flops=2 * edges * height * width * 9 * chans * outs,
            bytes_accessed=2 * edges * height * width * (chans + outs),
            transcendentals=0,
        ),
        name="gates",
    )(state, weights)


def motion_kernel(meta, own, near, far, flip_ref, mask_ref, base_ref, out_ref, src_buf, raw_buf, tgt_buf, w_buf, sems):
    edge = pl.program_id(0)
    edges = pl.num_programs(0)
    height, width, chans = own.shape[2:]
    slot = lax.rem(edge, 2)
    lanes = 2 * width
    tiles = base_ref.shape[0]

    def start(e, s):
        def cases(buf, frame):
            return ((buf == 0, own.at[frame, 0]), (buf == 1, far.at[frame]), (buf == 2, near.at[frame, 0]))

        fetch(cases(meta[e, 0], meta[e, 1]), src_buf.at[s, pl.ds(1, height)], sems.at[0, s])
        fetch(cases(meta[e, 2], meta[e, 3]), raw_buf.at[s], sems.at[1, s])

    @pl.when(edge == 0)
    def _():
        start(edge, slot)
        tgt_buf[0:MARGIN] = jnp.zeros((MARGIN, width, chans), BF16)
        below = tgt_buf.shape[0] - MARGIN - height
        tgt_buf[MARGIN + height :] = jnp.zeros((below, width, chans), BF16)

    @pl.when(edge + 1 < edges)
    def _():
        start(edge + 1, 1 - slot)

    oy, ox = meta[edge, 4], meta[edge, 5]
    for j in range(tiles):
        w_buf[j * lanes : (j + 1) * lanes] = pltpu.roll(base_ref[j], lax.rem(lanes - ox, lanes), 0).astype(BF16)

    await_copy(src_buf.at[slot, pl.ds(1, height)], sems.at[0, slot])
    await_copy(raw_buf.at[slot], sems.at[1, slot])

    flip = flip_ref[...]
    for y in range(0, height, 2):
        block = raw_buf[slot, y : y + 2].reshape(lanes, chans)
        turned = jnp.dot(flip, block, preferred_element_type=F32).astype(BF16)
        tgt_buf[MARGIN + y : MARGIN + y + 2] = turned.reshape(2, width, chans)

    mask = mask_ref[...]
    keep = mask != 0.0
    odd = lax.rem(oy + 2 * SHIFT, 2)
    weights = w_buf[...]
    unroll = 5

    @pl.loop(0, (height // 2 + unroll) // unroll)
    def _(i):
        starts = [2 * (i * unroll + u) - odd for u in range(unroll)]
        scores = []
        for y in starts:
            lhs = src_buf[slot, pl.ds(y + 1, 2)].reshape(lanes, chans)
            rhs = tgt_buf[pl.ds(y + oy - RADIUS + MARGIN, 2 * tiles)].reshape(tiles * lanes, chans)
            scores.append(lax.dot_general(lhs, rhs, (((1,), (1,)), ((), ())), preferred_element_type=F32))
        for y, pair in zip(starts, scores):
            volume = []
            for r in range(2):
                parts = []
                for j in range(tiles):
                    tile = pair[r * width : (r + 1) * width, j * lanes : (j + 1) * lanes] * (chans**-0.5)
                    tile = pltpu.roll(tile.astype(BF16), 0, 1, stride=1, stride_axis=0)
                    parts.append(jnp.where(keep, tile.astype(F32), 0.0).astype(BF16))
                volume.append(jnp.concatenate(parts, axis=1))
            res = jnp.dot(jnp.concatenate(volume, axis=0), weights, preferred_element_type=F32)
            out_ref[0, pl.ds(y + 1, 1)] = jnp.maximum(res[:width, :chans], 0.0).astype(BF16)[None]
            out_ref[0, pl.ds(y + 2, 1)] = jnp.maximum(res[width:, chans:], 0.0).astype(BF16)[None]


def motion_of(meta, own, near, far, w_motion):
    _, _, height, width, chans = own.shape
    edges = meta.shape[0]
    lanes = 2 * width
    rows = SPAN + 1
    taps = jnp.flip(w_motion.reshape(SPAN, SPAN, chans).astype(F32), axis=1)
    blank = jnp.zeros((1, SPAN, chans), F32)
    both = jnp.concatenate(
        [jnp.concatenate([taps, blank], axis=0), jnp.concatenate([blank, taps], axis=0)], axis=2
    )
    low = width - 1 - RADIUS
    padded = jnp.pad(both, ((0, 0), (0, lanes - SPAN), (0, 0))).reshape(rows // 2, 2, lanes, 2 * chans)
    base = jnp.roll(padded[:, 0], low, axis=1) + jnp.roll(padded[:, 1], low + width, axis=1)
    flip = jnp.kron(jnp.eye(2, dtype=F32), jnp.eye(width, dtype=F32)[::-1]).astype(BF16)
    x = jnp.arange(width)[:, None]
    lane = jnp.arange(lanes)[None]
    middle = (lane >= width // 2) & (lane < width + width // 2)
    inside = jnp.where(middle, (lane >= x) & (lane < x + width), jnp.where(lane < width, x > lane, lane >= x + width))
    mask = inside.astype(F32)
    buffer_rows = height + 4
    target_rows = height + 2 * MARGIN + 2
    return pl.pallas_call(
        motion_kernel,
        grid_spec=pltpu.PrefetchScalarGridSpec(
            num_scalar_prefetch=1,
            grid=(edges,),
            in_specs=[any_spec(), any_spec(), any_spec(), whole(flip), whole(mask), whole(base)],
            out_specs=pl.BlockSpec((1, buffer_rows, width, chans), lambda e, m: (e, 0, 0, 0)),
            scratch_shapes=[
                pltpu.VMEM((2, buffer_rows, width, chans), BF16),
                pltpu.VMEM((2, height, width, chans), BF16),
                pltpu.VMEM((target_rows, width, chans), BF16),
                pltpu.VMEM((rows * width, 2 * chans), BF16),
                pltpu.SemaphoreType.DMA((2, 2)),
            ],
        ),
        out_shape=jax.ShapeDtypeStruct((edges, buffer_rows, width, chans), BF16),
        compiler_params=pltpu.CompilerParams(vmem_limit_bytes=VMEM_LIMIT),
        cost_estimate=pl.CostEstimate(
            flops=8 * edges * height * width * chans * rows * width,
            bytes_accessed=6 * edges * height * width * chans,
            transcendentals=0,
        ),
        name="motion",
    )(meta, own, near, far, flip, mask, base)


def gru_kernel(
    first,
    last,
    split,
    meta,
    own,
    near,
    far_top,
    far_low,
    motion,
    gates,
    state,
    w_input,
    w_candidate,
    alias,
    new_ref,
    own_sum,
    near_sum,
    far_sum,
    ctx_buf,
    motion_buf,
    gates_buf,
    state_buf,
    columns,
    update_buf,
    drive_buf,
    totals,
    sems,
):
    edge = pl.program_id(0)
    edges = pl.num_programs(0)
    frames = own.shape[0]
    height, width, chans = own.shape[2:]
    slot = lax.rem(edge, 2)
    top = max(first - 1, 0)
    end = min(last + 1, height)
    rows = end - top

    def start(e, s):
        buf, frame = meta[e, 0], meta[e, 1]
        pltpu.make_async_copy(motion.at[e, pl.ds(top + 1, rows)], motion_buf.at[s], sems.at[1, s]).start()
        pltpu.make_async_copy(gates.at[e, pl.ds(top, rows)], gates_buf.at[s], sems.at[2, s]).start()
        pltpu.make_async_copy(state.at[e, pl.ds(top, rows)], state_buf.at[s], sems.at[3, s]).start()
        above = min(max(split - top, 0), rows)
        for piece, far, low, high, sem in ((0, far_top, 0, above, 0), (1, far_low, above, rows, 4)):
            if high > low:
                base = top + low
                fetch(
                    (
                        (buf == 0, own.at[frame, 1, pl.ds(base, high - low)]),
                        (buf == 1, far.at[frame, pl.ds(base - piece * split, high - low)]),
                        (buf == 2, near.at[frame, 1, pl.ds(base, high - low)]),
                    ),
                    ctx_buf.at[s, pl.ds(low, high - low)],
                    sems.at[sem, s],
                )

    def finish(s):
        await_copy(motion_buf.at[s], sems.at[1, s])
        await_copy(gates_buf.at[s], sems.at[2, s])
        await_copy(state_buf.at[s], sems.at[3, s])
        above = min(max(split - top, 0), rows)
        for low, high, sem in ((0, above, 0), (above, rows, 4)):
            if high > low:
                await_copy(ctx_buf.at[s, pl.ds(low, high - low)], sems.at[sem, s])

    @pl.when(edge == 0)
    def _():
        start(edge, slot)
        edge_row = jnp.zeros((1,) + columns.shape[1:], BF16)
        columns[0:1] = edge_row
        columns[rows + 1 :] = edge_row
        totals[...] = jnp.zeros(totals.shape, F32)

    @pl.when(edge + 1 < edges)
    def _():
        start(edge + 1, 1 - slot)

    finish(slot)

    weights = w_input[...]
    step = 5
    for y in range(0, rows, step):
        count = min(step, rows - y)
        span = slice(y, y + count)
        mixed = jnp.concatenate([motion_buf[slot, span], ctx_buf[slot, span]], axis=-1)
        inputs = jnp.dot(mixed.reshape(count * width, 2 * chans), weights, preferred_element_type=F32)
        inputs = inputs.reshape(count, width, 3 * chans)
        pre = gates_buf[slot, span].astype(F32)
        update_buf[span] = sigmoid(pre[..., :chans] + inputs[..., :chans])
        reset = sigmoid(pre[..., chans:] + inputs[..., chans : 2 * chans])
        drive_buf[span] = inputs[..., 2 * chans :]
        held = (reset * state_buf[slot, span].astype(F32)).astype(BF16).astype(F32)
        put_columns(columns, y + 1, held)

    weights = w_candidate[...]
    place = meta[edge, 0] * frames + meta[edge, 1]
    step = 8
    for y in range(first, last, step):
        count = min(step, last - y)
        span = slice(y - top, y - top + count)
        conv = conv_rows(columns, y - top, count, weights).reshape(count, width, chans)
        candidate = jnp.tanh(conv + drive_buf[span])
        update = update_buf[span]
        fresh = ((1.0 - update) * state_buf[slot, span].astype(F32) + update * candidate).astype(BF16)
        new_ref[0, y - first : y - first + count] = fresh
        totals[place, y - first : y - first + count] += fresh.astype(F32)

    @pl.when(edge == edges - 1)
    def _():
        for i, out in enumerate((own_sum, far_sum, near_sum)):
            out[...] = totals[i * frames : (i + 1) * frames].astype(BF16)


def gru_of(band, split, meta, own, near, far_top, far_low, motion, gates, state, w_input, w_candidate, earlier):
    frames, _, height, width, chans = own.shape
    edges = state.shape[0]
    size = height // 2
    first, last = band * size, (band + 1) * size
    rows = min(last + 1, height) - max(first - 1, 0)
    sums = jax.ShapeDtypeStruct((frames, size, width, chans), BF16)
    sum_spec = pl.BlockSpec(sums.shape, lambda e, m: (0, 0, 0, 0))
    body = functools.partial(gru_kernel, first, last, split)
    operands = [meta, own, near, far_top, far_low, motion, gates, state, w_input, w_candidate]
    if earlier is None:
        kernel = lambda *refs: body(*refs[:10], None, *refs[10:])
        aliases = {}
    else:
        kernel = body
        operands.append(earlier)
        aliases = {10: 0}
    return pl.pallas_call(
        kernel,
        grid_spec=pltpu.PrefetchScalarGridSpec(
            num_scalar_prefetch=1,
            grid=(edges,),
            in_specs=[any_spec()] * 7 + [whole(w_input), whole(w_candidate)] + [any_spec()] * (len(operands) - 10),
            out_specs=[pl.BlockSpec((1, size, width, chans), lambda e, m: (e, band, 0, 0)), sum_spec, sum_spec, sum_spec],
            scratch_shapes=[
                pltpu.VMEM((2, rows, width, chans), BF16),
                pltpu.VMEM((2, rows, width, chans), BF16),
                pltpu.VMEM((2, rows, width, 2 * chans), BF16),
                pltpu.VMEM((2, rows, width, chans), BF16),
                pltpu.VMEM((rows + 2, width, 3 * chans), BF16),
                pltpu.VMEM((rows, width, chans), F32),
                pltpu.VMEM((rows, width, chans), F32),
                pltpu.VMEM((3 * frames, size, width, chans), F32),
                pltpu.SemaphoreType.DMA((5, 2)),
            ],
        ),
        out_shape=[jax.ShapeDtypeStruct(state.shape, BF16), sums, sums, sums],
        input_output_aliases=aliases,
        compiler_params=pltpu.CompilerParams(vmem_limit_bytes=VMEM_LIMIT),
        cost_estimate=pl.CostEstimate(
            flops=2 * edges * rows * width * chans * (6 * chans + 9 * chans),
            bytes_accessed=2 * edges * rows * width * chans * 6,
            transcendentals=3 * edges * rows * width * chans,
        ),
        name=f"gru_band{band}",
    )(*operands)


def aggregate_kernel(counts, *refs):
    sums, weights_ref, out_ref, columns = refs[:-3], refs[-3], refs[-2], refs[-1]
    bands = [sums[i : i + 3] for i in range(0, len(sums), 3)]
    frame = pl.program_id(0)
    height, width, chans = out_ref.shape[1:]
    size = height // len(bands)
    edge_row = jnp.zeros((1,) + columns.shape[1:], BF16)
    columns[0:1] = edge_row
    columns[height + 1 :] = edge_row
    count = counts[frame]
    step = 8
    for band, (a, b, c) in enumerate(bands):
        for y in range(0, size, step):
            span = slice(y, y + step)
            total = a[0, span].astype(F32) + b[0, span].astype(F32) + c[0, span].astype(F32)
            mean = (total / count).astype(BF16).astype(F32)
            put_columns(columns, band * size + y + 1, mean)
    weights = weights_ref[...]
    for y in range(0, height, step):
        out = conv_rows(columns, y, step, weights)
        out_ref[0, y : y + step] = out.astype(BF16).reshape(step, width, chans)


def aggregate_of(counts, bands, weights):
    frames, size, width, chans = bands[0][0].shape
    height = size * len(bands)
    sums = [array for band in bands for array in band]
    return pl.pallas_call(
        aggregate_kernel,
        grid_spec=pltpu.PrefetchScalarGridSpec(
            num_scalar_prefetch=1,
            grid=(frames,),
            in_specs=[pl.BlockSpec((1, size, width, chans), lambda f, c: (f, 0, 0, 0))] * len(sums) + [whole(weights)],
            out_specs=pl.BlockSpec((1, height, width, chans), lambda f, c: (f, 0, 0, 0)),
            scratch_shapes=[pltpu.VMEM((height + 2, width, 3 * chans), BF16)],
        ),
        out_shape=jax.ShapeDtypeStruct((frames, height, width, chans), BF16),
        compiler_params=pltpu.CompilerParams(vmem_limit_bytes=VMEM_LIMIT),
        name="aggregate",
    )(counts, *sums, weights)


def per_device(
    frame_maps, net_state, edges, offsets, w_motion, w_input, w_gates, w_candidate, w_aggregate
):
    frames, _, height, width, chans = frame_maps.shape
    edge_count = net_state.shape[0]
    me = lax.axis_index("rows")
    count = lax.axis_size("rows")
    near_route = [(i, i ^ 1) for i in range(count)]
    far_route = [(i, i + 1 if i % 2 else i - 1) for i in range(1, count - 1)]

    def far_swap(block):
        return lax.ppermute(block, "rows", far_route)

    def near_swap(block):
        return lax.ppermute(block, "rows", near_route)

    split = height // 2 + 1
    far_feat = far_swap(frame_maps[:, 0])
    near = near_swap(frame_maps)
    far_top = far_swap(frame_maps[:, 1, :split])
    far_low = far_swap(frame_maps[:, 1, split:])

    my_edges = lax.dynamic_slice_in_dim(edges, me * edge_count, edge_count, 0)
    owner = my_edges // frames
    buf = jnp.where(owner == me, 0, jnp.where(owner == (me ^ 1), 2, 1))
    local = my_edges % frames
    meta = jnp.stack(
        [buf[:, 0], local[:, 0], buf[:, 1], local[:, 1], offsets[:, 0], offsets[:, 1]], axis=1
    ).astype(jnp.int32)
    mine = me * frames + jnp.arange(frames, dtype=jnp.int32)
    counts = jnp.maximum(jnp.sum((edges[:, 0][:, None] == mine[None]).astype(F32), axis=0), 1.0)

    gates = gates_of(net_state, w_gates)
    motion = motion_of(meta, frame_maps, near, far_feat, w_motion)
    new_state = None
    bands = []
    for band in range(2):
        new_state, own_sum, near_sum, far_sum = gru_of(
            band, split, meta, frame_maps, near, far_top, far_low if band else far_top,
            motion, gates, net_state, w_input, w_candidate, new_state,
        )
        bands.append((own_sum, near_swap(near_sum), far_swap(far_sum)))
    frame_update = aggregate_of(counts, bands, w_aggregate)
    return (new_state, frame_update)


def solution(mesh):
    in_specs = (
        P(("groups", "rows"), None, None, None, None),
        P(("groups", "rows"), None, None, None),
        P("groups", None),
        P(("groups", "rows"), None),
        P(),
        P(),
        P(),
        P(),
        P(),
    )
    out_specs = (P(("groups", "rows"), None, None, None), P(("groups", "rows"), None, None, None))
    return jax.shard_map(
        per_device, mesh=mesh, in_specs=in_specs, out_specs=out_specs, check_vma=False
    )
```

time: 700 us -> 172 us (0.25)
  local copies, waits for them, and re-layouts: 381 us -> 19.8 us
  matrix products: 113 us -> 0 us
  Pallas kernels: 0 us -> 64.8 us
  other arithmetic: 57.2 us -> 5.21 us
  waiting for transfers between devices: 97.7 us -> 61.1 us
  loops' own time: 33 us -> 0 us
    reshape x12 -> x0, local copies, waits for them, and re-layouts: 210 us -> none  [the longest x8 111 us: correlate(): flat = scores.reshape(height, span, width_px * wide)]
    dot_general x23 -> x0, matrix products: 113 us -> none  [the longest x4 59.4 us: correlate(): jnp.einsum('hwc,havc->hawv', source_feat, stacked, preferred_element_type...]
    while x121 -> x0, local copies, waits for them, and re-layouts: 68.8 us -> none
    pallas_call x0 -> x5, Pallas kernels: none -> 64.8 us  [the longest x2 24.7 us: gru_of(): pl.pallas_call(kernel, grid_spec=pltpu.PrefetchScalarGridSpec(num_scalar_...]
    convert_element_type x9 -> x4, other arithmetic: 47.8 us -> 2.81 us  [the longest x1 1.5 us: motion_of(): jnp.kron(jnp.eye(2, dtype=F32), jnp.eye(width, dtype=F32)[::-1])]
    ppermute x4 -> x8, waiting for transfers between devices: 97.7 us -> 61.1 us  [the longest x5 61.1 us: far_swap(): return lax.ppermute(block, 'rows', far_route)]
    slice x19 -> x5, local copies, waits for them, and re-layouts: 37.2 us -> 2.36 us  [the longest x2 0.93 us: motion_of(): jnp.roll(padded[:, 1], low + width, axis=1)]
    another operation x2 -> x0, loops' own time: 33 us -> none  [the longest x1 32.8 us: per_device(): lax.map(one_edge, (source_local, target_local, offsets, net_state))]
  transfers between devices with their start and end apart: 4 -> 8, of which waited for: 2 -> 3; matrix products, arithmetic and copies ran while one was open for 0% -> 13% of each run, Pallas kernels for 0% -> 26%
where the time goes in v1:
time: 172 us; the launch traced here: 170 us
  Pallas kernels  64.8 us (38%)
  waiting for transfers between devices  61.1 us (36%)
  local copies, waits for them, and re-layouts  19.8 us (12%)
  starting transfers between devices  18.7 us (11%)
  other arithmetic  5.21 us (3%)
    ppermute x5, waiting for transfers between devices, far_swap(): return lax.ppermute(block, 'rows', far_route)  61.1 us
    pallas_call x2, Pallas kernels, gru_of(): pl.pallas_call(kernel, grid_spec=pltpu.PrefetchScalarGridSpec(num_scalar_...  24.7 us
    pallas_call x1, Pallas kernels, motion_of(): pl.pallas_call(motion_kernel, grid_spec=pltpu.PrefetchScalarGridSpec(num_...  20.8 us
    ppermute x5, starting transfers between devices, far_swap(): return lax.ppermute(block, 'rows', far_route)  18.4 us
    pallas_call x1, Pallas kernels, gates_of(): pl.pallas_call(gates_kernel, grid=(edges,), in_specs=[pl.BlockSpec((1, he...  11.5 us
    pallas_call x1, Pallas kernels, aggregate_of(): pl.pallas_call(aggregate_kernel, grid_spec=pltpu.PrefetchScalarGridSpec(n...  7.74 us
    unnamed x20, local copies, waits for them, and re-layouts  4.69 us
  transfers between devices with their start and end apart: 8, of which 3 were waited for; matrix products, arithmetic and copies ran while one was open for 13% of the time, Pallas kernels for 26%

profile of v1, /device:TPU:1, one launch (start us, length us, event | category | flops | bytes accessed | tf_op | source)
XLA Modules:
  0.0 170.4 jit_solution(14424848318012012873)
XLA Ops:
  0.8 2.1 %slice_bitcast_fusion.2 = bf16[2,23,64,128]{3,2,1,0:T(8,128)(2,1)} fusion(bf16[2,2,48,64,128]{4,3,2,1,0:T(8,128)(2,1)} %own.3), kind=kLoop, calls=%fused_computation.2 | loop fusion | bytes 1507328 | tf_op jit(solution)/shard_map/squeeze | solution.py:437
  2.8 4.5 %collective-permute-start.2 = (bf16[2,23,64,128]{3,2,1,0:T(8,128)(2,1)}, bf16[2,23,64,128]{3,2,1,0:T(8,128)(2,1)}, u32[]{:S(2)}, u32[]{:S(2)}) collective-permute-start(bf16[2,23,64,128]{3,2,1,0:T(8,128)(2,1)} %slice_bitcast_fusion.2), channel_id=1, source_target_pairs={{1,2},{2,1},{3,4},{4,3},{5,6},{6,5},{7,8},{8,7},{9,10},{10,9},{11,... | collective-permute-start | bytes 2261000 | tf_op jit(solution)/shard_map/ppermute | solution.py:428
  7.3 2.1 %slice_bitcast_fusion.1 = bf16[2,25,64,128]{3,2,1,0:T(8,128)(2,1)} fusion(bf16[2,2,48,64,128]{4,3,2,1,0:T(8,128)(2,1)} %own.3), kind=kLoop, calls=%fused_computation.1 | loop fusion | bytes 1638400 | tf_op jit(solution)/shard_map/squeeze | solution.py:436
  9.4 1.9 %collective-permute-start.1 = (bf16[2,25,64,128]{3,2,1,0:T(8,128)(2,1)}, bf16[2,25,64,128]{3,2,1,0:T(8,128)(2,1)}, u32[]{:S(2)}, u32[]{:S(2)}) collective-permute-start(bf16[2,25,64,128]{3,2,1,0:T(8,128)(2,1)} %slice_bitcast_fusion.1), channel_id=1, source_target_pairs={{1,2},{2,1},{3,4},{4,3},{5,6},{6,5},{7,8},{8,7},{9,10},{10,9},{11,... | collective-permute-start | bytes 2457608 | tf_op jit(solution)/shard_map/ppermute | solution.py:428
  11.3 2.7 %slice_bitcast_fusion = bf16[2,48,64,128]{3,2,1,0:T(8,128)(2,1)} fusion(bf16[2,2,48,64,128]{4,3,2,1,0:T(8,128)(2,1)} %own.3), kind=kLoop, calls=%fused_computation | loop fusion | bytes 3145728 | tf_op jit(solution)/shard_map/squeeze | solution.py:434
  14.0 3.6 %collective-permute-start.3 = (bf16[2,48,64,128]{3,2,1,0:T(8,128)(2,1)}, bf16[2,48,64,128]{3,2,1,0:T(8,128)(2,1)}, u32[]{:S(2)}, u32[]{:S(2)}) collective-permute-start(bf16[2,48,64,128]{3,2,1,0:T(8,128)(2,1)} %slice_bitcast_fusion), channel_id=1, source_target_pairs={{1,2},{2,1},{3,4},{4,3},{5,6},{6,5},{7,8},{8,7},{9,10},{10,9},{11,... | collective-permute-start | bytes 4718600 | tf_op jit(solution)/shard_map/ppermute | solution.py:428
  19.7 1.3 constant_dynamic-slice_fusion
  21.0 1.3 copy.31
  23.0 1.4 rev.7
  26.4 1.5 multiply_convert_fusion
  27.9 11.5 %gates.1.refs_6_ = bf16[4,48,64,256]{3,2,1,0:T(8,128)(2,1)} custom-call(bf16[4,48,64,128]{3,2,1,0:T(8,128)(2,1)} %state.1, bf16[1152,256]{1,0:T(8,128)(2,1)} %weights_ref.1), custom_call_target="tpu_custom_call" | custom-call | flops 7247757312 | bytes 9437184 | tf_op jit(solution)/shard_map/gates/pallas_call | solution.py:82
  39.5 1.0 maximum_add_fusion.base_ref
  41.2 1.6 convert_element_type.32.flip_ref
  42.8 1.3 stack.3.meta.refs_0_
  44.1 31.4 %collective-permute-done.3.far = bf16[2,48,64,128]{3,2,1,0:T(8,128)(2,1)} collective-permute-done((bf16[2,48,64,128]{3,2,1,0:T(8,128)(2,1)}, bf16[2,48,64,128]{3,2,1,0:T(8,128)(2,1)}, u32[]{:S(2)}, u32[]{:S(2)}) %collective-permute-start.3) | collective-permute-done | bytes 1572896 | tf_op jit(solution)/shard_map/ppermute | solution.py:428
  75.5 1.7 copy-done
  77.2 20.8 %motion.1.refs_5_ = bf16[4,52,64,128]{3,2,1,0:T(8,128)(2,1)} custom-call(s32[4,6]{1,0:T(4,128)} %stack.3.meta.refs_0_, bf16[2,2,48,64,128]{4,3,2,1,0:T(8,128)(2,1)} %own.3, bf16[2,2,48,64,128]{4,3,2,1,0:T(8,128)(2,1)} %copy-done, bf16[2,48,64,128]{3,2,1,0:T(8,128)(2,1)} %collective-permute-done.3.far, bf16[128,128]{1,0:T(8,128)(2,1)} %convert_element_type.32.flip_ref, ...), custom_call_target="tpu_custom_call" | custom-call | flops 8053063680 | bytes 9437184 | tf_op jit(solution)/shard_map/motion/pallas_call | solution.py:187
  98.0 12.3 %gru_band0.1 = (bf16[4,48,64,128]{3,2,1,0:T(8,128)(2,1)}, bf16[2,24,64,128]{3,2,1,0:T(8,128)(2,1)}, bf16[2,24,64,128]{3,2,1,0:T(8,128)(2,1)}, bf16[2,24,64,128]{3,2,1,0:T(8,128)(2,1)}) custom-call(s32[4,6]{1,0:T(4,128)} %stack.3.meta.refs_0_, bf16[2,2,48,64,128]{4,3,2,1,0:T(8,128)(2,1)} %own.3, bf16[2,2,48,64,128]{4,3,2,1,0:T(8,128)(2,1)} %copy-done, ...), custom_call_target="tpu_custom_call" | custom-call | flops 3145728000 | bytes 9830400 | tf_op jit(solution)/shard_map/gru_band0/pallas_call | solution.py:344
  110.3 12.4 %gru_band1.1 = (bf16[4,48,64,128]{3,2,1,0:T(8,128)(2,1)}, bf16[2,24,64,128]{3,2,1,0:T(8,128)(2,1)}, bf16[2,24,64,128]{3,2,1,0:T(8,128)(2,1)}, bf16[2,24,64,128]{3,2,1,0:T(8,128)(2,1)}) custom-call(s32[4,6]{1,0:T(4,128)} %stack.3.meta.refs_0_, bf16[2,2,48,64,128]{4,3,2,1,0:T(8,128)(2,1)} %own.3, ...), custom_call_target="tpu_custom_call", output_to_operand_aliasing={{0}: (10, {})} | custom-call | flops 3145728000 | bytes 9830400 | tf_op jit(solution)/shard_map/gru_band1/pallas_call | solution.py:344
  122.9 4.4 %collective-permute-start.7 = (bf16[2,24,64,128]{3,2,1,0:T(8,128)(2,1)}, bf16[2,24,64,128]{3,2,1,0:T(8,128)(2,1)S(1)}, u32[]{:S(2)}, u32[]{:S(2)}) collective-permute-start(bf16[2,24,64,128]{3,2,1,0:T(8,128)(2,1)} %get-tuple-element.17), channel_id=1, source_target_pairs={{1,2},{2,1},{3,4},{4,3},{5,6},{6,5},{7,8},{8,7},{9,10},{10,9},{11,... | collective-permute-start | bytes 2359304 | tf_op jit(solution)/shard_map/ppermute | solution.py:428
  127.3 4.0 %collective-permute-start.5 = (bf16[2,24,64,128]{3,2,1,0:T(8,128)(2,1)}, bf16[2,24,64,128]{3,2,1,0:T(8,128)(2,1)S(1)}, u32[]{:S(2)}, u32[]{:S(2)}) collective-permute-start(bf16[2,24,64,128]{3,2,1,0:T(8,128)(2,1)} %get-tuple-element.14), channel_id=1, source_target_pairs={{1,2},{2,1},{3,4},{4,3},{5,6},{6,5},{7,8},{8,7},{9,10},{10,9},{11,... | collective-permute-start | bytes 2359304 | tf_op jit(solution)/shard_map/ppermute | solution.py:428
  132.1 21.2 %collective-permute-done.7.refs_5_ = bf16[2,24,64,128]{3,2,1,0:T(8,128)(2,1)S(1)} collective-permute-done((bf16[2,24,64,128]{3,2,1,0:T(8,128)(2,1)}, bf16[2,24,64,128]{3,2,1,0:T(8,128)(2,1)S(1)}, u32[]{:S(2)}, u32[]{:S(2)}) %collective-permute-start.7) | collective-permute-done | bytes 786464 | tf_op jit(solution)/shard_map/ppermute | solution.py:428
  153.3 8.4 %collective-permute-done.5.refs_2_ = bf16[2,24,64,128]{3,2,1,0:T(8,128)(2,1)S(1)} collective-permute-done((bf16[2,24,64,128]{3,2,1,0:T(8,128)(2,1)}, bf16[2,24,64,128]{3,2,1,0:T(8,128)(2,1)S(1)}, u32[]{:S(2)}, u32[]{:S(2)}) %collective-permute-start.5) | collective-permute-done | bytes 786464 | tf_op jit(solution)/shard_map/ppermute | solution.py:428
  162.6 7.7 %aggregate.1 = bf16[2,48,64,128]{3,2,1,0:T(8,128)(2,1)} custom-call(f32[2]{0:T(128)} %broadcast_maximum_fusion.counts, bf16[2,24,64,128]{3,2,1,0:T(8,128)(2,1)} %get-tuple-element.12.refs_0_, bf16[2,24,64,128]{3,2,1,0:T(8,128)(2,1)} %copy-done.5, bf16[2,24,64,128]{3,2,1,0:T(8,128)(2,1)} %copy-done.6, bf16[2,24,64,128]{3,2,1,0:T(8,128)(2,1)} %get-tuple-element.15.refs_3_, ...), custom_call_target="tpu_custom_call" | custom-call | tf_op jit(solution)/shard_map/aggregate/pallas_call | solution.py:402
  (46 shorter events, 7.3 us)
Async XLA Ops:
  0.6 17.0 %copy-start.7 = (bf16[81,128]{1,0:T(8,128)(2,1)S(1)}, bf16[81,128]{1,0:T(8,128)(2,1)}, u32[]{:S(2)}) copy-start(bf16[81,128]{1,0:T(8,128)(2,1)} %param.13) | copy-start | bytes 62212
  0.6 74.9 %collective-permute-start = (bf16[2,2,48,64,128]{4,3,2,1,0:T(8,128)(2,1)}, bf16[2,2,48,64,128]{4,3,2,1,0:T(8,128)(2,1)S(1)}, u32[]{:S(2)}, u32[]{:S(2)}) collective-permute-start(bf16[2,2,48,64,128]{4,3,2,1,0:T(8,128)(2,1)} %own.3), channel_id=1, source_target_pairs={{0,1},{1,0},{2,3},{3,2},{4,5},{5,4},{6,7},{7,6},{8,9},{9,8},{10,11... | collective-permute-start | bytes 9437192 | tf_op jit(solution)/shard_map/ppermute | solution.py:431
  2.8 107.5 %collective-permute-start.2 = (bf16[2,23,64,128]{3,2,1,0:T(8,128)(2,1)}, bf16[2,23,64,128]{3,2,1,0:T(8,128)(2,1)}, u32[]{:S(2)}, u32[]{:S(2)}) collective-permute-start(bf16[2,23,64,128]{3,2,1,0:T(8,128)(2,1)} %slice_bitcast_fusion.2), channel_id=1, source_target_pairs={{1,2},{2,1},{3,4},{4,3},{5,6},{6,5},{7,8},{8,7},{9,10},{10,9},{11,... | collective-permute-start | bytes 2261000 | tf_op jit(solution)/shard_map/ppermute | solution.py:428
  9.4 88.6 %collective-permute-start.1 = (bf16[2,25,64,128]{3,2,1,0:T(8,128)(2,1)}, bf16[2,25,64,128]{3,2,1,0:T(8,128)(2,1)}, u32[]{:S(2)}, u32[]{:S(2)}) collective-permute-start(bf16[2,25,64,128]{3,2,1,0:T(8,128)(2,1)} %slice_bitcast_fusion.1), channel_id=1, source_target_pairs={{1,2},{2,1},{3,4},{4,3},{5,6},{6,5},{7,8},{8,7},{9,10},{10,9},{11,... | collective-permute-start | bytes 2457608 | tf_op jit(solution)/shard_map/ppermute | solution.py:428
  14.0 61.5 %collective-permute-start.3 = (bf16[2,48,64,128]{3,2,1,0:T(8,128)(2,1)}, bf16[2,48,64,128]{3,2,1,0:T(8,128)(2,1)}, u32[]{:S(2)}, u32[]{:S(2)}) collective-permute-start(bf16[2,48,64,128]{3,2,1,0:T(8,128)(2,1)} %slice_bitcast_fusion), channel_id=1, source_target_pairs={{1,2},{2,1},{3,4},{4,3},{5,6},{6,5},{7,8},{8,7},{9,10},{10,9},{11,... | collective-permute-start | bytes 4718600 | tf_op jit(solution)/shard_map/ppermute | solution.py:428
  27.9 11.6 %copy-start.1 = (f32[5,123,256]{2,1,0:T(8,128)S(1)}, f32[5,123,256]{2,1,0:T(8,128)}, u32[]{:S(2)}) copy-start(f32[5,123,256]{2,1,0:T(8,128)} %slice.67) | copy-start | bytes 1889284
  27.9 11.6 %copy-start.2 = (f32[5,59,256]{2,1,0:T(8,128)S(1)}, f32[5,59,256]{2,1,0:T(8,128)}, u32[]{:S(2)}) copy-start(f32[5,59,256]{2,1,0:T(8,128)} %slice.64) | copy-start | bytes 906244
  75.5 1.7 copy-start
  110.3 21.0 %copy-start.8 = (s32[64,2]{0,1:T(2,128)S(1)}, s32[64,2]{0,1:T(2,128)}, u32[]{:S(2)}) copy-start(s32[64,2]{0,1:T(2,128)} %param.11) | copy-start | bytes 1540
  122.8 9.3 %collective-permute-start.6 = (bf16[2,24,64,128]{3,2,1,0:T(8,128)(2,1)}, bf16[2,24,64,128]{3,2,1,0:T(8,128)(2,1)S(1)}, u32[]{:S(2)}, u32[]{:S(2)}) collective-permute-start(bf16[2,24,64,128]{3,2,1,0:T(8,128)(2,1)} %get-tuple-element.16), channel_id=1, source_target_pairs={{0,1},{1,0},{2,3},{3,2},{4,5},{5,4},{6,7},{7,6},{8,9},{9,8},{10,11... | collective-permute-start | bytes 2359304 | tf_op jit(solution)/shard_map/ppermute | solution.py:431
  122.9 30.5 %collective-permute-start.7 = (bf16[2,24,64,128]{3,2,1,0:T(8,128)(2,1)}, bf16[2,24,64,128]{3,2,1,0:T(8,128)(2,1)S(1)}, u32[]{:S(2)}, u32[]{:S(2)}) collective-permute-start(bf16[2,24,64,128]{3,2,1,0:T(8,128)(2,1)} %get-tuple-element.17), channel_id=1, source_target_pairs={{1,2},{2,1},{3,4},{4,3},{5,6},{6,5},{7,8},{8,7},{9,10},{10,9},{11,... | collective-permute-start | bytes 2359304 | tf_op jit(solution)/shard_map/ppermute | solution.py:428
  127.3 26.1 %collective-permute-start.4 = (bf16[2,24,64,128]{3,2,1,0:T(8,128)(2,1)}, bf16[2,24,64,128]{3,2,1,0:T(8,128)(2,1)S(1)}, u32[]{:S(2)}, u32[]{:S(2)}) collective-permute-start(bf16[2,24,64,128]{3,2,1,0:T(8,128)(2,1)} %get-tuple-element.13), channel_id=1, source_target_pairs={{0,1},{1,0},{2,3},{3,2},{4,5},{5,4},{6,7},{7,6},{8,9},{9,8},{10,11... | collective-permute-start | bytes 2359304 | tf_op jit(solution)/shard_map/ppermute | solution.py:431
  127.3 34.4 %collective-permute-start.5 = (bf16[2,24,64,128]{3,2,1,0:T(8,128)(2,1)}, bf16[2,24,64,128]{3,2,1,0:T(8,128)(2,1)S(1)}, u32[]{:S(2)}, u32[]{:S(2)}) collective-permute-start(bf16[2,24,64,128]{3,2,1,0:T(8,128)(2,1)} %get-tuple-element.14), channel_id=1, source_target_pairs={{1,2},{2,1},{3,4},{4,3},{5,6},{6,5},{7,8},{8,7},{9,10},{10,9},{11,... | collective-permute-start | bytes 2359304 | tf_op jit(solution)/shard_map/ppermute | solution.py:428
  132.1 29.7 %copy-start.3 = (bf16[2,24,64,128]{3,2,1,0:T(8,128)(2,1)}, bf16[2,24,64,128]{3,2,1,0:T(8,128)(2,1)S(1)}, u32[]{:S(2)}) copy-start(bf16[2,24,64,128]{3,2,1,0:T(8,128)(2,1)S(1)} %collective-permute-done.6.refs_4_) | copy-start | bytes 2359300
  153.3 8.4 %copy-start.4 = (bf16[2,24,64,128]{3,2,1,0:T(8,128)(2,1)}, bf16[2,24,64,128]{3,2,1,0:T(8,128)(2,1)S(1)}, u32[]{:S(2)}) copy-start(bf16[2,24,64,128]{3,2,1,0:T(8,128)(2,1)S(1)} %collective-permute-done.7.refs_5_) | copy-start | bytes 2359300
  153.3 8.4 %copy-start.5 = (bf16[2,24,64,128]{3,2,1,0:T(8,128)(2,1)}, bf16[2,24,64,128]{3,2,1,0:T(8,128)(2,1)S(1)}, u32[]{:S(2)}) copy-start(bf16[2,24,64,128]{3,2,1,0:T(8,128)(2,1)S(1)} %collective-permute-done.4.refs_1_) | copy-start | bytes 2359300
  161.8 0.9 copy-start.6

commit v2 on v1

--- a/solution.py
+++ b/solution.py
@@ -13,7 +13,7 @@
 MARGIN = SHIFT + RADIUS
 F32 = jnp.float32
 BF16 = jnp.bfloat16
-VMEM_LIMIT = 56 << 20
+VMEM_LIMIT = 60 << 20
 
 
 def any_spec():
@@ -424,7 +424,9 @@
     near_route = [(i, i ^ 1) for i in range(count)]
     far_route = [(i, i + 1 if i % 2 else i - 1) for i in range(1, count - 1)]
 
-    def far_swap(block):
+    def far_swap(block, *after):
+        if after:
+            block = lax.optimization_barrier((block,) + after)[0]
         return lax.ppermute(block, "rows", far_route)
 
     def near_swap(block):
@@ -433,8 +435,6 @@
     split = height // 2 + 1
     far_feat = far_swap(frame_maps[:, 0])
     near = near_swap(frame_maps)
-    far_top = far_swap(frame_maps[:, 1, :split])
-    far_low = far_swap(frame_maps[:, 1, split:])
 
     my_edges = lax.dynamic_slice_in_dim(edges, me * edge_count, edge_count, 0)
     owner = my_edges // frames
@@ -447,15 +447,19 @@
     counts = jnp.maximum(jnp.sum((edges[:, 0][:, None] == mine[None]).astype(F32), axis=0), 1.0)
 
     gates = gates_of(net_state, w_gates)
+    far_top = far_swap(frame_maps[:, 1, :split], far_feat, gates)
     motion = motion_of(meta, frame_maps, near, far_feat, w_motion)
+    far_low = far_swap(frame_maps[:, 1, split:], far_top, motion)
     new_state = None
     bands = []
+    latest = far_low
     for band in range(2):
         new_state, own_sum, near_sum, far_sum = gru_of(
             band, split, meta, frame_maps, near, far_top, far_low if band else far_top,
             motion, gates, net_state, w_input, w_candidate, new_state,
         )
-        bands.append((own_sum, near_swap(near_sum), far_swap(far_sum)))
+        latest = far_swap(far_sum, latest)
+        bands.append((own_sum, near_swap(near_sum), latest))
     frame_update = aggregate_of(counts, bands, w_aggregate)
     return (new_state, frame_update)
 

time: 172 us -> 141 us (0.82)
  waiting for transfers between devices: 61.1 us -> 39.6 us
  local copies, waits for them, and re-layouts: 19.8 us -> 11.1 us
    ppermute x5, waiting for transfers between devices: 61.1 us -> 39.5 us  [far_swap(): return lax.ppermute(block, 'rows', far_route)]
    unnamed x20 -> x42, local copies, waits for them, and re-layouts: 4.69 us -> 1.17 us
    squeeze x2, local copies, waits for them, and re-layouts: 4.15 us -> 1.87 us  [the longest x1 0.94 us: per_device(): far_top = far_swap(frame_maps[:, 1, :split], far_feat, gates)]
    ppermute x5, starting transfers between devices: 18.4 us -> 16.4 us  [far_swap(): return lax.ppermute(block, 'rows', far_route)]
  transfers between devices with their start and end apart: 8 -> 8, of which waited for: 3 -> 2; matrix products, arithmetic and copies ran while one was open for 13% -> 11% of each run, Pallas kernels for 26% -> 41%
where the time goes in v2:
time: 141 us; the launch traced here: 138 us
  Pallas kernels  65 us (46%)
  waiting for transfers between devices  39.6 us (28%)
  starting transfers between devices  17.2 us (12%)
  local copies, waits for them, and re-layouts  11.1 us (8%)
  other arithmetic  4.55 us (3%)
    ppermute x5, waiting for transfers between devices, far_swap(): return lax.ppermute(block, 'rows', far_route)  39.5 us
    pallas_call x2, Pallas kernels, gru_of(): pl.pallas_call(kernel, grid_spec=pltpu.PrefetchScalarGridSpec(num_scalar_...  24.8 us
    pallas_call x1, Pallas kernels, motion_of(): pl.pallas_call(motion_kernel, grid_spec=pltpu.PrefetchScalarGridSpec(num_...  20.9 us
    ppermute x5, starting transfers between devices, far_swap(): return lax.ppermute(block, 'rows', far_route)  16.4 us
    pallas_call x1, Pallas kernels, gates_of(): pl.pallas_call(gates_kernel, grid=(edges,), in_specs=[pl.BlockSpec((1, he...  11.6 us
    pallas_call x1, Pallas kernels, aggregate_of(): pl.pallas_call(aggregate_kernel, grid_spec=pltpu.PrefetchScalarGridSpec(n...  7.74 us
  transfers between devices with their start and end apart: 8, of which 2 were waited for; matrix products, arithmetic and copies ran while one was open for 11% of the time, Pallas kernels for 41%

profile of v2, /device:TPU:1, one launch (start us, length us, event | category | flops | bytes accessed | tf_op | source)
XLA Modules:
  0.0 138.5 jit_solution(18223846739512850705)
XLA Ops:
  0.8 2.7 %slice_bitcast_fusion = bf16[2,48,64,128]{3,2,1,0:T(8,128)(2,1)} fusion(bf16[2,2,48,64,128]{4,3,2,1,0:T(8,128)(2,1)} %own.3), kind=kLoop, calls=%fused_computation | loop fusion | bytes 3145728 | tf_op jit(solution)/shard_map/squeeze | solution.py:436
  3.4 4.5 %collective-permute-start.1 = (bf16[2,48,64,128]{3,2,1,0:T(8,128)(2,1)}, bf16[2,48,64,128]{3,2,1,0:T(8,128)(2,1)}, u32[]{:S(2)}, u32[]{:S(2)}) collective-permute-start(bf16[2,48,64,128]{3,2,1,0:T(8,128)(2,1)} %slice_bitcast_fusion), channel_id=1, source_target_pairs={{1,2},{2,1},{3,4},{4,3},{5,6},{6,5},{7,8},{8,7},{9,10},{10,9},{11,... | collective-permute-start | bytes 4718600 | tf_op jit(solution)/shard_map/ppermute | solution.py:430
  9.0 0.7 fusion.3.mask_ref
  10.4 0.9 slice.67
  11.4 0.7 slice.64
  12.1 1.4 rev.7
  13.5 1.5 %multiply_convert_fusion = bf16[2,64,2,64]{3,2,1,0:T(2,128)(2,1)} fusion(f32[64,64]{1,0:T(8,128)} %rev.7, f32[2,2]{1,0:T(2,128)S(1)} %compare_convert_fusion.1), kind=kLoop, calls=%fused_computation.9 | loop fusion | flops 32768 | bytes 49168 | tf_op jit(solution)/shard_map/convert_element_type | solution.py:179
  15.0 0.9 slice_bitcast_fusion.2
  15.9 0.9 slice_bitcast_fusion.1
  16.9 11.6 %gates.1.refs_6_ = bf16[4,48,64,256]{3,2,1,0:T(8,128)(2,1)} custom-call(bf16[4,48,64,128]{3,2,1,0:T(8,128)(2,1)} %state.1, bf16[1152,256]{1,0:T(8,128)(2,1)} %weights_ref.1), custom_call_target="tpu_custom_call" | custom-call | flops 7247757312 | bytes 9437184 | tf_op jit(solution)/shard_map/gates/pallas_call | solution.py:82
  28.5 22.7 %collective-permute-done.1.far = bf16[2,48,64,128]{3,2,1,0:T(8,128)(2,1)} collective-permute-done((bf16[2,48,64,128]{3,2,1,0:T(8,128)(2,1)}, bf16[2,48,64,128]{3,2,1,0:T(8,128)(2,1)}, u32[]{:S(2)}, u32[]{:S(2)}) %collective-permute-start.1) | collective-permute-done | bytes 1572896 | tf_op jit(solution)/shard_map/ppermute | solution.py:430
  51.2 4.4 %collective-permute-start.2 = (bf16[2,25,64,128]{3,2,1,0:T(8,128)(2,1)S(1)}, bf16[2,25,64,128]{3,2,1,0:T(8,128)(2,1)S(1)}, u32[]{:S(2)}, u32[]{:S(2)}) collective-permute-start(bf16[2,25,64,128]{3,2,1,0:T(8,128)(2,1)S(1)} %copy-done.4), channel_id=1, source_target_pairs={{1,2},{2,1},{3,4},{4,3},{5,6},{6,5},{7,8},{8,7},{9,10},{10,9},{11,... | collective-permute-start | bytes 2457608 | tf_op jit(solution)/shard_map/ppermute | solution.py:430
  55.6 0.9 maximum_add_fusion.base_ref
  56.7 0.7 convert_element_type.32.flip_ref
  57.4 0.7 stack.3.meta.refs_0_
  58.1 20.9 %motion.1.refs_5_ = bf16[4,52,64,128]{3,2,1,0:T(8,128)(2,1)} custom-call(s32[4,6]{1,0:T(4,128)} %stack.3.meta.refs_0_, bf16[2,2,48,64,128]{4,3,2,1,0:T(8,128)(2,1)} %own.3, bf16[2,2,48,64,128]{4,3,2,1,0:T(8,128)(2,1)} %collective-permute-done.near.refs_2_, bf16[2,48,64,128]{3,2,1,0:T(8,128)(2,1)} %collective-permute-done.1.far, ...), custom_call_target="tpu_custom_call" | custom-call | flops 8053063680 | bytes 9437184 | tf_op jit(solution)/shard_map/motion/pallas_call | solution.py:187
  79.0 1.9 %collective-permute-start.3 = (bf16[2,23,64,128]{3,2,1,0:T(8,128)(2,1)S(1)}, bf16[2,23,64,128]{3,2,1,0:T(8,128)(2,1)S(1)}, u32[]{:S(2)}, u32[]{:S(2)}) collective-permute-start(bf16[2,23,64,128]{3,2,1,0:T(8,128)(2,1)S(1)} %copy-done.10), channel_id=1, source_target_pairs={{1,2},{2,1},{3,4},{4,3},{5,6},{6,5},{7,8},{8,7},{9,10},{10,9},{11,... | collective-permute-start | bytes 2261000 | tf_op jit(solution)/shard_map/ppermute | solution.py:430
  81.0 12.3 %gru_band0.1 = (bf16[4,48,64,128]{3,2,1,0:T(8,128)(2,1)}, bf16[2,24,64,128]{3,2,1,0:T(8,128)(2,1)}, bf16[2,24,64,128]{3,2,1,0:T(8,128)(2,1)}, bf16[2,24,64,128]{3,2,1,0:T(8,128)(2,1)}) custom-call(s32[4,6]{1,0:T(4,128)} %stack.3.meta.refs_0_, bf16[2,2,48,64,128]{4,3,2,1,0:T(8,128)(2,1)} %own.3, ...), custom_call_target="tpu_custom_call" | custom-call | flops 3145728000 | bytes 9830400 | tf_op jit(solution)/shard_map/gru_band0/pallas_call | solution.py:344
  93.3 3.7 %collective-permute-start.5 = (bf16[2,24,64,128]{3,2,1,0:T(8,128)(2,1)}, bf16[2,24,64,128]{3,2,1,0:T(8,128)(2,1)S(1)}, u32[]{:S(2)}, u32[]{:S(2)}) collective-permute-start(bf16[2,24,64,128]{3,2,1,0:T(8,128)(2,1)} %get-tuple-element.21), channel_id=1, source_target_pairs={{1,2},{2,1},{3,4},{4,3},{5,6},{6,5},{7,8},{8,7},{9,10},{10,9},{11,... | collective-permute-start | bytes 2359304 | tf_op jit(solution)/shard_map/ppermute | solution.py:430
  97.1 12.4 %gru_band1.1 = (bf16[4,48,64,128]{3,2,1,0:T(8,128)(2,1)}, bf16[2,24,64,128]{3,2,1,0:T(8,128)(2,1)}, bf16[2,24,64,128]{3,2,1,0:T(8,128)(2,1)}, bf16[2,24,64,128]{3,2,1,0:T(8,128)(2,1)}) custom-call(s32[4,6]{1,0:T(4,128)} %stack.3.meta.refs_0_, bf16[2,2,48,64,128]{4,3,2,1,0:T(8,128)(2,1)} %own.3, ...), custom_call_target="tpu_custom_call", output_to_operand_aliasing={{0}: (10, {})} | custom-call | flops 3145728000 | bytes 9830400 | tf_op jit(solution)/shard_map/gru_band1/pallas_call | solution.py:344
  110.2 1.9 %collective-permute-start.7 = (bf16[2,24,64,128]{3,2,1,0:T(8,128)(2,1)}, bf16[2,24,64,128]{3,2,1,0:T(8,128)(2,1)S(1)}, u32[]{:S(2)}, u32[]{:S(2)}) collective-permute-start(bf16[2,24,64,128]{3,2,1,0:T(8,128)(2,1)} %get-tuple-element.25), channel_id=1, source_target_pairs={{1,2},{2,1},{3,4},{4,3},{5,6},{6,5},{7,8},{8,7},{9,10},{10,9},{11,... | collective-permute-start | bytes 2359304 | tf_op jit(solution)/shard_map/ppermute | solution.py:430
  113.0 16.8 %collective-permute-done.7.refs_5_ = bf16[2,24,64,128]{3,2,1,0:T(8,128)(2,1)S(1)} collective-permute-done((bf16[2,24,64,128]{3,2,1,0:T(8,128)(2,1)}, bf16[2,24,64,128]{3,2,1,0:T(8,128)(2,1)S(1)}, u32[]{:S(2)}, u32[]{:S(2)}) %collective-permute-start.7) | collective-permute-done | bytes 786464 | tf_op jit(solution)/shard_map/ppermute | solution.py:430
  129.8 0.9 copy-done.8
  130.7 7.7 %aggregate.1 = bf16[2,48,64,128]{3,2,1,0:T(8,128)(2,1)} custom-call(f32[2]{0:T(128)} %broadcast_maximum_fusion.counts, bf16[2,24,64,128]{3,2,1,0:T(8,128)(2,1)} %get-tuple-element.18.refs_0_, bf16[2,24,64,128]{3,2,1,0:T(8,128)(2,1)} %copy-done.6, bf16[2,24,64,128]{3,2,1,0:T(8,128)(2,1)} %copy-done.5, bf16[2,24,64,128]{3,2,1,0:T(8,128)(2,1)} %get-tuple-element.22.refs_3_, ...), custom_call_target="tpu_custom_call" | custom-call | tf_op jit(solution)/shard_map/aggregate/pallas_call | solution.py:402
  (68 shorter events, 3.6 us)
Async XLA Ops:
  0.6 7.3 %copy-start.18 = (s32[64,2]{0,1:T(2,128)S(1)}, s32[64,2]{0,1:T(2,128)}, u32[]{:S(2)}) copy-start(s32[64,2]{0,1:T(2,128)} %param.11) | copy-start | bytes 1540
  0.6 7.5 %copy-start.12 = (bf16[81,128]{1,0:T(8,128)(2,1)S(1)}, bf16[81,128]{1,0:T(8,128)(2,1)}, u32[]{:S(2)}) copy-start(bf16[81,128]{1,0:T(8,128)(2,1)} %param.13) | copy-start | bytes 62212
  0.7 57.5 %collective-permute-start = (bf16[2,2,48,64,128]{4,3,2,1,0:T(8,128)(2,1)}, bf16[2,2,48,64,128]{4,3,2,1,0:T(8,128)(2,1)}, u32[]{:S(2)}, u32[]{:S(2)}) collective-permute-start(bf16[2,2,48,64,128]{4,3,2,1,0:T(8,128)(2,1)} %own.3), channel_id=1, source_target_pairs={{0,1},{1,0},{2,3},{3,2},{4,5},{5,4},{6,7},{7,6},{8,9},{9,8},{10,11... | collective-permute-start | bytes 9437192 | tf_op jit(solution)/shard_map/ppermute | solution.py:433
  3.4 47.8 %collective-permute-start.1 = (bf16[2,48,64,128]{3,2,1,0:T(8,128)(2,1)}, bf16[2,48,64,128]{3,2,1,0:T(8,128)(2,1)}, u32[]{:S(2)}, u32[]{:S(2)}) collective-permute-start(bf16[2,48,64,128]{3,2,1,0:T(8,128)(2,1)} %slice_bitcast_fusion), channel_id=1, source_target_pairs={{1,2},{2,1},{3,4},{4,3},{5,6},{6,5},{7,8},{8,7},{9,10},{10,9},{11,... | collective-permute-start | bytes 4718600 | tf_op jit(solution)/shard_map/ppermute | solution.py:430
  16.9 34.4 %copy-start.4 = (bf16[2,25,64,128]{3,2,1,0:T(8,128)(2,1)S(1)}, bf16[2,25,64,128]{3,2,1,0:T(8,128)(2,1)}, u32[]{:S(2)}) copy-start(bf16[2,25,64,128]{3,2,1,0:T(8,128)(2,1)} %slice_bitcast_fusion.1) | copy-start | bytes 2457604
  16.9 38.8 %copy-start.2 = (f32[5,123,256]{2,1,0:T(8,128)S(1)}, f32[5,123,256]{2,1,0:T(8,128)}, u32[]{:S(2)}) copy-start(f32[5,123,256]{2,1,0:T(8,128)} %slice.67) | copy-start | bytes 1889284
  16.9 38.8 %copy-start.3 = (f32[5,59,256]{2,1,0:T(8,128)S(1)}, f32[5,59,256]{2,1,0:T(8,128)}, u32[]{:S(2)}) copy-start(f32[5,59,256]{2,1,0:T(8,128)} %slice.64) | copy-start | bytes 906244
  16.9 39.7 %copy-start.17 = (s32[4,2]{0,1:T(2,128)S(1)}, s32[4,2]{0,1:T(2,128)}, u32[]{:S(2)}) copy-start(s32[4,2]{0,1:T(2,128)} %param.12) | copy-start | bytes 100
  16.9 39.8 %copy-start.11 = (bf16[2,64,2,64]{3,2,1,0:T(2,128)(2,1)S(1)}, bf16[2,64,2,64]{3,2,1,0:T(2,128)(2,1)}, u32[]{:S(2)}) copy-start(bf16[2,64,2,64]{3,2,1,0:T(2,128)(2,1)} %multiply_convert_fusion) | copy-start | bytes 98308
  16.9 40.5 %copy-start.13 = (s32[4,1]{1,0:T(4,128)S(1)}, s32[4,1]{1,0:T(4,128)}, u32[]{:S(2)}) copy-start(s32[4,1]{1,0:T(4,128)} %get-tuple-element.28) | copy-start | bytes 52
  16.9 40.5 %copy-start.14 = (s32[4,1]{1,0:T(4,128)S(1)}, s32[4,1]{1,0:T(4,128)}, u32[]{:S(2)}) copy-start(s32[4,1]{1,0:T(4,128)} %get-tuple-element.29) | copy-start | bytes 52
  16.9 40.5 %copy-start.15 = (s32[4,1]{1,0:T(4,128)S(1)}, s32[4,1]{1,0:T(4,128)}, u32[]{:S(2)}) copy-start(s32[4,1]{1,0:T(4,128)} %get-tuple-element.34) | copy-start | bytes 52
  16.9 40.5 %copy-start.16 = (s32[4,1]{1,0:T(4,128)S(1)}, s32[4,1]{1,0:T(4,128)}, u32[]{:S(2)}) copy-start(s32[4,1]{1,0:T(4,128)} %get-tuple-element.35) | copy-start | bytes 52
  51.2 27.8 %collective-permute-start.2 = (bf16[2,25,64,128]{3,2,1,0:T(8,128)(2,1)S(1)}, bf16[2,25,64,128]{3,2,1,0:T(8,128)(2,1)S(1)}, u32[]{:S(2)}, u32[]{:S(2)}) collective-permute-start(bf16[2,25,64,128]{3,2,1,0:T(8,128)(2,1)S(1)} %copy-done.4), channel_id=1, source_target_pairs={{1,2},{2,1},{3,4},{4,3},{5,6},{6,5},{7,8},{8,7},{9,10},{10,9},{11,... | collective-permute-start | bytes 2457608 | tf_op jit(solution)/shard_map/ppermute | solution.py:430
  58.1 20.9 %copy-start.10 = (bf16[2,23,64,128]{3,2,1,0:T(8,128)(2,1)S(1)}, bf16[2,23,64,128]{3,2,1,0:T(8,128)(2,1)}, u32[]{:S(2)}) copy-start(bf16[2,23,64,128]{3,2,1,0:T(8,128)(2,1)} %slice_bitcast_fusion.2) | copy-start | bytes 2260996
  79.0 14.3 %collective-permute-start.3 = (bf16[2,23,64,128]{3,2,1,0:T(8,128)(2,1)S(1)}, bf16[2,23,64,128]{3,2,1,0:T(8,128)(2,1)S(1)}, u32[]{:S(2)}, u32[]{:S(2)}) collective-permute-start(bf16[2,23,64,128]{3,2,1,0:T(8,128)(2,1)S(1)} %copy-done.10), channel_id=1, source_target_pairs={{1,2},{2,1},{3,4},{4,3},{5,6},{6,5},{7,8},{8,7},{9,10},{10,9},{11,... | collective-permute-start | bytes 2261000 | tf_op jit(solution)/shard_map/ppermute | solution.py:430
  93.3 16.9 %collective-permute-start.5 = (bf16[2,24,64,128]{3,2,1,0:T(8,128)(2,1)}, bf16[2,24,64,128]{3,2,1,0:T(8,128)(2,1)S(1)}, u32[]{:S(2)}, u32[]{:S(2)}) collective-permute-start(bf16[2,24,64,128]{3,2,1,0:T(8,128)(2,1)} %get-tuple-element.21), channel_id=1, source_target_pairs={{1,2},{2,1},{3,4},{4,3},{5,6},{6,5},{7,8},{8,7},{9,10},{10,9},{11,... | collective-permute-start | bytes 2359304 | tf_op jit(solution)/shard_map/ppermute | solution.py:430
  97.0 16.0 %collective-permute-start.4 = (bf16[2,24,64,128]{3,2,1,0:T(8,128)(2,1)}, bf16[2,24,64,128]{3,2,1,0:T(8,128)(2,1)S(1)}, u32[]{:S(2)}, u32[]{:S(2)}) collective-permute-start(bf16[2,24,64,128]{3,2,1,0:T(8,128)(2,1)} %get-tuple-element.19), channel_id=1, source_target_pairs={{0,1},{1,0},{2,3},{3,2},{4,5},{5,4},{6,7},{7,6},{8,9},{9,8},{10,11... | collective-permute-start | bytes 2359304 | tf_op jit(solution)/shard_map/ppermute | solution.py:433
  97.1 15.1 %copy-start.19 = (s32[64,2]{0,1:T(2,128)S(1)}, s32[64,2]{0,1:T(2,128)}, u32[]{:S(2)}) copy-start(s32[64,2]{0,1:T(2,128)} %param.11) | copy-start | bytes 1540
  109.6 3.4 %collective-permute-start.6 = (bf16[2,24,64,128]{3,2,1,0:T(8,128)(2,1)}, bf16[2,24,64,128]{3,2,1,0:T(8,128)(2,1)S(1)}, u32[]{:S(2)}, u32[]{:S(2)}) collective-permute-start(bf16[2,24,64,128]{3,2,1,0:T(8,128)(2,1)} %get-tuple-element.23), channel_id=1, source_target_pairs={{0,1},{1,0},{2,3},{3,2},{4,5},{5,4},{6,7},{7,6},{8,9},{9,8},{10,11... | collective-permute-start | bytes 2359304 | tf_op jit(solution)/shard_map/ppermute | solution.py:433
  110.2 19.6 %copy-start.5 = (bf16[2,24,64,128]{3,2,1,0:T(8,128)(2,1)}, bf16[2,24,64,128]{3,2,1,0:T(8,128)(2,1)S(1)}, u32[]{:S(2)}) copy-start(bf16[2,24,64,128]{3,2,1,0:T(8,128)(2,1)S(1)} %collective-permute-done.5.refs_2_) | copy-start | bytes 2359300
  110.2 19.6 %collective-permute-start.7 = (bf16[2,24,64,128]{3,2,1,0:T(8,128)(2,1)}, bf16[2,24,64,128]{3,2,1,0:T(8,128)(2,1)S(1)}, u32[]{:S(2)}, u32[]{:S(2)}) collective-permute-start(bf16[2,24,64,128]{3,2,1,0:T(8,128)(2,1)} %get-tuple-element.25), channel_id=1, source_target_pairs={{1,2},{2,1},{3,4},{4,3},{5,6},{6,5},{7,8},{8,7},{9,10},{10,9},{11,... | collective-permute-start | bytes 2359304 | tf_op jit(solution)/shard_map/ppermute | solution.py:430
  113.0 16.9 %copy-start.6 = (bf16[2,24,64,128]{3,2,1,0:T(8,128)(2,1)}, bf16[2,24,64,128]{3,2,1,0:T(8,128)(2,1)S(1)}, u32[]{:S(2)}) copy-start(bf16[2,24,64,128]{3,2,1,0:T(8,128)(2,1)S(1)} %collective-permute-done.4.refs_1_) | copy-start | bytes 2359300
  113.0 16.9 %copy-start.7 = (bf16[2,24,64,128]{3,2,1,0:T(8,128)(2,1)}, bf16[2,24,64,128]{3,2,1,0:T(8,128)(2,1)S(1)}, u32[]{:S(2)}) copy-start(bf16[2,24,64,128]{3,2,1,0:T(8,128)(2,1)S(1)} %collective-permute-done.6.refs_4_) | copy-start | bytes 2359300
  (4 other events, 13.3 us)

commit v3 on v2

--- a/solution.py
+++ b/solution.py
@@ -2,6 +2,7 @@
 
 import jax
 import jax.numpy as jnp
+import numpy as np
 from jax import lax
 from jax.experimental import pallas as pl
 from jax.experimental.pallas import tpu as pltpu
@@ -96,11 +97,12 @@
     )(state, weights)
 
 
-def motion_kernel(meta, own, near, far, flip_ref, mask_ref, base_ref, out_ref, src_buf, raw_buf, tgt_buf, w_buf, sems):
-    edge = pl.program_id(0)
-    edges = pl.num_programs(0)
+def motion_kernel(low, meta, own, near, far, flip_ref, mask_ref, base_ref, out_ref, src_buf, raw_buf, tgt_buf, w_buf, sems):
+    step = pl.program_id(0)
+    steps = pl.num_programs(0)
+    edge = step + low
     height, width, chans = own.shape[2:]
-    slot = lax.rem(edge, 2)
+    slot = lax.rem(step, 2)
     lanes = 2 * width
     tiles = base_ref.shape[0]
 
@@ -111,14 +113,14 @@
         fetch(cases(meta[e, 0], meta[e, 1]), src_buf.at[s, pl.ds(1, height)], sems.at[0, s])
         fetch(cases(meta[e, 2], meta[e, 3]), raw_buf.at[s], sems.at[1, s])
 
-    @pl.when(edge == 0)
+    @pl.when(step == 0)
     def _():
         start(edge, slot)
         tgt_buf[0:MARGIN] = jnp.zeros((MARGIN, width, chans), BF16)
         below = tgt_buf.shape[0] - MARGIN - height
         tgt_buf[MARGIN + height :] = jnp.zeros((below, width, chans), BF16)
 
-    @pl.when(edge + 1 < edges)
+    @pl.when(step + 1 < steps)
     def _():
         start(edge + 1, 1 - slot)
 
@@ -163,34 +165,52 @@
             out_ref[0, pl.ds(y + 2, 1)] = jnp.maximum(res[width:, chans:], 0.0).astype(BF16)[None]
 
 
-def motion_of(meta, own, near, far, w_motion):
+def motion_constants(width, chans):
+    lanes = 2 * width
+    rows = SPAN + 1
+    place = np.zeros((2, rows // 2, lanes, SPAN * SPAN), np.float32)
+    for r in range(rows):
+        for b in range(SPAN):
+            lane = (width - 1 + RADIUS - b + width * (r % 2)) % lanes
+            for parity in range(2):
+                if 0 <= r - parity < SPAN:
+                    place[parity, r // 2, lane, (r - parity) * SPAN + b] = 1.0
+    flip = np.kron(np.eye(2), np.eye(width)[::-1])
+    x = np.arange(width)[:, None]
+    lane = np.arange(lanes)[None]
+    middle = (lane >= width // 2) & (lane < width + width // 2)
+    inside = np.where(middle, (lane >= x) & (lane < x + width), np.where(lane < width, x > lane, lane >= x + width))
+    return place.astype(BF16), flip.astype(BF16), inside.astype(np.float32)
+
+
+def motion_weights(w_motion, width):
+    place = motion_constants(width, w_motion.shape[1])[0]
+    return jnp.concatenate(
+        [jnp.einsum("tlk,kc->tlc", side, w_motion, preferred_element_type=F32) for side in place], axis=2
+    )
+
+
+def motion_of(low, high, meta, own, near, far, base, earlier):
     _, _, height, width, chans = own.shape
     edges = meta.shape[0]
-    lanes = 2 * width
     rows = SPAN + 1
-    taps = jnp.flip(w_motion.reshape(SPAN, SPAN, chans).astype(F32), axis=1)
-    blank = jnp.zeros((1, SPAN, chans), F32)
-    both = jnp.concatenate(
-        [jnp.concatenate([taps, blank], axis=0), jnp.concatenate([blank, taps], axis=0)], axis=2
-    )
-    low = width - 1 - RADIUS
-    padded = jnp.pad(both, ((0, 0), (0, lanes - SPAN), (0, 0))).reshape(rows // 2, 2, lanes, 2 * chans)
-    base = jnp.roll(padded[:, 0], low, axis=1) + jnp.roll(padded[:, 1], low + width, axis=1)
-    flip = jnp.kron(jnp.eye(2, dtype=F32), jnp.eye(width, dtype=F32)[::-1]).astype(BF16)
-    x = jnp.arange(width)[:, None]
-    lane = jnp.arange(lanes)[None]
-    middle = (lane >= width // 2) & (lane < width + width // 2)
-    inside = jnp.where(middle, (lane >= x) & (lane < x + width), jnp.where(lane < width, x > lane, lane >= x + width))
-    mask = inside.astype(F32)
+    _, flip, mask = motion_constants(width, chans)
     buffer_rows = height + 4
     target_rows = height + 2 * MARGIN + 2
+    operands = [meta, own, near, far, flip, mask, base]
+    body = functools.partial(motion_kernel, low)
+    if earlier is None:
+        kernel, aliases = body, {}
+    else:
+        kernel, aliases = lambda *refs: body(*refs[:7], *refs[8:]), {7: 0}
+        operands.append(earlier)
     return pl.pallas_call(
-        motion_kernel,
+        kernel,
         grid_spec=pltpu.PrefetchScalarGridSpec(
             num_scalar_prefetch=1,
-            grid=(edges,),
-            in_specs=[any_spec(), any_spec(), any_spec(), whole(flip), whole(mask), whole(base)],
-            out_specs=pl.BlockSpec((1, buffer_rows, width, chans), lambda e, m: (e, 0, 0, 0)),
+            grid=(high - low,),
+            in_specs=[any_spec()] * 3 + [whole(flip), whole(mask), whole(base)] + [any_spec()] * (len(operands) - 7),
+            out_specs=pl.BlockSpec((1, buffer_rows, width, chans), lambda e, m: (e + low, 0, 0, 0)),
             scratch_shapes=[
                 pltpu.VMEM((2, buffer_rows, width, chans), BF16),
                 pltpu.VMEM((2, height, width, chans), BF16),
@@ -200,14 +220,15 @@
             ],
         ),
         out_shape=jax.ShapeDtypeStruct((edges, buffer_rows, width, chans), BF16),
+        input_output_aliases=aliases,
         compiler_params=pltpu.CompilerParams(vmem_limit_bytes=VMEM_LIMIT),
         cost_estimate=pl.CostEstimate(
-            flops=8 * edges * height * width * chans * rows * width,
-            bytes_accessed=6 * edges * height * width * chans,
+            flops=8 * (high - low) * height * width * chans * rows * width,
+            bytes_accessed=6 * (high - low) * height * width * chans,
             transcendentals=0,
         ),
-        name="motion",
-    )(meta, own, near, far, flip, mask, base)
+        name=f"motion_from{low}",
+    )(*operands)
 
 
 def gru_kernel(
@@ -372,46 +393,65 @@
     )(*operands)
 
 
-def aggregate_kernel(counts, *refs):
-    sums, weights_ref, out_ref, columns = refs[:-3], refs[-3], refs[-2], refs[-1]
-    bands = [sums[i : i + 3] for i in range(0, len(sums), 3)]
-    frame = pl.program_id(0)
-    height, width, chans = out_ref.shape[1:]
-    size = height // len(bands)
+def aggregate_kernel(pieces, first, last, counts, *refs):
+    sums, weights_ref, rest = refs[: 3 * len(pieces)], refs[3 * len(pieces)], refs[3 * len(pieces) + 1 :]
+    out_ref, columns = rest[-2:]
+    width, chans = out_ref.shape[2:]
     edge_row = jnp.zeros((1,) + columns.shape[1:], BF16)
     columns[0:1] = edge_row
-    columns[height + 1 :] = edge_row
-    count = counts[frame]
+    columns[columns.shape[0] - 1 :] = edge_row
+    count = counts[pl.program_id(0)]
     step = 8
-    for band, (a, b, c) in enumerate(bands):
-        for y in range(0, size, step):
-            span = slice(y, y + step)
-            total = a[0, span].astype(F32) + b[0, span].astype(F32) + c[0, span].astype(F32)
-            mean = (total / count).astype(BF16).astype(F32)
-            put_columns(columns, band * size + y + 1, mean)
+    at = 1
+    for i, (low, high) in enumerate(pieces):
+        for y in range(low, high, step):
+            span = slice(y, min(y + step, high))
+            a, b, c = (ref[0, span].astype(F32) for ref in sums[3 * i : 3 * i + 3])
+            mean = ((a + b + c) / count).astype(BF16).astype(F32)
+            put_columns(columns, at, mean)
+            at += mean.shape[0]
+    base = 0
+    if len(rest) == 3:
+        out_ref[0, :first] = rest[0][0]
+        base = first
     weights = weights_ref[...]
-    for y in range(0, height, step):
-        out = conv_rows(columns, y, step, weights)
-        out_ref[0, y : y + step] = out.astype(BF16).reshape(step, width, chans)
-
-
-def aggregate_of(counts, bands, weights):
+    skip = 0 if first == 0 else 1
+    for y in range(0, last - first, step):
+        rows = min(step, last - first - y)
+        out = conv_rows(columns, y + skip, rows, weights)
+        out_ref[0, base + y : base + y + rows] = out.astype(BF16).reshape(rows, width, chans)
+
+
+def aggregate_of(first, last, pieces, bands, counts, weights, earlier):
     frames, size, width, chans = bands[0][0].shape
-    height = size * len(bands)
     sums = [array for band in bands for array in band]
+    depth = sum(high - low for low, high in pieces)
+    rows = last if earlier is not None else last - first
+    operands = [counts, *sums, weights]
+    more = []
+    if earlier is not None:
+        operands.append(earlier)
+        more = [pl.BlockSpec((1,) + earlier.shape[1:], lambda f, c: (f, 0, 0, 0))]
     return pl.pallas_call(
-        aggregate_kernel,
+        functools.partial(aggregate_kernel, pieces, first, last),
         grid_spec=pltpu.PrefetchScalarGridSpec(
             num_scalar_prefetch=1,
             grid=(frames,),
-            in_specs=[pl.BlockSpec((1, size, width, chans), lambda f, c: (f, 0, 0, 0))] * len(sums) + [whole(weights)],
-            out_specs=pl.BlockSpec((1, height, width, chans), lambda f, c: (f, 0, 0, 0)),
-            scratch_shapes=[pltpu.VMEM((height + 2, width, 3 * chans), BF16)],
-        ),
-        out_shape=jax.ShapeDtypeStruct((frames, height, width, chans), BF16),
-        compiler_params=pltpu.CompilerParams(vmem_limit_bytes=VMEM_LIMIT),
-        name="aggregate",
-    )(counts, *sums, weights)
+            in_specs=[pl.BlockSpec((1, size, width, chans), lambda f, c: (f, 0, 0, 0))] * len(sums)
+            + [whole(weights)]
+            + more,
+            out_specs=pl.BlockSpec((1, rows, width, chans), lambda f, c: (f, 0, 0, 0)),
+            scratch_shapes=[pltpu.VMEM((depth + 2, width, 3 * chans), BF16)],
+        ),
+        out_shape=jax.ShapeDtypeStruct((frames, rows, width, chans), BF16),
+        compiler_params=pltpu.CompilerParams(vmem_limit_bytes=16 << 20),
+        cost_estimate=pl.CostEstimate(
+            flops=2 * frames * (last - first) * width * 9 * chans * chans,
+            bytes_accessed=8 * frames * depth * width * chans,
+            transcendentals=0,
+        ),
+        name=f"aggregate_from{first}",
+    )(*operands)
 
 
 def per_device(
@@ -446,21 +486,34 @@
     mine = me * frames + jnp.arange(frames, dtype=jnp.int32)
     counts = jnp.maximum(jnp.sum((edges[:, 0][:, None] == mine[None]).astype(F32), axis=0), 1.0)
 
-    gates = gates_of(net_state, w_gates)
-    far_top = far_swap(frame_maps[:, 1, :split], far_feat, gates)
-    motion = motion_of(meta, frame_maps, near, far_feat, w_motion)
+    base = motion_weights(w_motion, width)
+    gates = gates_of(net_state, lax.optimization_barrier((w_gates, near))[0])
+    half = edge_count // 2
+    held_meta = lax.optimization_barrier((meta, gates))[0]
+    motion = motion_of(0, half, held_meta, frame_maps, near, far_feat, base, None)
+    far_top = far_swap(frame_maps[:, 1, :split], motion)
+    motion = motion_of(half, edge_count, meta, frame_maps, near, far_feat, base, motion)
     far_low = far_swap(frame_maps[:, 1, split:], far_top, motion)
-    new_state = None
-    bands = []
-    latest = far_low
-    for band in range(2):
-        new_state, own_sum, near_sum, far_sum = gru_of(
+    size = height // 2
+
+    def gru(band, earlier):
+        return gru_of(
             band, split, meta, frame_maps, near, far_top, far_low if band else far_top,
-            motion, gates, net_state, w_input, w_candidate, new_state,
+            motion, gates, net_state, w_input, w_candidate, earlier,
         )
-        latest = far_swap(far_sum, latest)
-        bands.append((own_sum, near_swap(near_sum), latest))
-    frame_update = aggregate_of(counts, bands, w_aggregate)
+
+    new_state, own_sum, near_sum, far_sum = gru(0, None)
+    far_first = far_swap(far_sum, far_low)
+    near_first = near_swap(near_sum)
+    first_sums = (own_sum, near_first, far_first)
+    new_state, own_sum, near_sum, far_sum = gru(1, new_state)
+    far_second = far_swap(far_sum, far_first)
+    near_second = near_swap(near_sum)
+    second_sums = (own_sum, near_second, far_second)
+    upper = aggregate_of(0, size - 1, ((0, size),), (first_sums,), counts, w_aggregate, None)
+    frame_update = aggregate_of(
+        size - 1, height, ((size - 2, size), (0, size)), (first_sums, second_sums), counts, w_aggregate, upper
+    )
     return (new_state, frame_update)
 
 

time: 141 us -> 140 us (level)
  Pallas kernels: 65 us -> 70.5 us
  local copies, waits for them, and re-layouts: 11.1 us -> 7.01 us
  other arithmetic: 4.55 us -> 1.09 us
  starting transfers between devices: 17.2 us -> 20.3 us
  waiting for transfers between devices: 39.6 us -> 37.1 us
    pallas_call x2 -> x4, Pallas kernels: 28.6 us -> 32.9 us  [the longest x2 25 us: motion_of(): pl.pallas_call(kernel, grid_spec=pltpu.PrefetchScalarGridSpec(num_scalar_...]
    ppermute x5, starting transfers between devices: 16.4 us -> 19.6 us  [far_swap(): return lax.ppermute(block, 'rows', far_route)]
    convert_element_type x4 -> x0, other arithmetic: 2.79 us -> none  [the longest x1 1.48 us: motion_of(): jnp.kron(jnp.eye(2, dtype=F32), jnp.eye(width, dtype=F32)[::-1])]
    ppermute x5, waiting for transfers between devices: 39.5 us -> 37.1 us  [far_swap(): return lax.ppermute(block, 'rows', far_route)]
    slice x4 -> x0, local copies, waits for them, and re-layouts: 1.68 us -> none  [the longest x2 0.91 us: motion_of(): jnp.roll(padded[:, 1], low + width, axis=1)]
  transfers between devices with their start and end apart: 8 -> 8, of which waited for: 2 -> 4; matrix products, arithmetic and copies ran while one was open for 11% -> 6% of each run, Pallas kernels for 41% -> 39%
where the time goes in v3:
time: 140 us; the launch traced here: 137 us
  Pallas kernels  70.5 us (50%)
  waiting for transfers between devices  37.1 us (26%)
  starting transfers between devices  20.3 us (14%)
  local copies, waits for them, and re-layouts  7.01 us (5%)
    ppermute x5, waiting for transfers between devices, far_swap(): return lax.ppermute(block, 'rows', far_route)  37.1 us
    pallas_call x2, Pallas kernels, gru_of(): pl.pallas_call(kernel, grid_spec=pltpu.PrefetchScalarGridSpec(num_scalar_...  25.1 us
    pallas_call x2, Pallas kernels, motion_of(): pl.pallas_call(kernel, grid_spec=pltpu.PrefetchScalarGridSpec(num_scalar_...  25 us
    ppermute x5, starting transfers between devices, far_swap(): return lax.ppermute(block, 'rows', far_route)  19.6 us
    pallas_call x1, Pallas kernels, gates_of(): pl.pallas_call(gates_kernel, grid=(edges,), in_specs=[pl.BlockSpec((1, he...  12.5 us
    pallas_call x2, Pallas kernels, aggregate_of(): pl.pallas_call(functools.partial(aggregate_kernel, pieces, first, last),...  7.97 us
  transfers between devices with their start and end apart: 8, of which 4 were waited for; matrix products, arithmetic and copies ran while one was open for 6% of the time, Pallas kernels for 39%

profile of v3, /device:TPU:1, one launch (start us, length us, event | category | flops | bytes accessed | tf_op | source)
XLA Modules:
  0.0 137.3 jit_solution(10258224863425240307)
XLA Ops:
  0.8 2.7 %slice_bitcast_fusion = bf16[2,48,64,128]{3,2,1,0:T(8,128)(2,1)} fusion(bf16[2,2,48,64,128]{4,3,2,1,0:T(8,128)(2,1)} %own.3), kind=kLoop, calls=%fused_computation | loop fusion | bytes 3145728 | tf_op jit(solution)/shard_map/squeeze | solution.py:476
  3.5 4.5 %collective-permute-start.1 = (bf16[2,48,64,128]{3,2,1,0:T(8,128)(2,1)}, bf16[2,48,64,128]{3,2,1,0:T(8,128)(2,1)}, u32[]{:S(2)}, u32[]{:S(2)}) collective-permute-start(bf16[2,48,64,128]{3,2,1,0:T(8,128)(2,1)} %slice_bitcast_fusion), channel_id=1, source_target_pairs={{1,2},{2,1},{3,4},{4,3},{5,6},{6,5},{7,8},{8,7},{9,10},{10,9},{11,... | collective-permute-start | bytes 4718600 | tf_op jit(solution)/shard_map/ppermute | solution.py:470
  8.4 0.7 stack.3.meta.refs_0_
  9.0 0.2 fusion.2
  9.3 0.2 fusion
  9.5 0.9 pad_maximum_fusion.base_ref.refs_6_
  10.4 2.1 %slice_bitcast_fusion.1 = bf16[2,25,64,128]{3,2,1,0:T(8,128)(2,1)} fusion(bf16[2,2,48,64,128]{4,3,2,1,0:T(8,128)(2,1)} %own.3), kind=kLoop, calls=%fused_computation.1 | loop fusion | bytes 1638400 | tf_op jit(solution)/shard_map/squeeze | solution.py:494
  12.5 12.5 %gates.1.refs_6_ = bf16[4,48,64,256]{3,2,1,0:T(8,128)(2,1)} custom-call(bf16[4,48,64,128]{3,2,1,0:T(8,128)(2,1)} %state.1, bf16[1152,256]{1,0:T(8,128)(2,1)} %weights_ref), custom_call_target="tpu_custom_call" | custom-call | flops 7247757312 | bytes 9437184 | tf_op jit(solution)/shard_map/gates/pallas_call | solution.py:83
  25.0 17.5 %collective-permute-done.1.far.refs_3_ = bf16[2,48,64,128]{3,2,1,0:T(8,128)(2,1)} collective-permute-done((bf16[2,48,64,128]{3,2,1,0:T(8,128)(2,1)}, bf16[2,48,64,128]{3,2,1,0:T(8,128)(2,1)}, u32[]{:S(2)}, u32[]{:S(2)}) %collective-permute-start.1) | collective-permute-done | bytes 1572896 | tf_op jit(solution)/shard_map/ppermute | solution.py:470
  42.5 12.6 %motion_from0.1.refs_7_ = bf16[4,52,64,128]{3,2,1,0:T(8,128)(2,1)} custom-call(s32[4,6]{1,0:T(4,128)} %stack.3.meta.refs_0_, bf16[2,2,48,64,128]{4,3,2,1,0:T(8,128)(2,1)} %own.3, bf16[2,2,48,64,128]{4,3,2,1,0:T(8,128)(2,1)} %copy-done.4, bf16[2,48,64,128]{3,2,1,0:T(8,128)(2,1)} %collective-permute-done.1.far.refs_3_, ...), custom_call_target="tpu_custom_call" | custom-call | flops 4026531840 | bytes 4718592 | tf_op jit(solution)/shard_map/motion_from0/pallas_call | solution.py:207
  55.1 4.4 %collective-permute-start.2 = (bf16[2,25,64,128]{3,2,1,0:T(8,128)(2,1)S(1)}, bf16[2,25,64,128]{3,2,1,0:T(8,128)(2,1)S(1)}, u32[]{:S(2)}, u32[]{:S(2)}) collective-permute-start(bf16[2,25,64,128]{3,2,1,0:T(8,128)(2,1)S(1)} %copy-done.6), channel_id=1, source_target_pairs={{1,2},{2,1},{3,4},{4,3},{5,6},{6,5},{7,8},{8,7},{9,10},{10,9},{11,... | collective-permute-start | bytes 2457608 | tf_op jit(solution)/shard_map/ppermute | solution.py:470
  59.5 1.2 slice_bitcast_fusion.2
  60.7 12.4 %motion_from2.1.refs_5_.motion = bf16[4,52,64,128]{3,2,1,0:T(8,128)(2,1)} custom-call(s32[4,6]{1,0:T(4,128)} %stack.3.meta.refs_0_, bf16[2,2,48,64,128]{4,3,2,1,0:T(8,128)(2,1)} %own.3, bf16[2,2,48,64,128]{4,3,2,1,0:T(8,128)(2,1)} %copy-done.4, bf16[2,48,64,128]{3,2,1,0:T(8,128)(2,1)} %collective-permute-done.1.far.refs_3_, ...), custom_call_target="tpu_custom_call", output_to_operand_aliasing={{}: (7, {})} | custom-call | flops 4026531840 | bytes 4718592 | tf_op jit(solution)/shard_map/motion_from2/pallas_call | solution.py:207
  73.1 3.7 %collective-permute-done.2.refs_3_.refs_4_.far_top = bf16[2,25,64,128]{3,2,1,0:T(8,128)(2,1)S(1)} collective-permute-done((bf16[2,25,64,128]{3,2,1,0:T(8,128)(2,1)S(1)}, bf16[2,25,64,128]{3,2,1,0:T(8,128)(2,1)S(1)}, u32[]{:S(2)}, u32[]{:S(2)}) %collective-permute-start.2) | collective-permute-done | bytes 819232 | tf_op jit(solution)/shard_map/ppermute | solution.py:470
  76.8 4.4 %collective-permute-start.3 = (bf16[2,23,64,128]{3,2,1,0:T(8,128)(2,1)S(1)}, bf16[2,23,64,128]{3,2,1,0:T(8,128)(2,1)S(1)}, u32[]{:S(2)}, u32[]{:S(2)}) collective-permute-start(bf16[2,23,64,128]{3,2,1,0:T(8,128)(2,1)S(1)} %slice_bitcast_fusion.2), channel_id=1, source_target_pairs={{1,2},{2,1},{3,4},{4,3},{5,6},{6,5},{7,8},{8,7},{9,10},{10,9},{11,... | collective-permute-start | bytes 2261000 | tf_op jit(solution)/shard_map/ppermute | solution.py:470
  81.2 12.4 %gru_band0.1 = (bf16[4,48,64,128]{3,2,1,0:T(8,128)(2,1)}, bf16[2,24,64,128]{3,2,1,0:T(8,128)(2,1)}, bf16[2,24,64,128]{3,2,1,0:T(8,128)(2,1)}, bf16[2,24,64,128]{3,2,1,0:T(8,128)(2,1)}) custom-call(s32[4,6]{1,0:T(4,128)} %stack.3.meta.refs_0_, bf16[2,2,48,64,128]{4,3,2,1,0:T(8,128)(2,1)} %own.3, bf16[2,2,48,64,128]{4,3,2,1,0:T(8,128)(2,1)} %copy-done.4, ...), custom_call_target="tpu_custom_call" | custom-call | flops 3145728000 | bytes 9830400 | tf_op jit(solution)/shard_map/gru_band0/pallas_call | solution.py:365
  93.6 1.3 collective-permute-done.3.far_low
  94.9 4.4 %collective-permute-start.5 = (bf16[2,24,64,128]{3,2,1,0:T(8,128)(2,1)}, bf16[2,24,64,128]{3,2,1,0:T(8,128)(2,1)S(1)}, u32[]{:S(2)}, u32[]{:S(2)}) collective-permute-start(bf16[2,24,64,128]{3,2,1,0:T(8,128)(2,1)} %get-tuple-element.25), channel_id=1, source_target_pairs={{1,2},{2,1},{3,4},{4,3},{5,6},{6,5},{7,8},{8,7},{9,10},{10,9},{11,... | collective-permute-start | bytes 2359304 | tf_op jit(solution)/shard_map/ppermute | solution.py:470
  99.4 12.7 %gru_band1.1 = (bf16[4,48,64,128]{3,2,1,0:T(8,128)(2,1)}, bf16[2,24,64,128]{3,2,1,0:T(8,128)(2,1)}, bf16[2,24,64,128]{3,2,1,0:T(8,128)(2,1)}, bf16[2,24,64,128]{3,2,1,0:T(8,128)(2,1)}) custom-call(s32[4,6]{1,0:T(4,128)} %stack.3.meta.refs_0_, bf16[2,2,48,64,128]{4,3,2,1,0:T(8,128)(2,1)} %own.3, ...), custom_call_target="tpu_custom_call", output_to_operand_aliasing={{0}: (10, {})} | custom-call | flops 3145728000 | bytes 9830400 | tf_op jit(solution)/shard_map/gru_band1/pallas_call | solution.py:365
  112.1 0.5 collective-permute-start.6
  112.7 1.9 %collective-permute-start.7 = (bf16[2,24,64,128]{3,2,1,0:T(8,128)(2,1)}, bf16[2,24,64,128]{3,2,1,0:T(8,128)(2,1)}, u32[]{:S(2)}, u32[]{:S(2)}) collective-permute-start(bf16[2,24,64,128]{3,2,1,0:T(8,128)(2,1)} %get-tuple-element.29), channel_id=1, source_target_pairs={{1,2},{2,1},{3,4},{4,3},{5,6},{6,5},{7,8},{8,7},{9,10},{10,9},{11,... | collective-permute-start | bytes 2359304 | tf_op jit(solution)/shard_map/ppermute | solution.py:470
  114.8 2.9 %aggregate_from0.1.refs_7_ = bf16[2,23,64,128]{3,2,1,0:T(8,128)(2,1)S(1)} custom-call(f32[2]{0:T(128)S(1)} %broadcast_maximum_fusion.counts, bf16[2,24,64,128]{3,2,1,0:T(8,128)(2,1)S(1)} %copy-done.1, bf16[2,24,64,128]{3,2,1,0:T(8,128)(2,1)S(1)} %collective-permute-done.4.refs_1_, bf16[2,24,64,128]{3,2,1,0:T(8,128)(2,1)S(1)} %collective-permute-done.5.refs_2_, ...), custom_call_target="tpu_custom_call" | custom-call | flops 868220928 | bytes 3145728 | tf_op jit(solution)/shard_map/aggregate_from0/pallas_call | solution.py:435
  117.7 14.5 %collective-permute-done.7.refs_5_ = bf16[2,24,64,128]{3,2,1,0:T(8,128)(2,1)} collective-permute-done((bf16[2,24,64,128]{3,2,1,0:T(8,128)(2,1)}, bf16[2,24,64,128]{3,2,1,0:T(8,128)(2,1)}, u32[]{:S(2)}, u32[]{:S(2)}) %collective-permute-start.7) | collective-permute-done | bytes 786464 | tf_op jit(solution)/shard_map/ppermute | solution.py:470
  132.2 5.1 %aggregate_from23.1 = bf16[2,48,64,128]{3,2,1,0:T(8,128)(2,1)} custom-call(f32[2]{0:T(128)S(1)} %broadcast_maximum_fusion.counts, bf16[2,24,64,128]{3,2,1,0:T(8,128)(2,1)S(1)} %copy-done.1, bf16[2,24,64,128]{3,2,1,0:T(8,128)(2,1)S(1)} %collective-permute-done.4.refs_1_, bf16[2,24,64,128]{3,2,1,0:T(8,128)(2,1)S(1)} %collective-permute-done.5.refs_2_, ...), custom_call_target="tpu_custom_call" | custom-call | flops 943718400 | bytes 3407872 | tf_op jit(solution)/shard_map/aggregate_from23/pallas_call | solution.py:435
  (39 shorter events, 0.8 us)
Async XLA Ops:
  0.6 8.4 %copy-start = (bf16[81,128]{1,0:T(8,128)(2,1)S(1)}, bf16[81,128]{1,0:T(8,128)(2,1)}, u32[]{:S(2)}) copy-start(bf16[81,128]{1,0:T(8,128)(2,1)} %param.19) | copy-start | bytes 62212
  0.6 8.4 %copy-start.9 = (bf16[5,128,81]{1,2,0:T(8,128)(2,1)S(1)}, bf16[5,128,81]{1,2,0:T(8,128)(2,1)}, u32[]{:S(2)}) copy-start(bf16[5,128,81]{1,2,0:T(8,128)(2,1)} %constant.48.clone) | copy-start | bytes 311044
  0.7 8.6 %copy-start.8 = (bf16[5,128,81]{1,2,0:T(8,128)(2,1)S(1)}, bf16[5,128,81]{1,2,0:T(8,128)(2,1)}, u32[]{:S(2)}) copy-start(bf16[5,128,81]{1,2,0:T(8,128)(2,1)} %constant.49.clone) | copy-start | bytes 311044
  0.7 7.3 %copy-start.11 = (s32[64,2]{0,1:T(2,128)S(1)}, s32[64,2]{0,1:T(2,128)}, u32[]{:S(2)}) copy-start(s32[64,2]{0,1:T(2,128)} %param.17) | copy-start | bytes 1540
  0.7 7.6 %copy-start.10 = (s32[4,2]{0,1:T(2,128)S(1)}, s32[4,2]{0,1:T(2,128)}, u32[]{:S(2)}) copy-start(s32[4,2]{0,1:T(2,128)} %param.18) | copy-start | bytes 100
  0.7 11.8 %collective-permute-start = (bf16[2,2,48,64,128]{4,3,2,1,0:T(8,128)(2,1)}, bf16[2,2,48,64,128]{4,3,2,1,0:T(8,128)(2,1)S(1)}, u32[]{:S(2)}, u32[]{:S(2)}) collective-permute-start(bf16[2,2,48,64,128]{4,3,2,1,0:T(8,128)(2,1)} %own.3), channel_id=1, source_target_pairs={{0,1},{1,0},{2,3},{3,2},{4,5},{5,4},{6,7},{7,6},{8,9},{9,8},{10,11... | collective-permute-start | bytes 9437192 | tf_op jit(solution)/shard_map/ppermute | solution.py:473
  3.5 39.0 %collective-permute-start.1 = (bf16[2,48,64,128]{3,2,1,0:T(8,128)(2,1)}, bf16[2,48,64,128]{3,2,1,0:T(8,128)(2,1)}, u32[]{:S(2)}, u32[]{:S(2)}) collective-permute-start(bf16[2,48,64,128]{3,2,1,0:T(8,128)(2,1)} %slice_bitcast_fusion), channel_id=1, source_target_pairs={{1,2},{2,1},{3,4},{4,3},{5,6},{6,5},{7,8},{8,7},{9,10},{10,9},{11,... | collective-permute-start | bytes 4718600 | tf_op jit(solution)/shard_map/ppermute | solution.py:470
  12.5 12.5 %copy-start.4 = (bf16[2,2,48,64,128]{4,3,2,1,0:T(8,128)(2,1)}, bf16[2,2,48,64,128]{4,3,2,1,0:T(8,128)(2,1)S(1)}, u32[]{:S(2)}) copy-start(bf16[2,2,48,64,128]{4,3,2,1,0:T(8,128)(2,1)S(1)} %collective-permute-done.near.refs_2_) | copy-start | bytes 9437188
  42.5 12.6 %copy-start.6 = (bf16[2,25,64,128]{3,2,1,0:T(8,128)(2,1)S(1)}, bf16[2,25,64,128]{3,2,1,0:T(8,128)(2,1)}, u32[]{:S(2)}) copy-start(bf16[2,25,64,128]{3,2,1,0:T(8,128)(2,1)} %slice_bitcast_fusion.1) | copy-start | bytes 2457604
  55.1 21.7 %collective-permute-start.2 = (bf16[2,25,64,128]{3,2,1,0:T(8,128)(2,1)S(1)}, bf16[2,25,64,128]{3,2,1,0:T(8,128)(2,1)S(1)}, u32[]{:S(2)}, u32[]{:S(2)}) collective-permute-start(bf16[2,25,64,128]{3,2,1,0:T(8,128)(2,1)S(1)} %copy-done.6), channel_id=1, source_target_pairs={{1,2},{2,1},{3,4},{4,3},{5,6},{6,5},{7,8},{8,7},{9,10},{10,9},{11,... | collective-permute-start | bytes 2457608 | tf_op jit(solution)/shard_map/ppermute | solution.py:470
  76.8 4.4 %copy-start.5 = (bf16[2,25,64,128]{3,2,1,0:T(8,128)(2,1)}, bf16[2,25,64,128]{3,2,1,0:T(8,128)(2,1)S(1)}, u32[]{:S(2)}) copy-start(bf16[2,25,64,128]{3,2,1,0:T(8,128)(2,1)S(1)} %collective-permute-done.2.refs_3_.refs_4_.far_top) | copy-start | bytes 2457604
  76.8 18.1 %collective-permute-start.3 = (bf16[2,23,64,128]{3,2,1,0:T(8,128)(2,1)S(1)}, bf16[2,23,64,128]{3,2,1,0:T(8,128)(2,1)S(1)}, u32[]{:S(2)}, u32[]{:S(2)}) collective-permute-start(bf16[2,23,64,128]{3,2,1,0:T(8,128)(2,1)S(1)} %slice_bitcast_fusion.2), channel_id=1, source_target_pairs={{1,2},{2,1},{3,4},{4,3},{5,6},{6,5},{7,8},{8,7},{9,10},{10,9},{11,... | collective-permute-start | bytes 2261000 | tf_op jit(solution)/shard_map/ppermute | solution.py:470
  94.9 4.5 %copy-start.7 = (bf16[2,23,64,128]{3,2,1,0:T(8,128)(2,1)}, bf16[2,23,64,128]{3,2,1,0:T(8,128)(2,1)S(1)}, u32[]{:S(2)}) copy-start(bf16[2,23,64,128]{3,2,1,0:T(8,128)(2,1)S(1)} %collective-permute-done.3.far_low) | copy-start | bytes 2260996
  94.9 17.7 %collective-permute-start.5 = (bf16[2,24,64,128]{3,2,1,0:T(8,128)(2,1)}, bf16[2,24,64,128]{3,2,1,0:T(8,128)(2,1)S(1)}, u32[]{:S(2)}, u32[]{:S(2)}) collective-permute-start(bf16[2,24,64,128]{3,2,1,0:T(8,128)(2,1)} %get-tuple-element.25), channel_id=1, source_target_pairs={{1,2},{2,1},{3,4},{4,3},{5,6},{6,5},{7,8},{8,7},{9,10},{10,9},{11,... | collective-permute-start | bytes 2359304 | tf_op jit(solution)/shard_map/ppermute | solution.py:470
  99.3 15.5 %collective-permute-start.4 = (bf16[2,24,64,128]{3,2,1,0:T(8,128)(2,1)}, bf16[2,24,64,128]{3,2,1,0:T(8,128)(2,1)S(1)}, u32[]{:S(2)}, u32[]{:S(2)}) collective-permute-start(bf16[2,24,64,128]{3,2,1,0:T(8,128)(2,1)} %get-tuple-element.23), channel_id=1, source_target_pairs={{0,1},{1,0},{2,3},{3,2},{4,5},{5,4},{6,7},{7,6},{8,9},{9,8},{10,11... | collective-permute-start | bytes 2359304 | tf_op jit(solution)/shard_map/ppermute | solution.py:473
  99.4 15.4 %copy-start.1 = (bf16[2,24,64,128]{3,2,1,0:T(8,128)(2,1)S(1)}, bf16[2,24,64,128]{3,2,1,0:T(8,128)(2,1)}, u32[]{:S(2)}) copy-start(bf16[2,24,64,128]{3,2,1,0:T(8,128)(2,1)} %get-tuple-element.22.refs_0_) | copy-start | bytes 2359300
  99.4 15.4 %copy-start.2 = (bf16[1152,128]{1,0:T(8,128)(2,1)S(1)}, bf16[1152,128]{1,0:T(8,128)(2,1)}, u32[]{:S(2)}) copy-start(bf16[1152,128]{1,0:T(8,128)(2,1)} %refs_6_.1) | copy-start | bytes 884740
  112.1 20.1 %copy-start.3 = (bf16[2,24,64,128]{3,2,1,0:T(8,128)(2,1)S(1)}, bf16[2,24,64,128]{3,2,1,0:T(8,128)(2,1)}, u32[]{:S(2)}) copy-start(bf16[2,24,64,128]{3,2,1,0:T(8,128)(2,1)} %get-tuple-element.26.refs_3_) | copy-start | bytes 2359300
  112.1 5.6 %collective-permute-start.6 = (bf16[2,24,64,128]{3,2,1,0:T(8,128)(2,1)}, bf16[2,24,64,128]{3,2,1,0:T(8,128)(2,1)}, u32[]{:S(2)}, u32[]{:S(2)}) collective-permute-start(bf16[2,24,64,128]{3,2,1,0:T(8,128)(2,1)} %get-tuple-element.27), channel_id=1, source_target_pairs={{0,1},{1,0},{2,3},{3,2},{4,5},{5,4},{6,7},{7,6},{8,9},{9,8},{10,11... | collective-permute-start | bytes 2359304 | tf_op jit(solution)/shard_map/ppermute | solution.py:473
  112.7 19.6 %collective-permute-start.7 = (bf16[2,24,64,128]{3,2,1,0:T(8,128)(2,1)}, bf16[2,24,64,128]{3,2,1,0:T(8,128)(2,1)}, u32[]{:S(2)}, u32[]{:S(2)}) collective-permute-start(bf16[2,24,64,128]{3,2,1,0:T(8,128)(2,1)} %get-tuple-element.29), channel_id=1, source_target_pairs={{1,2},{2,1},{3,4},{4,3},{5,6},{6,5},{7,8},{8,7},{9,10},{10,9},{11,... | collective-permute-start | bytes 2359304 | tf_op jit(solution)/shard_map/ppermute | solution.py:470

commit v4 on v3

--- a/solution.py
+++ b/solution.py
@@ -234,22 +234,21 @@
 def gru_kernel(
     first,
     last,
-    split,
     meta,
     own,
     near,
-    far_top,
-    far_low,
+    far,
     motion,
     gates,
     state,
     w_input,
     w_candidate,
-    alias,
+    _,
     new_ref,
     own_sum,
-    near_sum,
     far_sum,
+    near_top,
+    near_low,
     ctx_buf,
     motion_buf,
     gates_buf,
@@ -274,28 +273,18 @@
         pltpu.make_async_copy(motion.at[e, pl.ds(top + 1, rows)], motion_buf.at[s], sems.at[1, s]).start()
         pltpu.make_async_copy(gates.at[e, pl.ds(top, rows)], gates_buf.at[s], sems.at[2, s]).start()
         pltpu.make_async_copy(state.at[e, pl.ds(top, rows)], state_buf.at[s], sems.at[3, s]).start()
-        above = min(max(split - top, 0), rows)
-        for piece, far, low, high, sem in ((0, far_top, 0, above, 0), (1, far_low, above, rows, 4)):
-            if high > low:
-                base = top + low
-                fetch(
-                    (
-                        (buf == 0, own.at[frame, 1, pl.ds(base, high - low)]),
-                        (buf == 1, far.at[frame, pl.ds(base - piece * split, high - low)]),
-                        (buf == 2, near.at[frame, 1, pl.ds(base, high - low)]),
-                    ),
-                    ctx_buf.at[s, pl.ds(low, high - low)],
-                    sems.at[sem, s],
-                )
+        cases = (
+            (buf == 0, own.at[frame, 1, pl.ds(top, rows)]),
+            (buf == 1, far.at[frame, pl.ds(top, rows)]),
+            (buf == 2, near.at[frame, 1, pl.ds(top, rows)]),
+        )
+        fetch(cases, ctx_buf.at[s], sems.at[0, s])
 
     def finish(s):
         await_copy(motion_buf.at[s], sems.at[1, s])
         await_copy(gates_buf.at[s], sems.at[2, s])
         await_copy(state_buf.at[s], sems.at[3, s])
-        above = min(max(split - top, 0), rows)
-        for low, high, sem in ((0, above, 0), (above, rows, 4)):
-            if high > low:
-                await_copy(ctx_buf.at[s, pl.ds(low, high - low)], sems.at[sem, s])
+        await_copy(ctx_buf.at[s], sems.at[0, s])
 
     @pl.when(edge == 0)
     def _():
@@ -341,34 +330,45 @@
 
     @pl.when(edge == edges - 1)
     def _():
-        for i, out in enumerate((own_sum, far_sum, near_sum)):
-            out[...] = totals[i * frames : (i + 1) * frames].astype(BF16)
-
-
-def gru_of(band, split, meta, own, near, far_top, far_low, motion, gates, state, w_input, w_candidate, earlier):
+        half = near_top.shape[1]
+        own_sum[...] = totals[:frames].astype(BF16)
+        far_sum[...] = totals[frames : 2 * frames].astype(BF16)
+        near_top[...] = totals[2 * frames :, :half].astype(BF16)
+        near_low[...] = totals[2 * frames :, half:].astype(BF16)
+
+
+def gru_of(band, meta, own, near, far, motion, gates, state, w_input, w_candidate, earlier):
     frames, _, height, width, chans = own.shape
     edges = state.shape[0]
     size = height // 2
     first, last = band * size, (band + 1) * size
     rows = min(last + 1, height) - max(first - 1, 0)
     sums = jax.ShapeDtypeStruct((frames, size, width, chans), BF16)
+    pieces = jax.ShapeDtypeStruct((frames, size // 2, width, chans), BF16)
     sum_spec = pl.BlockSpec(sums.shape, lambda e, m: (0, 0, 0, 0))
-    body = functools.partial(gru_kernel, first, last, split)
-    operands = [meta, own, near, far_top, far_low, motion, gates, state, w_input, w_candidate]
+    piece_spec = pl.BlockSpec(pieces.shape, lambda e, m: (0, 0, 0, 0))
+    body = functools.partial(gru_kernel, first, last)
+    operands = [meta, own, near, far, motion, gates, state, w_input, w_candidate]
     if earlier is None:
-        kernel = lambda *refs: body(*refs[:10], None, *refs[10:])
+        kernel = lambda *refs: body(*refs[:9], None, *refs[9:])
         aliases = {}
     else:
         kernel = body
         operands.append(earlier)
-        aliases = {10: 0}
+        aliases = {9: 0}
     return pl.pallas_call(
         kernel,
         grid_spec=pltpu.PrefetchScalarGridSpec(
             num_scalar_prefetch=1,
             grid=(edges,),
-            in_specs=[any_spec()] * 7 + [whole(w_input), whole(w_candidate)] + [any_spec()] * (len(operands) - 10),
-            out_specs=[pl.BlockSpec((1, size, width, chans), lambda e, m: (e, band, 0, 0)), sum_spec, sum_spec, sum_spec],
+            in_specs=[any_spec()] * 6 + [whole(w_input), whole(w_candidate)] + [any_spec()] * (len(operands) - 9),
+            out_specs=[
+                pl.BlockSpec((1, size, width, chans), lambda e, m: (e, band, 0, 0)),
+                sum_spec,
+                sum_spec,
+                piece_spec,
+                piece_spec,
+            ],
             scratch_shapes=[
                 pltpu.VMEM((2, rows, width, chans), BF16),
                 pltpu.VMEM((2, rows, width, chans), BF16),
@@ -378,10 +378,16 @@
                 pltpu.VMEM((rows, width, chans), F32),
                 pltpu.VMEM((rows, width, chans), F32),
                 pltpu.VMEM((3 * frames, size, width, chans), F32),
-                pltpu.SemaphoreType.DMA((5, 2)),
+                pltpu.SemaphoreType.DMA((4, 2)),
             ],
         ),
-        out_shape=[jax.ShapeDtypeStruct(state.shape, BF16), sums, sums, sums],
+        out_shape=[
+            jax.ShapeDtypeStruct(state.shape, BF16),
+            sums,
+            sums,
+            pieces,
+            pieces,
+        ],
         input_output_aliases=aliases,
         compiler_params=pltpu.CompilerParams(vmem_limit_bytes=VMEM_LIMIT),
         cost_estimate=pl.CostEstimate(
@@ -394,22 +400,26 @@
 
 
 def aggregate_kernel(pieces, first, last, counts, *refs):
-    sums, weights_ref, rest = refs[: 3 * len(pieces)], refs[3 * len(pieces)], refs[3 * len(pieces) + 1 :]
+    sums, weights_ref, rest = refs[: 4 * len(pieces)], refs[4 * len(pieces)], refs[4 * len(pieces) + 1 :]
     out_ref, columns = rest[-2:]
     width, chans = out_ref.shape[2:]
     edge_row = jnp.zeros((1,) + columns.shape[1:], BF16)
     columns[0:1] = edge_row
     columns[columns.shape[0] - 1 :] = edge_row
     count = counts[pl.program_id(0)]
-    step = 8
     at = 1
     for i, (low, high) in enumerate(pieces):
-        for y in range(low, high, step):
-            span = slice(y, min(y + step, high))
-            a, b, c = (ref[0, span].astype(F32) for ref in sums[3 * i : 3 * i + 3])
-            mean = ((a + b + c) / count).astype(BF16).astype(F32)
-            put_columns(columns, at, mean)
-            at += mean.shape[0]
+        own, far, *near = sums[4 * i : 4 * i + 4]
+        half = near[0].shape[1]
+        for k in range(2):
+            top, end = max(low - k * half, 0), min(high - k * half, half)
+            if end > top:
+                span = slice(k * half + top, k * half + end)
+                total = own[0, span].astype(F32) + far[0, span].astype(F32) + near[k][0, top:end].astype(F32)
+                mean = (total / count).astype(BF16).astype(F32)
+                put_columns(columns, at, mean)
+                at += end - top
+    step = 8
     base = 0
     if len(rest) == 3:
         out_ref[0, :first] = rest[0][0]
@@ -423,7 +433,7 @@
 
 
 def aggregate_of(first, last, pieces, bands, counts, weights, earlier):
-    frames, size, width, chans = bands[0][0].shape
+    frames, _, width, chans = bands[0][0].shape
     sums = [array for band in bands for array in band]
     depth = sum(high - low for low, high in pieces)
     rows = last if earlier is not None else last - first
@@ -437,7 +447,7 @@
         grid_spec=pltpu.PrefetchScalarGridSpec(
             num_scalar_prefetch=1,
             grid=(frames,),
-            in_specs=[pl.BlockSpec((1, size, width, chans), lambda f, c: (f, 0, 0, 0))] * len(sums)
+            in_specs=[pl.BlockSpec((1,) + array.shape[1:], lambda f, c: (f, 0, 0, 0)) for array in sums]
             + [whole(weights)]
             + more,
             out_specs=pl.BlockSpec((1, rows, width, chans), lambda f, c: (f, 0, 0, 0)),
@@ -472,7 +482,6 @@
     def near_swap(block):
         return lax.ppermute(block, "rows", near_route)
 
-    split = height // 2 + 1
     far_feat = far_swap(frame_maps[:, 0])
     near = near_swap(frame_maps)
 
@@ -491,28 +500,25 @@
     half = edge_count // 2
     held_meta = lax.optimization_barrier((meta, gates))[0]
     motion = motion_of(0, half, held_meta, frame_maps, near, far_feat, base, None)
-    far_top = far_swap(frame_maps[:, 1, :split], motion)
+    context = lax.optimization_barrier((frame_maps, near))[0][:, 1]
+    far_ctx = far_swap(context, motion)
     motion = motion_of(half, edge_count, meta, frame_maps, near, far_feat, base, motion)
-    far_low = far_swap(frame_maps[:, 1, split:], far_top, motion)
+    maps = (meta, frame_maps, near, far_ctx, motion, gates, net_state, w_input, w_candidate)
+
+    new_state, own_first, far_sum, *near_first = gru_of(0, *maps, None)
+    far_first = far_swap(far_sum)
+    new_state, own_second, far_sum, *near_second = gru_of(1, *maps, new_state)
+    far_second = far_swap(far_sum, far_first)
+    near_first, near_second = (
+        [near_swap(piece) for piece in lax.optimization_barrier((*pieces, far_first))[:2]]
+        for pieces in (near_first, near_second)
+    )
+    first = (own_first, far_first, *near_first)
+    second = (own_second, far_second, *near_second)
     size = height // 2
-
-    def gru(band, earlier):
-        return gru_of(
-            band, split, meta, frame_maps, near, far_top, far_low if band else far_top,
-            motion, gates, net_state, w_input, w_candidate, earlier,
-        )
-
-    new_state, own_sum, near_sum, far_sum = gru(0, None)
-    far_first = far_swap(far_sum, far_low)
-    near_first = near_swap(near_sum)
-    first_sums = (own_sum, near_first, far_first)
-    new_state, own_sum, near_sum, far_sum = gru(1, new_state)
-    far_second = far_swap(far_sum, far_first)
-    near_second = near_swap(near_sum)
-    second_sums = (own_sum, near_second, far_second)
-    upper = aggregate_of(0, size - 1, ((0, size),), (first_sums,), counts, w_aggregate, None)
+    upper = aggregate_of(0, size - 1, ((0, size),), (first,), counts, w_aggregate, None)
     frame_update = aggregate_of(
-        size - 1, height, ((size - 2, size), (0, size)), (first_sums, second_sums), counts, w_aggregate, upper
+        size - 1, height, ((size - 2, size), (0, size)), (first, second), counts, w_aggregate, upper
     )
     return (new_state, frame_update)
 

time: 140 us -> 133 us (0.950); the launches traced: 137 us -> 133 us
  Pallas kernels: 70.5 us -> 68.3 us
  starting transfers between devices: 20.3 us -> 18.9 us
    squeeze x2 -> x1, local copies, waits for them, and re-layouts: 3.27 us -> 1.26 us  [per_device(): context = lax.optimization_barrier((frame_maps, near))[0][:, 1]]
    ppermute x5 -> x4, starting transfers between devices: 19.6 us -> 17.7 us  [far_swap(): return lax.ppermute(block, 'rows', far_route)]
    ppermute x5 -> x4, waiting for transfers between devices: 37.1 us -> 35.9 us  [far_swap(): return lax.ppermute(block, 'rows', far_route)]
  transfers between devices with their start and end apart: 8 -> 9, of which waited for: 4 -> 6; matrix products, arithmetic and copies ran while one was open for 6% -> 5% of each run, Pallas kernels for 39% -> 30%
where the time goes in v4:
time: 133 us
  Pallas kernels  68.3 us (51%)
  waiting for transfers between devices  37.2 us (28%)
  starting transfers between devices  18.9 us (14%)
  local copies, waits for them, and re-layouts  6.13 us (5%)
    ppermute x4, waiting for transfers between devices, far_swap(): return lax.ppermute(block, 'rows', far_route)  35.9 us
    pallas_call x2, Pallas kernels, gru_of(): pl.pallas_call(kernel, grid_spec=pltpu.PrefetchScalarGridSpec(num_scalar_...  25 us
    pallas_call x2, Pallas kernels, motion_of(): pl.pallas_call(kernel, grid_spec=pltpu.PrefetchScalarGridSpec(num_scalar_...  24.8 us
    ppermute x4, starting transfers between devices, far_swap(): return lax.ppermute(block, 'rows', far_route)  17.7 us
    pallas_call x1, Pallas kernels, gates_of(): pl.pallas_call(gates_kernel, grid=(edges,), in_specs=[pl.BlockSpec((1, he...  11.6 us
    pallas_call x2, Pallas kernels, aggregate_of(): pl.pallas_call(functools.partial(aggregate_kernel, pieces, first, last),...  6.85 us
    squeeze x1, local copies, waits for them, and re-layouts, per_device(): far_feat = far_swap(frame_maps[:, 0])  2.67 us
  transfers between devices with their start and end apart: 9, of which 6 were waited for; matrix products, arithmetic and copies ran while one was open for 5% of the time, Pallas kernels for 30%

profile of v4, /device:TPU:1, one launch (start us, length us, event | category | flops | bytes accessed | tf_op | source)
XLA Modules:
  0.0 133.0 jit_solution(13986406605229827552)
XLA Ops:
  0.8 2.7 %slice_bitcast_fusion.1 = bf16[2,48,64,128]{3,2,1,0:T(8,128)(2,1)} fusion(bf16[2,2,48,64,128]{4,3,2,1,0:T(8,128)(2,1)} %own.3), kind=kLoop, calls=%fused_computation.1 | loop fusion | bytes 3145728 | tf_op jit(solution)/shard_map/squeeze | solution.py:485
  3.5 4.5 %collective-permute-start.1 = (bf16[2,48,64,128]{3,2,1,0:T(8,128)(2,1)}, bf16[2,48,64,128]{3,2,1,0:T(8,128)(2,1)}, u32[]{:S(2)}, u32[]{:S(2)}) collective-permute-start(bf16[2,48,64,128]{3,2,1,0:T(8,128)(2,1)} %slice_bitcast_fusion.1), channel_id=1, source_target_pairs={{1,2},{2,1},{3,4},{4,3},{5,6},{6,5},{7,8},{8,7},{9,10},{10,9},{11,... | collective-permute-start | bytes 4718600 | tf_op jit(solution)/shard_map/ppermute | solution.py:480
  8.4 0.7 stack.3.meta.refs_0_
  9.5 0.9 pad_maximum_fusion.base_ref.refs_6_
  10.4 11.6 %gates.1.refs_5_ = bf16[4,48,64,256]{3,2,1,0:T(8,128)(2,1)} custom-call(bf16[4,48,64,128]{3,2,1,0:T(8,128)(2,1)} %state.1, bf16[1152,256]{1,0:T(8,128)(2,1)} %weights_ref), custom_call_target="tpu_custom_call" | custom-call | flops 7247757312 | bytes 9437184 | tf_op jit(solution)/shard_map/gates/pallas_call | solution.py:83
  22.0 1.3 slice_bitcast_fusion
  23.3 19.2 %collective-permute-done.1.far.refs_3_ = bf16[2,48,64,128]{3,2,1,0:T(8,128)(2,1)} collective-permute-done((bf16[2,48,64,128]{3,2,1,0:T(8,128)(2,1)}, bf16[2,48,64,128]{3,2,1,0:T(8,128)(2,1)}, u32[]{:S(2)}, u32[]{:S(2)}) %collective-permute-start.1) | collective-permute-done | bytes 1572896 | tf_op jit(solution)/shard_map/ppermute | solution.py:480
  42.5 12.4 %motion_from0.1.refs_7_ = bf16[4,52,64,128]{3,2,1,0:T(8,128)(2,1)} custom-call(s32[4,6]{1,0:T(4,128)} %stack.3.meta.refs_0_, bf16[2,2,48,64,128]{4,3,2,1,0:T(8,128)(2,1)} %own.3, bf16[2,2,48,64,128]{4,3,2,1,0:T(8,128)(2,1)} %collective-permute-done.near.refs_2_, bf16[2,48,64,128]{3,2,1,0:T(8,128)(2,1)} %collective-permute-done.1.far.refs_3_, ...), custom_call_target="tpu_custom_call" | custom-call | flops 4026531840 | bytes 4718592 | tf_op jit(solution)/shard_map/motion_from0/pallas_call | solution.py:207
  54.9 4.4 %collective-permute-start.2 = (bf16[2,48,64,128]{3,2,1,0:T(8,128)(2,1)S(1)}, bf16[2,48,64,128]{3,2,1,0:T(8,128)(2,1)S(1)}, u32[]{:S(2)}, u32[]{:S(2)}) collective-permute-start(bf16[2,48,64,128]{3,2,1,0:T(8,128)(2,1)S(1)} %copy-done.6), channel_id=1, source_target_pairs={{1,2},{2,1},{3,4},{4,3},{5,6},{6,5},{7,8},{8,7},{9,10},{10,9},{11,... | collective-permute-start | bytes 4718600 | tf_op jit(solution)/shard_map/ppermute | solution.py:480
  59.3 12.4 %motion_from2.1.refs_4_.motion = bf16[4,52,64,128]{3,2,1,0:T(8,128)(2,1)} custom-call(s32[4,6]{1,0:T(4,128)} %stack.3.meta.refs_0_, bf16[2,2,48,64,128]{4,3,2,1,0:T(8,128)(2,1)} %own.3, bf16[2,2,48,64,128]{4,3,2,1,0:T(8,128)(2,1)} %collective-permute-done.near.refs_2_, ...), custom_call_target="tpu_custom_call", output_to_operand_aliasing={{}: (7, {})} | custom-call | flops 4026531840 | bytes 4718592 | tf_op jit(solution)/shard_map/motion_from2/pallas_call | solution.py:207
  71.8 7.5 %collective-permute-done.2.refs_3_.far = bf16[2,48,64,128]{3,2,1,0:T(8,128)(2,1)S(1)} collective-permute-done((bf16[2,48,64,128]{3,2,1,0:T(8,128)(2,1)S(1)}, bf16[2,48,64,128]{3,2,1,0:T(8,128)(2,1)S(1)}, u32[]{:S(2)}, u32[]{:S(2)}) %collective-permute-start.2) | collective-permute-done | bytes 1572896 | tf_op jit(solution)/shard_map/ppermute | solution.py:480
  79.3 1.1 copy-done.5
  80.4 12.4 %gru_band0.1 = (bf16[4,48,64,128]{3,2,1,0:T(8,128)(2,1)}, bf16[2,24,64,128]{3,2,1,0:T(8,128)(2,1)}, bf16[2,24,64,128]{3,2,1,0:T(8,128)(2,1)}, bf16[2,12,64,128]{3,2,1,0:T(8,128)(2,1)}, bf16[2,12,64,128]{3,2,1,0:T(8,128)(2,1)}) custom-call(s32[4,6]{1,0:T(4,128)} %stack.3.meta.refs_0_, bf16[2,2,48,64,128]{4,3,2,1,0:T(8,128)(2,1)} %own.3, ...), custom_call_target="tpu_custom_call" | custom-call | flops 3145728000 | bytes 9830400 | tf_op jit(solution)/shard_map/gru_band0/pallas_call | solution.py:359
  92.8 4.4 %collective-permute-start.3 = (bf16[2,24,64,128]{3,2,1,0:T(8,128)(2,1)}, bf16[2,24,64,128]{3,2,1,0:T(8,128)(2,1)S(1)}, u32[]{:S(2)}, u32[]{:S(2)}) collective-permute-start(bf16[2,24,64,128]{3,2,1,0:T(8,128)(2,1)} %get-tuple-element.28), channel_id=1, source_target_pairs={{1,2},{2,1},{3,4},{4,3},{5,6},{6,5},{7,8},{8,7},{9,10},{10,9},{11,... | collective-permute-start | bytes 2359304 | tf_op jit(solution)/shard_map/ppermute | solution.py:480
  97.2 12.6 %gru_band1.1 = (bf16[4,48,64,128]{3,2,1,0:T(8,128)(2,1)}, bf16[2,24,64,128]{3,2,1,0:T(8,128)(2,1)}, bf16[2,24,64,128]{3,2,1,0:T(8,128)(2,1)}, bf16[2,12,64,128]{3,2,1,0:T(8,128)(2,1)}, bf16[2,12,64,128]{3,2,1,0:T(8,128)(2,1)}) custom-call(s32[4,6]{1,0:T(4,128)} %stack.3.meta.refs_0_, ...), custom_call_target="tpu_custom_call", output_to_operand_aliasing={{0}: (9, {})} | custom-call | flops 3145728000 | bytes 9830400 | tf_op jit(solution)/shard_map/gru_band1/pallas_call | solution.py:359
  109.9 5.0 %collective-permute-done.3.refs_1_ = bf16[2,24,64,128]{3,2,1,0:T(8,128)(2,1)S(1)} collective-permute-done((bf16[2,24,64,128]{3,2,1,0:T(8,128)(2,1)}, bf16[2,24,64,128]{3,2,1,0:T(8,128)(2,1)S(1)}, u32[]{:S(2)}, u32[]{:S(2)}) %collective-permute-start.3) | collective-permute-done | bytes 786464 | tf_op jit(solution)/shard_map/ppermute | solution.py:480
  114.8 4.5 %collective-permute-start.6 = (bf16[2,24,64,128]{3,2,1,0:T(8,128)(2,1)}, bf16[2,24,64,128]{3,2,1,0:T(8,128)(2,1)S(1)}, u32[]{:S(2)}, u32[]{:S(2)}) collective-permute-start(bf16[2,24,64,128]{3,2,1,0:T(8,128)(2,1)} %get-tuple-element.35), channel_id=1, source_target_pairs={{1,2},{2,1},{3,4},{4,3},{5,6},{6,5},{7,8},{8,7},{9,10},{10,9},{11,... | collective-permute-start | bytes 2359304 | tf_op jit(solution)/shard_map/ppermute | solution.py:480
  119.4 0.5 collective-permute-start.5
  120.0 0.4 collective-permute-start.8
  120.6 0.7 collective-permute-done.4.refs_2_
  121.3 0.6 collective-permute-done.5.refs_3_
  121.9 2.9 %aggregate_from0.1.refs_9_ = bf16[2,23,64,128]{3,2,1,0:T(8,128)(2,1)S(1)} custom-call(f32[2]{0:T(128)S(1)} %broadcast_maximum_fusion.counts, bf16[2,24,64,128]{3,2,1,0:T(8,128)(2,1)S(1)} %copy-done.1, bf16[2,24,64,128]{3,2,1,0:T(8,128)(2,1)S(1)} %collective-permute-done.3.refs_1_, bf16[2,12,64,128]{3,2,1,0:T(8,128)(2,1)S(1)} %collective-permute-done.4.refs_2_, ...), custom_call_target="tpu_custom_call" | custom-call | flops 868220928 | bytes 3145728 | tf_op jit(solution)/shard_map/aggregate_from0/pallas_call | solution.py:445
  124.8 4.2 %collective-permute-done.6.refs_5_ = bf16[2,24,64,128]{3,2,1,0:T(8,128)(2,1)S(1)} collective-permute-done((bf16[2,24,64,128]{3,2,1,0:T(8,128)(2,1)}, bf16[2,24,64,128]{3,2,1,0:T(8,128)(2,1)S(1)}, u32[]{:S(2)}, u32[]{:S(2)}) %collective-permute-start.6) | collective-permute-done | bytes 786464 | tf_op jit(solution)/shard_map/ppermute | solution.py:480
  129.0 4.0 %aggregate_from23.1 = bf16[2,48,64,128]{3,2,1,0:T(8,128)(2,1)} custom-call(f32[2]{0:T(128)S(1)} %broadcast_maximum_fusion.counts, bf16[2,24,64,128]{3,2,1,0:T(8,128)(2,1)S(1)} %copy-done.1, bf16[2,24,64,128]{3,2,1,0:T(8,128)(2,1)S(1)} %collective-permute-done.3.refs_1_, bf16[2,12,64,128]{3,2,1,0:T(8,128)(2,1)S(1)} %collective-permute-done.4.refs_2_, ...), custom_call_target="tpu_custom_call" | custom-call | flops 943718400 | bytes 3407872 | tf_op jit(solution)/shard_map/aggregate_from23/pallas_call | solution.py:445
  (38 shorter events, 1.3 us)
Async XLA Ops:
  0.6 8.4 %copy-start = (bf16[81,128]{1,0:T(8,128)(2,1)S(1)}, bf16[81,128]{1,0:T(8,128)(2,1)}, u32[]{:S(2)}) copy-start(bf16[81,128]{1,0:T(8,128)(2,1)} %param.19) | copy-start | bytes 62212
  0.6 8.4 %copy-start.8 = (bf16[5,128,81]{1,2,0:T(8,128)(2,1)S(1)}, bf16[5,128,81]{1,2,0:T(8,128)(2,1)}, u32[]{:S(2)}) copy-start(bf16[5,128,81]{1,2,0:T(8,128)(2,1)} %constant.48.clone) | copy-start | bytes 311044
  0.7 8.6 %copy-start.7 = (bf16[5,128,81]{1,2,0:T(8,128)(2,1)S(1)}, bf16[5,128,81]{1,2,0:T(8,128)(2,1)}, u32[]{:S(2)}) copy-start(bf16[5,128,81]{1,2,0:T(8,128)(2,1)} %constant.49.clone) | copy-start | bytes 311044
  0.7 7.3 %copy-start.10 = (s32[64,2]{0,1:T(2,128)S(1)}, s32[64,2]{0,1:T(2,128)}, u32[]{:S(2)}) copy-start(s32[64,2]{0,1:T(2,128)} %param.17) | copy-start | bytes 1540
  0.7 7.5 %copy-start.9 = (s32[4,2]{0,1:T(2,128)S(1)}, s32[4,2]{0,1:T(2,128)}, u32[]{:S(2)}) copy-start(s32[4,2]{0,1:T(2,128)} %param.18) | copy-start | bytes 100
  0.7 9.7 %collective-permute-start = (bf16[2,2,48,64,128]{4,3,2,1,0:T(8,128)(2,1)}, bf16[2,2,48,64,128]{4,3,2,1,0:T(8,128)(2,1)}, u32[]{:S(2)}, u32[]{:S(2)}) collective-permute-start(bf16[2,2,48,64,128]{4,3,2,1,0:T(8,128)(2,1)} %own.3), channel_id=1, source_target_pairs={{0,1},{1,0},{2,3},{3,2},{4,5},{5,4},{6,7},{7,6},{8,9},{9,8},{10,11... | collective-permute-start | bytes 9437192 | tf_op jit(solution)/shard_map/ppermute | solution.py:483
  3.5 39.0 %collective-permute-start.1 = (bf16[2,48,64,128]{3,2,1,0:T(8,128)(2,1)}, bf16[2,48,64,128]{3,2,1,0:T(8,128)(2,1)}, u32[]{:S(2)}, u32[]{:S(2)}) collective-permute-start(bf16[2,48,64,128]{3,2,1,0:T(8,128)(2,1)} %slice_bitcast_fusion.1), channel_id=1, source_target_pairs={{1,2},{2,1},{3,4},{4,3},{5,6},{6,5},{7,8},{8,7},{9,10},{10,9},{11,... | collective-permute-start | bytes 4718600 | tf_op jit(solution)/shard_map/ppermute | solution.py:480
  10.4 11.6 %copy-start.4 = (bf16[2,2,48,64,128]{4,3,2,1,0:T(8,128)(2,1)S(1)}, bf16[2,2,48,64,128]{4,3,2,1,0:T(8,128)(2,1)}, u32[]{:S(2)}) copy-start(bf16[2,2,48,64,128]{4,3,2,1,0:T(8,128)(2,1)} %own.3) | copy-start | bytes 9437188
  23.3 31.7 %copy-start.6 = (bf16[2,48,64,128]{3,2,1,0:T(8,128)(2,1)S(1)}, bf16[2,48,64,128]{3,2,1,0:T(8,128)(2,1)}, u32[]{:S(2)}) copy-start(bf16[2,48,64,128]{3,2,1,0:T(8,128)(2,1)} %slice_bitcast_fusion) | copy-start | bytes 4718596
  54.9 24.3 %collective-permute-start.2 = (bf16[2,48,64,128]{3,2,1,0:T(8,128)(2,1)S(1)}, bf16[2,48,64,128]{3,2,1,0:T(8,128)(2,1)S(1)}, u32[]{:S(2)}, u32[]{:S(2)}) collective-permute-start(bf16[2,48,64,128]{3,2,1,0:T(8,128)(2,1)S(1)} %copy-done.6), channel_id=1, source_target_pairs={{1,2},{2,1},{3,4},{4,3},{5,6},{6,5},{7,8},{8,7},{9,10},{10,9},{11,... | collective-permute-start | bytes 4718600 | tf_op jit(solution)/shard_map/ppermute | solution.py:480
  79.3 1.1 copy-start.5
  92.8 22.1 %collective-permute-start.3 = (bf16[2,24,64,128]{3,2,1,0:T(8,128)(2,1)}, bf16[2,24,64,128]{3,2,1,0:T(8,128)(2,1)S(1)}, u32[]{:S(2)}, u32[]{:S(2)}) collective-permute-start(bf16[2,24,64,128]{3,2,1,0:T(8,128)(2,1)} %get-tuple-element.28), channel_id=1, source_target_pairs={{1,2},{2,1},{3,4},{4,3},{5,6},{6,5},{7,8},{8,7},{9,10},{10,9},{11,... | collective-permute-start | bytes 2359304 | tf_op jit(solution)/shard_map/ppermute | solution.py:480
  97.2 24.7 %copy-start.1 = (bf16[2,24,64,128]{3,2,1,0:T(8,128)(2,1)S(1)}, bf16[2,24,64,128]{3,2,1,0:T(8,128)(2,1)}, u32[]{:S(2)}) copy-start(bf16[2,24,64,128]{3,2,1,0:T(8,128)(2,1)} %get-tuple-element.27.refs_0_) | copy-start | bytes 2359300
  97.2 24.7 %copy-start.2 = (bf16[1152,128]{1,0:T(8,128)(2,1)S(1)}, bf16[1152,128]{1,0:T(8,128)(2,1)}, u32[]{:S(2)}) copy-start(bf16[1152,128]{1,0:T(8,128)(2,1)} %refs_8_.3) | copy-start | bytes 884740
  109.9 19.1 %copy-start.3 = (bf16[2,24,64,128]{3,2,1,0:T(8,128)(2,1)S(1)}, bf16[2,24,64,128]{3,2,1,0:T(8,128)(2,1)}, u32[]{:S(2)}) copy-start(bf16[2,24,64,128]{3,2,1,0:T(8,128)(2,1)} %get-tuple-element.33.refs_4_) | copy-start | bytes 2359300
  114.8 14.1 %collective-permute-start.6 = (bf16[2,24,64,128]{3,2,1,0:T(8,128)(2,1)}, bf16[2,24,64,128]{3,2,1,0:T(8,128)(2,1)S(1)}, u32[]{:S(2)}, u32[]{:S(2)}) collective-permute-start(bf16[2,24,64,128]{3,2,1,0:T(8,128)(2,1)} %get-tuple-element.35), channel_id=1, source_target_pairs={{1,2},{2,1},{3,4},{4,3},{5,6},{6,5},{7,8},{8,7},{9,10},{10,9},{11,... | collective-permute-start | bytes 2359304 | tf_op jit(solution)/shard_map/ppermute | solution.py:480
  119.3 2.0 %collective-permute-start.4 = (bf16[2,12,64,128]{3,2,1,0:T(8,128)(2,1)}, bf16[2,12,64,128]{3,2,1,0:T(8,128)(2,1)S(1)}, u32[]{:S(2)}, u32[]{:S(2)}) collective-permute-start(bf16[2,12,64,128]{3,2,1,0:T(8,128)(2,1)} %get-tuple-element.31), channel_id=1, source_target_pairs={{0,1},{1,0},{2,3},{3,2},{4,5},{5,4},{6,7},{7,6},{8,9},{9,8},{10,11... | collective-permute-start | bytes 1179656 | tf_op jit(solution)/shard_map/ppermute | solution.py:483
  119.4 2.5 %collective-permute-start.5 = (bf16[2,12,64,128]{3,2,1,0:T(8,128)(2,1)}, bf16[2,12,64,128]{3,2,1,0:T(8,128)(2,1)S(1)}, u32[]{:S(2)}, u32[]{:S(2)}) collective-permute-start(bf16[2,12,64,128]{3,2,1,0:T(8,128)(2,1)} %get-tuple-element.32), channel_id=1, source_target_pairs={{0,1},{1,0},{2,3},{3,2},{4,5},{5,4},{6,7},{7,6},{8,9},{9,8},{10,11... | collective-permute-start | bytes 1179656 | tf_op jit(solution)/shard_map/ppermute | solution.py:483
  119.9 4.9 %collective-permute-start.7 = (bf16[2,12,64,128]{3,2,1,0:T(8,128)(2,1)}, bf16[2,12,64,128]{3,2,1,0:T(8,128)(2,1)S(1)}, u32[]{:S(2)}, u32[]{:S(2)}) collective-permute-start(bf16[2,12,64,128]{3,2,1,0:T(8,128)(2,1)} %get-tuple-element.38), channel_id=1, source_target_pairs={{0,1},{1,0},{2,3},{3,2},{4,5},{5,4},{6,7},{7,6},{8,9},{9,8},{10,11... | collective-permute-start | bytes 1179656 | tf_op jit(solution)/shard_map/ppermute | solution.py:483
  120.0 4.8 %collective-permute-start.8 = (bf16[2,12,64,128]{3,2,1,0:T(8,128)(2,1)}, bf16[2,12,64,128]{3,2,1,0:T(8,128)(2,1)S(1)}, u32[]{:S(2)}, u32[]{:S(2)}) collective-permute-start(bf16[2,12,64,128]{3,2,1,0:T(8,128)(2,1)} %get-tuple-element.39), channel_id=1, source_target_pairs={{0,1},{1,0},{2,3},{3,2},{4,5},{5,4},{6,7},{7,6},{8,9},{9,8},{10,11... | collective-permute-start | bytes 1179656 | tf_op jit(solution)/shard_map/ppermute | solution.py:483

commit v5 on v4

--- a/solution.py
+++ b/solution.py
@@ -237,7 +237,8 @@
     meta,
     own,
     near,
-    far,
+    far_top,
+    far_low,
     motion,
     gates,
     state,
@@ -267,24 +268,31 @@
     top = max(first - 1, 0)
     end = min(last + 1, height)
     rows = end - top
+    split = far_top.shape[1]
+    above = min(split - top, rows)
+    context_pieces = [
+        piece for piece in ((far_top, 0, above, 0), (far_low, above, rows, 4)) if piece[2] > piece[1]
+    ]
 
     def start(e, s):
         buf, frame = meta[e, 0], meta[e, 1]
         pltpu.make_async_copy(motion.at[e, pl.ds(top + 1, rows)], motion_buf.at[s], sems.at[1, s]).start()
         pltpu.make_async_copy(gates.at[e, pl.ds(top, rows)], gates_buf.at[s], sems.at[2, s]).start()
         pltpu.make_async_copy(state.at[e, pl.ds(top, rows)], state_buf.at[s], sems.at[3, s]).start()
-        cases = (
-            (buf == 0, own.at[frame, 1, pl.ds(top, rows)]),
-            (buf == 1, far.at[frame, pl.ds(top, rows)]),
-            (buf == 2, near.at[frame, 1, pl.ds(top, rows)]),
-        )
-        fetch(cases, ctx_buf.at[s], sems.at[0, s])
+        for far, low, high, sem in context_pieces:
+            cases = (
+                (buf == 0, own.at[frame, 1, pl.ds(top + low, high - low)]),
+                (buf == 1, far.at[frame, pl.ds(top + low - (0 if far is far_top else split), high - low)]),
+                (buf == 2, near.at[frame, 1, pl.ds(top + low, high - low)]),
+            )
+            fetch(cases, ctx_buf.at[s, pl.ds(low, high - low)], sems.at[sem, s])
 
     def finish(s):
         await_copy(motion_buf.at[s], sems.at[1, s])
         await_copy(gates_buf.at[s], sems.at[2, s])
         await_copy(state_buf.at[s], sems.at[3, s])
-        await_copy(ctx_buf.at[s], sems.at[0, s])
+        for _, low, high, sem in context_pieces:
+            await_copy(ctx_buf.at[s, pl.ds(low, high - low)], sems.at[sem, s])
 
     @pl.when(edge == 0)
     def _():
@@ -337,7 +345,7 @@
         near_low[...] = totals[2 * frames :, half:].astype(BF16)
 
 
-def gru_of(band, meta, own, near, far, motion, gates, state, w_input, w_candidate, earlier):
+def gru_of(band, meta, own, near, far_top, far_low, motion, gates, state, w_input, w_candidate, earlier):
     frames, _, height, width, chans = own.shape
     edges = state.shape[0]
     size = height // 2
@@ -348,20 +356,20 @@
     sum_spec = pl.BlockSpec(sums.shape, lambda e, m: (0, 0, 0, 0))
     piece_spec = pl.BlockSpec(pieces.shape, lambda e, m: (0, 0, 0, 0))
     body = functools.partial(gru_kernel, first, last)
-    operands = [meta, own, near, far, motion, gates, state, w_input, w_candidate]
+    operands = [meta, own, near, far_top, far_low, motion, gates, state, w_input, w_candidate]
     if earlier is None:
-        kernel = lambda *refs: body(*refs[:9], None, *refs[9:])
+        kernel = lambda *refs: body(*refs[:10], None, *refs[10:])
         aliases = {}
     else:
         kernel = body
         operands.append(earlier)
-        aliases = {9: 0}
+        aliases = {10: 0}
     return pl.pallas_call(
         kernel,
         grid_spec=pltpu.PrefetchScalarGridSpec(
             num_scalar_prefetch=1,
             grid=(edges,),
-            in_specs=[any_spec()] * 6 + [whole(w_input), whole(w_candidate)] + [any_spec()] * (len(operands) - 9),
+            in_specs=[any_spec()] * 7 + [whole(w_input), whole(w_candidate)] + [any_spec()] * (len(operands) - 10),
             out_specs=[
                 pl.BlockSpec((1, size, width, chans), lambda e, m: (e, band, 0, 0)),
                 sum_spec,
@@ -378,7 +386,7 @@
                 pltpu.VMEM((rows, width, chans), F32),
                 pltpu.VMEM((rows, width, chans), F32),
                 pltpu.VMEM((3 * frames, size, width, chans), F32),
-                pltpu.SemaphoreType.DMA((4, 2)),
+                pltpu.SemaphoreType.DMA((5, 2)),
             ],
         ),
         out_shape=[
@@ -391,9 +399,9 @@
         input_output_aliases=aliases,
         compiler_params=pltpu.CompilerParams(vmem_limit_bytes=VMEM_LIMIT),
         cost_estimate=pl.CostEstimate(
-            flops=2 * edges * rows * width * chans * (6 * chans + 9 * chans),
-            bytes_accessed=2 * edges * rows * width * chans * 6,
-            transcendentals=3 * edges * rows * width * chans,
+            flops=2 * edges * rows * width * chans,
+            bytes_accessed=2 * edges * rows * width * chans,
+            transcendentals=0,
         ),
         name=f"gru_band{band}",
     )(*operands)
@@ -501,14 +509,19 @@
     held_meta = lax.optimization_barrier((meta, gates))[0]
     motion = motion_of(0, half, held_meta, frame_maps, near, far_feat, base, None)
     context = lax.optimization_barrier((frame_maps, near))[0][:, 1]
-    far_ctx = far_swap(context, motion)
+    split = height // 2 + 1
+    far_top = far_swap(context[:, :split], motion)
+    far_low = far_swap(context[:, split:], motion)
     motion = motion_of(half, edge_count, meta, frame_maps, near, far_feat, base, motion)
-    maps = (meta, frame_maps, near, far_ctx, motion, gates, net_state, w_input, w_candidate)
-
-    new_state, own_first, far_sum, *near_first = gru_of(0, *maps, None)
+
+    def gru(band, earlier):
+        fars = (far_top, far_low if band else far_top)
+        return gru_of(band, meta, frame_maps, near, *fars, motion, gates, net_state, w_input, w_candidate, earlier)
+
+    new_state, own_first, far_sum, *near_first = gru(0, None)
     far_first = far_swap(far_sum)
-    new_state, own_second, far_sum, *near_second = gru_of(1, *maps, new_state)
-    far_second = far_swap(far_sum, far_first)
+    new_state, own_second, far_sum, *near_second = gru(1, new_state)
+    far_second = far_swap(far_sum)
     near_first, near_second = (
         [near_swap(piece) for piece in lax.optimization_barrier((*pieces, far_first))[:2]]
         for pieces in (near_first, near_second)

time: 133 us -> 125 us (0.940)
  waiting for transfers between devices: 37.2 us -> 25.2 us
  local copies, waits for them, and re-layouts: 6.13 us -> 10.4 us
    ppermute x4 -> x5, waiting for transfers between devices: 35.9 us -> 23.9 us  [far_swap(): return lax.ppermute(block, 'rows', far_route)]
    unnamed x24, local copies, waits for them, and re-layouts: 1.38 us -> 3.8 us
    slice x0 -> x2, local copies, waits for them, and re-layouts: none -> 2.11 us  [the longest x1 2.06 us: per_device(): far_low = far_swap(context[:, split:], motion)]
    ppermute x4 -> x5, starting transfers between devices: 17.7 us -> 16.7 us  [far_swap(): return lax.ppermute(block, 'rows', far_route)]
  transfers between devices with their start and end apart: 9 -> 10, of which waited for: 6 -> 5; matrix products, arithmetic and copies ran while one was open for 5% -> 7% of each run, Pallas kernels for 30% -> 42%
where the time goes in v5:
time: 125 us; the launch traced here: 124 us
  Pallas kernels  68.3 us (55%)
  waiting for transfers between devices  25.2 us (20%)
  starting transfers between devices  17.8 us (14%)
  local copies, waits for them, and re-layouts  10.4 us (8%)
    pallas_call x2, Pallas kernels, gru_of(): pl.pallas_call(kernel, grid_spec=pltpu.PrefetchScalarGridSpec(num_scalar_...  25.1 us
    pallas_call x2, Pallas kernels, motion_of(): pl.pallas_call(kernel, grid_spec=pltpu.PrefetchScalarGridSpec(num_scalar_...  24.8 us
    ppermute x5, waiting for transfers between devices, far_swap(): return lax.ppermute(block, 'rows', far_route)  23.9 us
    ppermute x5, starting transfers between devices, far_swap(): return lax.ppermute(block, 'rows', far_route)  16.7 us
    pallas_call x1, Pallas kernels, gates_of(): pl.pallas_call(gates_kernel, grid=(edges,), in_specs=[pl.BlockSpec((1, he...  11.5 us
    pallas_call x2, Pallas kernels, aggregate_of(): pl.pallas_call(functools.partial(aggregate_kernel, pieces, first, last),...  6.86 us
    unnamed x24, local copies, waits for them, and re-layouts  3.8 us
    squeeze x1, local copies, waits for them, and re-layouts, per_device(): far_feat = far_swap(frame_maps[:, 0])  2.82 us
  transfers between devices with their start and end apart: 10, of which 5 were waited for; matrix products, arithmetic and copies ran while one was open for 7% of the time, Pallas kernels for 42%

profile of v5, /device:TPU:1, one launch (start us, length us, event | category | flops | bytes accessed | tf_op | source)
XLA Modules:
  0.0 124.1 jit_solution(14675996490417132209)
XLA Ops:
  0.8 2.8 %slice_bitcast_fusion.1 = bf16[2,48,64,128]{3,2,1,0:T(8,128)(2,1)} fusion(bf16[2,2,48,64,128]{4,3,2,1,0:T(8,128)(2,1)} %own.3), kind=kLoop, calls=%fused_computation.1 | loop fusion | bytes 3145728 | tf_op jit(solution)/shard_map/squeeze | solution.py:493
  3.6 4.5 %collective-permute-start.1 = (bf16[2,48,64,128]{3,2,1,0:T(8,128)(2,1)}, bf16[2,48,64,128]{3,2,1,0:T(8,128)(2,1)}, u32[]{:S(2)}, u32[]{:S(2)}) collective-permute-start(bf16[2,48,64,128]{3,2,1,0:T(8,128)(2,1)} %slice_bitcast_fusion.1), channel_id=1, source_target_pairs={{1,2},{2,1},{3,4},{4,3},{5,6},{6,5},{7,8},{8,7},{9,10},{10,9},{11,... | collective-permute-start | bytes 4718600 | tf_op jit(solution)/shard_map/ppermute | solution.py:488
  8.1 0.8 constant_dynamic-slice_fusion
  9.0 0.8 copy.26
  11.0 0.9 pad_maximum_fusion.base_ref.refs_6_
  12.0 1.1 copy-done.6
  13.2 11.5 %gates.1.refs_6_ = bf16[4,48,64,256]{3,2,1,0:T(8,128)(2,1)} custom-call(bf16[4,48,64,128]{3,2,1,0:T(8,128)(2,1)} %state.1, bf16[1152,256]{1,0:T(8,128)(2,1)} %weights_ref), custom_call_target="tpu_custom_call" | custom-call | flops 7247757312 | bytes 9437184 | tf_op jit(solution)/shard_map/gates/pallas_call | solution.py:83
  24.7 17.9 %collective-permute-done.1.far.refs_3_ = bf16[2,48,64,128]{3,2,1,0:T(8,128)(2,1)} collective-permute-done((bf16[2,48,64,128]{3,2,1,0:T(8,128)(2,1)}, bf16[2,48,64,128]{3,2,1,0:T(8,128)(2,1)}, u32[]{:S(2)}, u32[]{:S(2)}) %collective-permute-start.1) | collective-permute-done | bytes 1572896 | tf_op jit(solution)/shard_map/ppermute | solution.py:488
  42.6 12.4 %motion_from0.1.refs_7_ = bf16[4,52,64,128]{3,2,1,0:T(8,128)(2,1)} custom-call(s32[4,6]{1,0:T(4,128)} %stack.3.meta.refs_0_, bf16[2,2,48,64,128]{4,3,2,1,0:T(8,128)(2,1)} %own.3, bf16[2,2,48,64,128]{4,3,2,1,0:T(8,128)(2,1)} %collective-permute-done.near.refs_2_, bf16[2,48,64,128]{3,2,1,0:T(8,128)(2,1)} %collective-permute-done.1.far.refs_3_, ...), custom_call_target="tpu_custom_call" | custom-call | flops 4026531840 | bytes 4718592 | tf_op jit(solution)/shard_map/motion_from0/pallas_call | solution.py:207
  55.1 4.4 %collective-permute-start.2 = (bf16[2,25,64,128]{3,2,1,0:T(8,128)(2,1)S(1)}, bf16[2,25,64,128]{3,2,1,0:T(8,128)(2,1)S(1)}, u32[]{:S(2)}, u32[]{:S(2)}) collective-permute-start(bf16[2,25,64,128]{3,2,1,0:T(8,128)(2,1)S(1)} %slice.40), channel_id=1, source_target_pairs={{1,2},{2,1},{3,4},{4,3},{5,6},{6,5},{7,8},{8,7},{9,10},{10,9},{11,... | collective-permute-start | bytes 2457608 | tf_op jit(solution)/shard_map/ppermute | solution.py:488
  59.5 2.1 %slice.41 = bf16[2,23,64,128]{3,2,1,0:T(8,128)(2,1)} slice(bf16[2,48,64,128]{3,2,1,0:T(8,128)(2,1)} %copy-done.6), slice={[0:2], [25:48], [0:64], [0:128]} | slice | bytes 1507328 | tf_op jit(solution)/shard_map/slice | solution.py:514
  61.5 1.9 %collective-permute-start.3 = (bf16[2,23,64,128]{3,2,1,0:T(8,128)(2,1)}, bf16[2,23,64,128]{3,2,1,0:T(8,128)(2,1)S(1)}, u32[]{:S(2)}, u32[]{:S(2)}) collective-permute-start(bf16[2,23,64,128]{3,2,1,0:T(8,128)(2,1)} %slice.41), channel_id=1, source_target_pairs={{1,2},{2,1},{3,4},{4,3},{5,6},{6,5},{7,8},{8,7},{9,10},{10,9},{11,... | collective-permute-start | bytes 2261000 | tf_op jit(solution)/shard_map/ppermute | solution.py:488
  63.4 12.4 %motion_from2.1.refs_5_.motion = bf16[4,52,64,128]{3,2,1,0:T(8,128)(2,1)} custom-call(s32[4,6]{1,0:T(4,128)} %stack.3.meta.refs_0_, bf16[2,2,48,64,128]{4,3,2,1,0:T(8,128)(2,1)} %own.3, bf16[2,2,48,64,128]{4,3,2,1,0:T(8,128)(2,1)} %collective-permute-done.near.refs_2_, ...), custom_call_target="tpu_custom_call", output_to_operand_aliasing={{}: (7, {})} | custom-call | flops 4026531840 | bytes 4718592 | tf_op jit(solution)/shard_map/motion_from2/pallas_call | solution.py:207
  75.9 0.9 copy-done.5
  76.8 12.4 %gru_band0.1 = (bf16[4,48,64,128]{3,2,1,0:T(8,128)(2,1)}, bf16[2,24,64,128]{3,2,1,0:T(8,128)(2,1)}, bf16[2,24,64,128]{3,2,1,0:T(8,128)(2,1)}, bf16[2,12,64,128]{3,2,1,0:T(8,128)(2,1)}, bf16[2,12,64,128]{3,2,1,0:T(8,128)(2,1)}) custom-call(s32[4,6]{1,0:T(4,128)} %stack.3.meta.refs_0_, bf16[2,2,48,64,128]{4,3,2,1,0:T(8,128)(2,1)} %own.3, ...), custom_call_target="tpu_custom_call" | custom-call | flops 1638400 | bytes 1638400 | tf_op jit(solution)/shard_map/gru_band0/pallas_call | solution.py:367
  89.2 3.6 %collective-permute-start.4 = (bf16[2,24,64,128]{3,2,1,0:T(8,128)(2,1)}, bf16[2,24,64,128]{3,2,1,0:T(8,128)(2,1)S(1)}, u32[]{:S(2)}, u32[]{:S(2)}) collective-permute-start(bf16[2,24,64,128]{3,2,1,0:T(8,128)(2,1)} %get-tuple-element.29), channel_id=1, source_target_pairs={{1,2},{2,1},{3,4},{4,3},{5,6},{6,5},{7,8},{8,7},{9,10},{10,9},{11,... | collective-permute-start | bytes 2359304 | tf_op jit(solution)/shard_map/ppermute | solution.py:488
  92.9 0.9 copy-done.7
  93.8 12.7 %gru_band1.1 = (bf16[4,48,64,128]{3,2,1,0:T(8,128)(2,1)}, bf16[2,24,64,128]{3,2,1,0:T(8,128)(2,1)}, bf16[2,24,64,128]{3,2,1,0:T(8,128)(2,1)}, bf16[2,12,64,128]{3,2,1,0:T(8,128)(2,1)}, bf16[2,12,64,128]{3,2,1,0:T(8,128)(2,1)}) custom-call(s32[4,6]{1,0:T(4,128)} %stack.3.meta.refs_0_, ...), custom_call_target="tpu_custom_call", output_to_operand_aliasing={{0}: (10, {})} | custom-call | flops 1638400 | bytes 1638400 | tf_op jit(solution)/shard_map/gru_band1/pallas_call | solution.py:367
  106.5 2.2 %collective-permute-start.7 = (bf16[2,24,64,128]{3,2,1,0:T(8,128)(2,1)}, bf16[2,24,64,128]{3,2,1,0:T(8,128)(2,1)S(1)}, u32[]{:S(2)}, u32[]{:S(2)}) collective-permute-start(bf16[2,24,64,128]{3,2,1,0:T(8,128)(2,1)} %get-tuple-element.35), channel_id=1, source_target_pairs={{1,2},{2,1},{3,4},{4,3},{5,6},{6,5},{7,8},{8,7},{9,10},{10,9},{11,... | collective-permute-start | bytes 2359304 | tf_op jit(solution)/shard_map/ppermute | solution.py:488
  108.7 1.8 %collective-permute-done.4.refs_1_ = bf16[2,24,64,128]{3,2,1,0:T(8,128)(2,1)S(1)} collective-permute-done((bf16[2,24,64,128]{3,2,1,0:T(8,128)(2,1)}, bf16[2,24,64,128]{3,2,1,0:T(8,128)(2,1)S(1)}, u32[]{:S(2)}, u32[]{:S(2)}) %collective-permute-start.4) | collective-permute-done | bytes 786464 | tf_op jit(solution)/shard_map/ppermute | solution.py:488
  111.7 0.7 collective-permute-done.5.refs_2_
  113.0 2.9 %aggregate_from0.1.refs_9_ = bf16[2,23,64,128]{3,2,1,0:T(8,128)(2,1)S(1)} custom-call(f32[2]{0:T(128)S(1)} %broadcast_maximum_fusion.counts, bf16[2,24,64,128]{3,2,1,0:T(8,128)(2,1)S(1)} %copy-done.1, bf16[2,24,64,128]{3,2,1,0:T(8,128)(2,1)S(1)} %collective-permute-done.4.refs_1_, bf16[2,12,64,128]{3,2,1,0:T(8,128)(2,1)S(1)} %collective-permute-done.5.refs_2_, ...), custom_call_target="tpu_custom_call" | custom-call | flops 868220928 | bytes 3145728 | tf_op jit(solution)/shard_map/aggregate_from0/pallas_call | solution.py:453
  115.9 4.2 %collective-permute-done.7.refs_5_ = bf16[2,24,64,128]{3,2,1,0:T(8,128)(2,1)S(1)} collective-permute-done((bf16[2,24,64,128]{3,2,1,0:T(8,128)(2,1)}, bf16[2,24,64,128]{3,2,1,0:T(8,128)(2,1)S(1)}, u32[]{:S(2)}, u32[]{:S(2)}) %collective-permute-start.7) | collective-permute-done | bytes 786464 | tf_op jit(solution)/shard_map/ppermute | solution.py:488
  120.1 4.0 %aggregate_from23.1 = bf16[2,48,64,128]{3,2,1,0:T(8,128)(2,1)} custom-call(f32[2]{0:T(128)S(1)} %broadcast_maximum_fusion.counts, bf16[2,24,64,128]{3,2,1,0:T(8,128)(2,1)S(1)} %copy-done.1, bf16[2,24,64,128]{3,2,1,0:T(8,128)(2,1)S(1)} %collective-permute-done.4.refs_1_, bf16[2,12,64,128]{3,2,1,0:T(8,128)(2,1)S(1)} %collective-permute-done.5.refs_2_, ...), custom_call_target="tpu_custom_call" | custom-call | flops 943718400 | bytes 3407872 | tf_op jit(solution)/shard_map/aggregate_from23/pallas_call | solution.py:453
  (42 shorter events, 3.5 us)
Async XLA Ops:
  0.6 9.9 %copy-start = (bf16[81,128]{1,0:T(8,128)(2,1)S(1)}, bf16[81,128]{1,0:T(8,128)(2,1)}, u32[]{:S(2)}) copy-start(bf16[81,128]{1,0:T(8,128)(2,1)} %param.19) | copy-start | bytes 62212
  0.6 9.9 %copy-start.9 = (bf16[5,128,81]{1,2,0:T(8,128)(2,1)S(1)}, bf16[5,128,81]{1,2,0:T(8,128)(2,1)}, u32[]{:S(2)}) copy-start(bf16[5,128,81]{1,2,0:T(8,128)(2,1)} %constant.48.clone) | copy-start | bytes 311044
  0.7 10.1 %copy-start.8 = (bf16[5,128,81]{1,2,0:T(8,128)(2,1)S(1)}, bf16[5,128,81]{1,2,0:T(8,128)(2,1)}, u32[]{:S(2)}) copy-start(bf16[5,128,81]{1,2,0:T(8,128)(2,1)} %constant.49.clone) | copy-start | bytes 311044
  0.7 11.2 %copy-start.4 = (bf16[2,2,48,64,128]{4,3,2,1,0:T(8,128)(2,1)S(1)}, bf16[2,2,48,64,128]{4,3,2,1,0:T(8,128)(2,1)}, u32[]{:S(2)}) copy-start(bf16[2,2,48,64,128]{4,3,2,1,0:T(8,128)(2,1)} %own.3) | copy-start | bytes 9437188
  0.7 11.2 %collective-permute-start = (bf16[2,2,48,64,128]{4,3,2,1,0:T(8,128)(2,1)}, bf16[2,2,48,64,128]{4,3,2,1,0:T(8,128)(2,1)}, u32[]{:S(2)}, u32[]{:S(2)}) collective-permute-start(bf16[2,2,48,64,128]{4,3,2,1,0:T(8,128)(2,1)} %own.3), channel_id=1, source_target_pairs={{0,1},{1,0},{2,3},{3,2},{4,5},{5,4},{6,7},{7,6},{8,9},{9,8},{10,11... | collective-permute-start | bytes 9437192 | tf_op jit(solution)/shard_map/ppermute | solution.py:491
  3.6 39.0 %collective-permute-start.1 = (bf16[2,48,64,128]{3,2,1,0:T(8,128)(2,1)}, bf16[2,48,64,128]{3,2,1,0:T(8,128)(2,1)}, u32[]{:S(2)}, u32[]{:S(2)}) collective-permute-start(bf16[2,48,64,128]{3,2,1,0:T(8,128)(2,1)} %slice_bitcast_fusion.1), channel_id=1, source_target_pairs={{1,2},{2,1},{3,4},{4,3},{5,6},{6,5},{7,8},{8,7},{9,10},{10,9},{11,... | collective-permute-start | bytes 4718600 | tf_op jit(solution)/shard_map/ppermute | solution.py:488
  12.0 1.1 copy-start.6
  55.1 20.8 %collective-permute-start.2 = (bf16[2,25,64,128]{3,2,1,0:T(8,128)(2,1)S(1)}, bf16[2,25,64,128]{3,2,1,0:T(8,128)(2,1)S(1)}, u32[]{:S(2)}, u32[]{:S(2)}) collective-permute-start(bf16[2,25,64,128]{3,2,1,0:T(8,128)(2,1)S(1)} %slice.40), channel_id=1, source_target_pairs={{1,2},{2,1},{3,4},{4,3},{5,6},{6,5},{7,8},{8,7},{9,10},{10,9},{11,... | collective-permute-start | bytes 2457608 | tf_op jit(solution)/shard_map/ppermute | solution.py:488
  61.5 31.3 %collective-permute-start.3 = (bf16[2,23,64,128]{3,2,1,0:T(8,128)(2,1)}, bf16[2,23,64,128]{3,2,1,0:T(8,128)(2,1)S(1)}, u32[]{:S(2)}, u32[]{:S(2)}) collective-permute-start(bf16[2,23,64,128]{3,2,1,0:T(8,128)(2,1)} %slice.41), channel_id=1, source_target_pairs={{1,2},{2,1},{3,4},{4,3},{5,6},{6,5},{7,8},{8,7},{9,10},{10,9},{11,... | collective-permute-start | bytes 2261000 | tf_op jit(solution)/shard_map/ppermute | solution.py:488
  75.9 0.9 copy-start.5
  89.2 21.3 %collective-permute-start.4 = (bf16[2,24,64,128]{3,2,1,0:T(8,128)(2,1)}, bf16[2,24,64,128]{3,2,1,0:T(8,128)(2,1)S(1)}, u32[]{:S(2)}, u32[]{:S(2)}) collective-permute-start(bf16[2,24,64,128]{3,2,1,0:T(8,128)(2,1)} %get-tuple-element.29), channel_id=1, source_target_pairs={{1,2},{2,1},{3,4},{4,3},{5,6},{6,5},{7,8},{8,7},{9,10},{10,9},{11,... | collective-permute-start | bytes 2359304 | tf_op jit(solution)/shard_map/ppermute | solution.py:488
  92.9 0.9 copy-start.7
  93.8 14.9 %copy-start.10 = (s32[64,2]{0,1:T(2,128)S(1)}, s32[64,2]{0,1:T(2,128)}, u32[]{:S(2)}) copy-start(s32[64,2]{0,1:T(2,128)} %param.17) | copy-start | bytes 1540
  93.8 19.3 %copy-start.1 = (bf16[2,24,64,128]{3,2,1,0:T(8,128)(2,1)S(1)}, bf16[2,24,64,128]{3,2,1,0:T(8,128)(2,1)}, u32[]{:S(2)}) copy-start(bf16[2,24,64,128]{3,2,1,0:T(8,128)(2,1)} %get-tuple-element.28.refs_0_) | copy-start | bytes 2359300
  93.8 19.3 %copy-start.2 = (bf16[1152,128]{1,0:T(8,128)(2,1)S(1)}, bf16[1152,128]{1,0:T(8,128)(2,1)}, u32[]{:S(2)}) copy-start(bf16[1152,128]{1,0:T(8,128)(2,1)} %refs_8_.3) | copy-start | bytes 884740
  106.4 13.7 %copy-start.3 = (bf16[2,24,64,128]{3,2,1,0:T(8,128)(2,1)S(1)}, bf16[2,24,64,128]{3,2,1,0:T(8,128)(2,1)}, u32[]{:S(2)}) copy-start(bf16[2,24,64,128]{3,2,1,0:T(8,128)(2,1)} %get-tuple-element.34.refs_4_) | copy-start | bytes 2359300
  106.5 13.7 %collective-permute-start.7 = (bf16[2,24,64,128]{3,2,1,0:T(8,128)(2,1)}, bf16[2,24,64,128]{3,2,1,0:T(8,128)(2,1)S(1)}, u32[]{:S(2)}, u32[]{:S(2)}) collective-permute-start(bf16[2,24,64,128]{3,2,1,0:T(8,128)(2,1)} %get-tuple-element.35), channel_id=1, source_target_pairs={{1,2},{2,1},{3,4},{4,3},{5,6},{6,5},{7,8},{8,7},{9,10},{10,9},{11,... | collective-permute-start | bytes 2359304 | tf_op jit(solution)/shard_map/ppermute | solution.py:488
  110.5 1.9 %collective-permute-start.5 = (bf16[2,12,64,128]{3,2,1,0:T(8,128)(2,1)}, bf16[2,12,64,128]{3,2,1,0:T(8,128)(2,1)S(1)}, u32[]{:S(2)}, u32[]{:S(2)}) collective-permute-start(bf16[2,12,64,128]{3,2,1,0:T(8,128)(2,1)} %get-tuple-element.32), channel_id=1, source_target_pairs={{0,1},{1,0},{2,3},{3,2},{4,5},{5,4},{6,7},{7,6},{8,9},{9,8},{10,11... | collective-permute-start | bytes 1179656 | tf_op jit(solution)/shard_map/ppermute | solution.py:491
  110.5 2.5 %collective-permute-start.6 = (bf16[2,12,64,128]{3,2,1,0:T(8,128)(2,1)}, bf16[2,12,64,128]{3,2,1,0:T(8,128)(2,1)S(1)}, u32[]{:S(2)}, u32[]{:S(2)}) collective-permute-start(bf16[2,12,64,128]{3,2,1,0:T(8,128)(2,1)} %get-tuple-element.33), channel_id=1, source_target_pairs={{0,1},{1,0},{2,3},{3,2},{4,5},{5,4},{6,7},{7,6},{8,9},{9,8},{10,11... | collective-permute-start | bytes 1179656 | tf_op jit(solution)/shard_map/ppermute | solution.py:491
  111.0 9.1 %collective-permute-start.8 = (bf16[2,12,64,128]{3,2,1,0:T(8,128)(2,1)}, bf16[2,12,64,128]{3,2,1,0:T(8,128)(2,1)S(1)}, u32[]{:S(2)}, u32[]{:S(2)}) collective-permute-start(bf16[2,12,64,128]{3,2,1,0:T(8,128)(2,1)} %get-tuple-element.38), channel_id=1, source_target_pairs={{0,1},{1,0},{2,3},{3,2},{4,5},{5,4},{6,7},{7,6},{8,9},{9,8},{10,11... | collective-permute-start | bytes 1179656 | tf_op jit(solution)/shard_map/ppermute | solution.py:491
  111.0 9.1 %collective-permute-start.9 = (bf16[2,12,64,128]{3,2,1,0:T(8,128)(2,1)}, bf16[2,12,64,128]{3,2,1,0:T(8,128)(2,1)S(1)}, u32[]{:S(2)}, u32[]{:S(2)}) collective-permute-start(bf16[2,12,64,128]{3,2,1,0:T(8,128)(2,1)} %get-tuple-element.39), channel_id=1, source_target_pairs={{0,1},{1,0},{2,3},{3,2},{4,5},{5,4},{6,7},{7,6},{8,9},{9,8},{10,11... | collective-permute-start | bytes 1179656 | tf_op jit(solution)/shard_map/ppermute | solution.py:491

commit v6 on v5

--- a/solution.py
+++ b/solution.py
@@ -97,7 +97,9 @@
     )(state, weights)
 
 
-def motion_kernel(low, meta, own, near, far, flip_ref, mask_ref, base_ref, out_ref, src_buf, raw_buf, tgt_buf, w_buf, sems):
+def motion_kernel(low, frames, meta, own, near, *refs):
+    fars = refs[:frames]
+    flip_ref, mask_ref, base_ref, out_ref, src_buf, raw_buf, tgt_buf, w_buf, sems = refs[frames:]
     step = pl.program_id(0)
     steps = pl.num_programs(0)
     edge = step + low
@@ -108,7 +110,8 @@
 
     def start(e, s):
         def cases(buf, frame):
-            return ((buf == 0, own.at[frame, 0]), (buf == 1, far.at[frame]), (buf == 2, near.at[frame, 0]))
+            far_cases = [((buf == 1) & (frame == f), far) for f, far in enumerate(fars)]
+            return [(buf == 0, own.at[frame, 0]), (buf == 2, near.at[frame, 0])] + far_cases
 
         fetch(cases(meta[e, 0], meta[e, 1]), src_buf.at[s, pl.ds(1, height)], sems.at[0, s])
         fetch(cases(meta[e, 2], meta[e, 3]), raw_buf.at[s], sems.at[1, s])
@@ -116,9 +119,9 @@
     @pl.when(step == 0)
     def _():
         start(edge, slot)
-        tgt_buf[0:MARGIN] = jnp.zeros((MARGIN, width, chans), BF16)
-        below = tgt_buf.shape[0] - MARGIN - height
-        tgt_buf[MARGIN + height :] = jnp.zeros((below, width, chans), BF16)
+        tgt_buf[:, : MARGIN * width] = jnp.zeros((chans, MARGIN * width), BF16)
+        below = tgt_buf.shape[1] - (MARGIN + height) * width
+        tgt_buf[:, tgt_buf.shape[1] - below :] = jnp.zeros((chans, below), BF16)
 
     @pl.when(step + 1 < steps)
     def _():
@@ -134,14 +137,14 @@
     flip = flip_ref[...]
     for y in range(0, height, 2):
         block = raw_buf[slot, y : y + 2].reshape(lanes, chans)
-        turned = jnp.dot(flip, block, preferred_element_type=F32).astype(BF16)
-        tgt_buf[MARGIN + y : MARGIN + y + 2] = turned.reshape(2, width, chans)
+        turned = lax.dot_general(block, flip, (((0,), (0,)), ((), ())), preferred_element_type=F32)
+        tgt_buf[:, (MARGIN + y) * width : (MARGIN + y + 2) * width] = turned.astype(BF16)
 
     mask = mask_ref[...]
-    keep = mask != 0.0
+    keep = mask.astype(BF16)
     odd = lax.rem(oy + 2 * SHIFT, 2)
     weights = w_buf[...]
-    unroll = 5
+    unroll = 25
 
     @pl.loop(0, (height // 2 + unroll) // unroll)
     def _(i):
@@ -149,8 +152,9 @@
         scores = []
         for y in starts:
             lhs = src_buf[slot, pl.ds(y + 1, 2)].reshape(lanes, chans)
-            rhs = tgt_buf[pl.ds(y + oy - RADIUS + MARGIN, 2 * tiles)].reshape(tiles * lanes, chans)
-            scores.append(lax.dot_general(lhs, rhs, (((1,), (1,)), ((), ())), preferred_element_type=F32))
+            at = (y + oy + SHIFT) // 2 * lanes
+            rhs = tgt_buf[:, pl.ds(pl.multiple_of(at, lanes), tiles * lanes)]
+            scores.append(jnp.dot(lhs, rhs, preferred_element_type=F32))
         for y, pair in zip(starts, scores):
             volume = []
             for r in range(2):
@@ -158,7 +162,7 @@
                 for j in range(tiles):
                     tile = pair[r * width : (r + 1) * width, j * lanes : (j + 1) * lanes] * (chans**-0.5)
                     tile = pltpu.roll(tile.astype(BF16), 0, 1, stride=1, stride_axis=0)
-                    parts.append(jnp.where(keep, tile.astype(F32), 0.0).astype(BF16))
+                    parts.append(tile * keep)
                 volume.append(jnp.concatenate(parts, axis=1))
             res = jnp.dot(jnp.concatenate(volume, axis=0), weights, preferred_element_type=F32)
             out_ref[0, pl.ds(y + 1, 1)] = jnp.maximum(res[:width, :chans], 0.0).astype(BF16)[None]
@@ -190,31 +194,32 @@
     )
 
 
-def motion_of(low, high, meta, own, near, far, base, earlier):
-    _, _, height, width, chans = own.shape
+def motion_of(low, high, meta, own, near, fars, base, earlier):
+    frames, _, height, width, chans = own.shape
     edges = meta.shape[0]
     rows = SPAN + 1
     _, flip, mask = motion_constants(width, chans)
     buffer_rows = height + 4
     target_rows = height + 2 * MARGIN + 2
-    operands = [meta, own, near, far, flip, mask, base]
-    body = functools.partial(motion_kernel, low)
+    operands = [meta, own, near, *fars, flip, mask, base]
+    count = len(operands)
+    body = functools.partial(motion_kernel, low, frames)
     if earlier is None:
         kernel, aliases = body, {}
     else:
-        kernel, aliases = lambda *refs: body(*refs[:7], *refs[8:]), {7: 0}
+        kernel, aliases = lambda *refs: body(*refs[:count], *refs[count + 1 :]), {count: 0}
         operands.append(earlier)
     return pl.pallas_call(
         kernel,
         grid_spec=pltpu.PrefetchScalarGridSpec(
             num_scalar_prefetch=1,
             grid=(high - low,),
-            in_specs=[any_spec()] * 3 + [whole(flip), whole(mask), whole(base)] + [any_spec()] * (len(operands) - 7),
+            in_specs=[any_spec()] * (2 + frames) + [whole(flip), whole(mask), whole(base)] + [any_spec()] * (len(operands) - count),
             out_specs=pl.BlockSpec((1, buffer_rows, width, chans), lambda e, m: (e + low, 0, 0, 0)),
             scratch_shapes=[
                 pltpu.VMEM((2, buffer_rows, width, chans), BF16),
                 pltpu.VMEM((2, height, width, chans), BF16),
-                pltpu.VMEM((target_rows, width, chans), BF16),
+                pltpu.VMEM((chans, target_rows * width), BF16),
                 pltpu.VMEM((rows * width, 2 * chans), BF16),
                 pltpu.SemaphoreType.DMA((2, 2)),
             ],
@@ -264,7 +269,7 @@
     edges = pl.num_programs(0)
     frames = own.shape[0]
     height, width, chans = own.shape[2:]
-    slot = lax.rem(edge, 2)
+    slot = edge
     top = max(first - 1, 0)
     end = min(last + 1, height)
     rows = end - top
@@ -296,15 +301,12 @@
 
     @pl.when(edge == 0)
     def _():
-        start(edge, slot)
+        for e in range(state.shape[0]):
+            start(e, e)
         edge_row = jnp.zeros((1,) + columns.shape[1:], BF16)
         columns[0:1] = edge_row
         columns[rows + 1 :] = edge_row
         totals[...] = jnp.zeros(totals.shape, F32)
-
-    @pl.when(edge + 1 < edges)
-    def _():
-        start(edge + 1, 1 - slot)
 
     finish(slot)
 
@@ -320,12 +322,11 @@
         update_buf[span] = sigmoid(pre[..., :chans] + inputs[..., :chans])
         reset = sigmoid(pre[..., chans:] + inputs[..., chans : 2 * chans])
         drive_buf[span] = inputs[..., 2 * chans :]
-        held = (reset * state_buf[slot, span].astype(F32)).astype(BF16).astype(F32)
-        put_columns(columns, y + 1, held)
+        put_columns(columns, y + 1, reset * state_buf[slot, span].astype(F32))
 
     weights = w_candidate[...]
     place = meta[edge, 0] * frames + meta[edge, 1]
-    step = 8
+    step = 12
     for y in range(first, last, step):
         count = min(step, last - y)
         span = slice(y - top, y - top + count)
@@ -378,15 +379,15 @@
                 piece_spec,
             ],
             scratch_shapes=[
-                pltpu.VMEM((2, rows, width, chans), BF16),
-                pltpu.VMEM((2, rows, width, chans), BF16),
-                pltpu.VMEM((2, rows, width, 2 * chans), BF16),
-                pltpu.VMEM((2, rows, width, chans), BF16),
+                pltpu.VMEM((edges, rows, width, chans), BF16),
+                pltpu.VMEM((edges, rows, width, chans), BF16),
+                pltpu.VMEM((edges, rows, width, 2 * chans), BF16),
+                pltpu.VMEM((edges, rows, width, chans), BF16),
                 pltpu.VMEM((rows + 2, width, 3 * chans), BF16),
                 pltpu.VMEM((rows, width, chans), F32),
                 pltpu.VMEM((rows, width, chans), F32),
                 pltpu.VMEM((3 * frames, size, width, chans), F32),
-                pltpu.SemaphoreType.DMA((5, 2)),
+                pltpu.SemaphoreType.DMA((5, edges)),
             ],
         ),
         out_shape=[
@@ -416,17 +417,16 @@
     columns[columns.shape[0] - 1 :] = edge_row
     count = counts[pl.program_id(0)]
     at = 1
-    for i, (low, high) in enumerate(pieces):
+    for i in range(len(pieces)):
         own, far, *near = sums[4 * i : 4 * i + 4]
-        half = near[0].shape[1]
-        for k in range(2):
-            top, end = max(low - k * half, 0), min(high - k * half, half)
-            if end > top:
-                span = slice(k * half + top, k * half + end)
-                total = own[0, span].astype(F32) + far[0, span].astype(F32) + near[k][0, top:end].astype(F32)
-                mean = (total / count).astype(BF16).astype(F32)
-                put_columns(columns, at, mean)
-                at += end - top
+        top = 0
+        for piece in near[pieces[i][2] :]:
+            span = slice(top, top + piece.shape[1])
+            total = own[0, span].astype(F32) + far[0, span].astype(F32) + piece[0].astype(F32)
+            mean = (total / count).astype(BF16).astype(F32)
+            put_columns(columns, at, mean)
+            at += piece.shape[1]
+            top += piece.shape[1]
     step = 8
     base = 0
     if len(rest) == 3:
@@ -443,7 +443,16 @@
 def aggregate_of(first, last, pieces, bands, counts, weights, earlier):
     frames, _, width, chans = bands[0][0].shape
     sums = [array for band in bands for array in band]
-    depth = sum(high - low for low, high in pieces)
+    depth = sum(high - low for low, high, _ in pieces)
+
+    def blocks(band, low, high):
+        specs = []
+        for array in band:
+            count = min(high - low, array.shape[1])
+            index = low // count if array.shape[1] >= high else array.shape[1] // count - 1 if low else 0
+            specs.append(pl.BlockSpec((1, count) + array.shape[2:], lambda f, c, i=index: (f, i, 0, 0)))
+        return specs
+
     rows = last if earlier is not None else last - first
     operands = [counts, *sums, weights]
     more = []
@@ -455,7 +464,7 @@
         grid_spec=pltpu.PrefetchScalarGridSpec(
             num_scalar_prefetch=1,
             grid=(frames,),
-            in_specs=[pl.BlockSpec((1,) + array.shape[1:], lambda f, c: (f, 0, 0, 0)) for array in sums]
+            in_specs=[spec for band, (low, high, _) in zip(bands, pieces) for spec in blocks(band, low, high)]
             + [whole(weights)]
             + more,
             out_specs=pl.BlockSpec((1, rows, width, chans), lambda f, c: (f, 0, 0, 0)),
@@ -490,8 +499,12 @@
     def near_swap(block):
         return lax.ppermute(block, "rows", near_route)
 
-    far_feat = far_swap(frame_maps[:, 0])
-    near = near_swap(frame_maps)
+    far_feat, held = [], frame_maps
+    for f in range(frames):
+        feature = held[f, 0]
+        held = lax.optimization_barrier((frame_maps, feature))[0]
+        far_feat.append(far_swap(feature))
+    near = near_swap(held)
 
     my_edges = lax.dynamic_slice_in_dim(edges, me * edge_count, edge_count, 0)
     owner = my_edges // frames
@@ -505,13 +518,14 @@
 
     base = motion_weights(w_motion, width)
     gates = gates_of(net_state, lax.optimization_barrier((w_gates, near))[0])
-    half = edge_count // 2
-    held_meta = lax.optimization_barrier((meta, gates))[0]
+    half = 3 * edge_count // 4
+    split = height // 2 + 1
+    later_maps = lax.optimization_barrier((frame_maps, near))[0]
+    context_top, context_low = later_maps[:, 1, :split], later_maps[:, 1, split:]
+    held_meta = lax.optimization_barrier((meta, gates, context_top, context_low))[0]
     motion = motion_of(0, half, held_meta, frame_maps, near, far_feat, base, None)
-    context = lax.optimization_barrier((frame_maps, near))[0][:, 1]
-    split = height // 2 + 1
-    far_top = far_swap(context[:, :split], motion)
-    far_low = far_swap(context[:, split:], motion)
+    far_top = far_swap(context_top, motion)
+    far_low = far_swap(context_low, motion)
     motion = motion_of(half, edge_count, meta, frame_maps, near, far_feat, base, motion)
 
     def gru(band, earlier):
@@ -529,9 +543,9 @@
     first = (own_first, far_first, *near_first)
     second = (own_second, far_second, *near_second)
     size = height // 2
-    upper = aggregate_of(0, size - 1, ((0, size),), (first,), counts, w_aggregate, None)
+    upper = aggregate_of(0, size - 1, ((0, size, 0),), (first,), counts, w_aggregate, None)
     frame_update = aggregate_of(
-        size - 1, height, ((size - 2, size), (0, size)), (first, second), counts, w_aggregate, upper
+        size - 1, height, ((size - 2, size, 1), (0, size, 0)), (first, second), counts, w_aggregate, upper
     )
     return (new_state, frame_update)
 

time: 125 us -> 124 us (level)
  Pallas kernels: 68.3 us -> 63.3 us
  starting transfers between devices: 17.8 us -> 22.1 us
    ppermute x5 -> x6, starting transfers between devices: 16.7 us -> 21 us  [far_swap(): return lax.ppermute(block, 'rows', far_route)]
    pallas_call x2, Pallas kernels: 24.8 us -> 20.9 us  [motion_of(): pl.pallas_call(kernel, grid_spec=pltpu.PrefetchScalarGridSpec(num_scalar_...]
    squeeze x2 -> x4, local copies, waits for them, and re-layouts: 2.94 us -> 6.15 us  [the longest x2 4.28 us: per_device(): feature = held[f, 0]]
    slice x2 -> x0, local copies, waits for them, and re-layouts: 2.11 us -> none  [the longest x1 2.06 us: per_device(): far_low = far_swap(context[:, split:], motion)]
    ppermute x5 -> x6, waiting for transfers between devices: 23.9 us -> 23.6 us  [far_swap(): return lax.ppermute(block, 'rows', far_route)]
  transfers between devices with their start and end apart: 10 -> 11, of which waited for: 5 -> 7; matrix products, arithmetic and copies ran while one was open for 7% -> 5% of each run, Pallas kernels for 42% -> 37%
where the time goes in v6:
time: 124 us; the launch traced here: 123 us
  Pallas kernels  63.3 us (51%)
  waiting for transfers between devices  24.9 us (20%)
  starting transfers between devices  22.1 us (18%)
  local copies, waits for them, and re-layouts  10.3 us (8%)
    pallas_call x2, Pallas kernels, gru_of(): pl.pallas_call(kernel, grid_spec=pltpu.PrefetchScalarGridSpec(num_scalar_...  24.1 us
    ppermute x6, waiting for transfers between devices, far_swap(): return lax.ppermute(block, 'rows', far_route)  23.6 us
    ppermute x6, starting transfers between devices, far_swap(): return lax.ppermute(block, 'rows', far_route)  21 us
    pallas_call x2, Pallas kernels, motion_of(): pl.pallas_call(kernel, grid_spec=pltpu.PrefetchScalarGridSpec(num_scalar_...  20.9 us
    pallas_call x1, Pallas kernels, gates_of(): pl.pallas_call(gates_kernel, grid=(edges,), in_specs=[pl.BlockSpec((1, he...  11.5 us
    pallas_call x2, Pallas kernels, aggregate_of(): pl.pallas_call(functools.partial(aggregate_kernel, pieces, first, last),...  6.86 us
    squeeze x2, local copies, waits for them, and re-layouts, per_device(): feature = held[f, 0]  4.28 us
    unnamed x24, local copies, waits for them, and re-layouts  2.67 us
  transfers between devices with their start and end apart: 11, of which 7 were waited for; matrix products, arithmetic and copies ran while one was open for 5% of the time, Pallas kernels for 37%

profile of v6, /device:TPU:1, one launch (start us, length us, event | category | flops | bytes accessed | tf_op | source)
XLA Modules:
  0.0 123.0 jit_solution(1251921880609530283)
XLA Ops:
  0.7 2.2 %slice_bitcast_fusion.2 = bf16[48,64,128]{2,1,0:T(8,128)(2,1)} fusion(bf16[2,2,48,64,128]{4,3,2,1,0:T(8,128)(2,1)} %own.3), kind=kLoop, calls=%fused_computation.2 | loop fusion | bytes 1572864 | tf_op jit(solution)/shard_map/squeeze | solution.py:504
  2.9 2.1 %slice_bitcast_fusion.1 = bf16[48,64,128]{2,1,0:T(8,128)(2,1)} fusion(bf16[2,2,48,64,128]{4,3,2,1,0:T(8,128)(2,1)} %own.3), kind=kLoop, calls=%fused_computation.1 | loop fusion | bytes 1572864 | tf_op jit(solution)/shard_map/squeeze | solution.py:504
  5.0 4.5 %collective-permute-start.2 = (bf16[48,64,128]{2,1,0:T(8,128)(2,1)}, bf16[48,64,128]{2,1,0:T(8,128)(2,1)}, u32[]{:S(2)}, u32[]{:S(2)}) collective-permute-start(bf16[48,64,128]{2,1,0:T(8,128)(2,1)} %slice_bitcast_fusion.1), channel_id=1, source_target_pairs={{1,2},{2,1},{3,4},{4,3},{5,6},{6,5},{7,8},{8,7},{9,10},{10,9},{11,... | collective-permute-start | bytes 2359304 | tf_op jit(solution)/shard_map/ppermute | solution.py:497
  9.5 1.9 %collective-permute-start.1 = (bf16[48,64,128]{2,1,0:T(8,128)(2,1)}, bf16[48,64,128]{2,1,0:T(8,128)(2,1)}, u32[]{:S(2)}, u32[]{:S(2)}) collective-permute-start(bf16[48,64,128]{2,1,0:T(8,128)(2,1)} %slice_bitcast_fusion.2), channel_id=1, source_target_pairs={{1,2},{2,1},{3,4},{4,3},{5,6},{6,5},{7,8},{8,7},{9,10},{10,9},{11,... | collective-permute-start | bytes 2359304 | tf_op jit(solution)/shard_map/ppermute | solution.py:497
  14.3 0.9 pad_maximum_fusion.refs_4_.refs_7_
  15.2 0.9 slice_bitcast_fusion
  16.1 0.9 slice_bitcast_fusion.3
  17.1 11.5 %gates.1.refs_6_ = bf16[4,48,64,256]{3,2,1,0:T(8,128)(2,1)} custom-call(bf16[4,48,64,128]{3,2,1,0:T(8,128)(2,1)} %state.1, bf16[1152,256]{1,0:T(8,128)(2,1)} %weights_ref), custom_call_target="tpu_custom_call" | custom-call | flops 7247757312 | bytes 9437184 | tf_op jit(solution)/shard_map/gates/pallas_call | solution.py:83
  28.5 7.1 %collective-permute-done.2.refs_1_.refs_4_ = bf16[48,64,128]{2,1,0:T(8,128)(2,1)} collective-permute-done((bf16[48,64,128]{2,1,0:T(8,128)(2,1)}, bf16[48,64,128]{2,1,0:T(8,128)(2,1)}, u32[]{:S(2)}, u32[]{:S(2)}) %collective-permute-start.2) | collective-permute-done | bytes 786464 | tf_op jit(solution)/shard_map/ppermute | solution.py:497
  35.6 8.4 %collective-permute-done.1.refs_0_.refs_3_ = bf16[48,64,128]{2,1,0:T(8,128)(2,1)} collective-permute-done((bf16[48,64,128]{2,1,0:T(8,128)(2,1)}, bf16[48,64,128]{2,1,0:T(8,128)(2,1)}, u32[]{:S(2)}, u32[]{:S(2)}) %collective-permute-start.1) | collective-permute-done | bytes 786464 | tf_op jit(solution)/shard_map/ppermute | solution.py:497
  44.0 13.7 %motion_from0.1.refs_8_ = bf16[4,52,64,128]{3,2,1,0:T(8,128)(2,1)} custom-call(s32[4,6]{1,0:T(4,128)} %stack.3.meta.refs_0_, bf16[2,2,48,64,128]{4,3,2,1,0:T(8,128)(2,1)} %own.3, bf16[2,2,48,64,128]{4,3,2,1,0:T(8,128)(2,1)} %collective-permute-done.near.refs_2_, bf16[48,64,128]{2,1,0:T(8,128)(2,1)} %collective-permute-done.1.refs_0_.refs_3_, ...), custom_call_target="tpu_custom_call" | custom-call | flops 6039797760 | bytes 7077888 | tf_op jit(solution)/shard_map/motion_from0/pallas_call | solution.py:212
  57.8 4.3 %collective-permute-start.3 = (bf16[2,25,64,128]{3,2,1,0:T(8,128)(2,1)S(1)}, bf16[2,25,64,128]{3,2,1,0:T(8,128)(2,1)S(1)}, u32[]{:S(2)}, u32[]{:S(2)}) collective-permute-start(bf16[2,25,64,128]{3,2,1,0:T(8,128)(2,1)S(1)} %copy-done.6), channel_id=1, source_target_pairs={{1,2},{2,1},{3,4},{4,3},{5,6},{6,5},{7,8},{8,7},{9,10},{10,9},{11,... | collective-permute-start | bytes 2457608 | tf_op jit(solution)/shard_map/ppermute | solution.py:497
  62.1 1.9 %collective-permute-start.4 = (bf16[2,23,64,128]{3,2,1,0:T(8,128)(2,1)}, bf16[2,23,64,128]{3,2,1,0:T(8,128)(2,1)S(1)}, u32[]{:S(2)}, u32[]{:S(2)}) collective-permute-start(bf16[2,23,64,128]{3,2,1,0:T(8,128)(2,1)} %slice_bitcast_fusion.3), channel_id=1, source_target_pairs={{1,2},{2,1},{3,4},{4,3},{5,6},{6,5},{7,8},{8,7},{9,10},{10,9},{11,... | collective-permute-start | bytes 2261000 | tf_op jit(solution)/shard_map/ppermute | solution.py:497
  64.0 7.1 %motion_from3.1.refs_5_.motion = bf16[4,52,64,128]{3,2,1,0:T(8,128)(2,1)} custom-call(s32[4,6]{1,0:T(4,128)} %stack.3.meta.refs_0_, bf16[2,2,48,64,128]{4,3,2,1,0:T(8,128)(2,1)} %own.3, bf16[2,2,48,64,128]{4,3,2,1,0:T(8,128)(2,1)} %collective-permute-done.near.refs_2_, ...), custom_call_target="tpu_custom_call", output_to_operand_aliasing={{}: (8, {})} | custom-call | flops 2013265920 | bytes 2359296 | tf_op jit(solution)/shard_map/motion_from3/pallas_call | solution.py:212
  71.1 3.5 %collective-permute-done.3.refs_3_.refs_4_.far_top = bf16[2,25,64,128]{3,2,1,0:T(8,128)(2,1)S(1)} collective-permute-done((bf16[2,25,64,128]{3,2,1,0:T(8,128)(2,1)S(1)}, bf16[2,25,64,128]{3,2,1,0:T(8,128)(2,1)S(1)}, u32[]{:S(2)}, u32[]{:S(2)}) %collective-permute-start.3) | collective-permute-done | bytes 819232 | tf_op jit(solution)/shard_map/ppermute | solution.py:497
  74.6 0.9 copy-done.5
  75.5 12.0 %gru_band0.1 = (bf16[4,48,64,128]{3,2,1,0:T(8,128)(2,1)}, bf16[2,24,64,128]{3,2,1,0:T(8,128)(2,1)}, bf16[2,24,64,128]{3,2,1,0:T(8,128)(2,1)}, bf16[2,12,64,128]{3,2,1,0:T(8,128)(2,1)}, bf16[2,12,64,128]{3,2,1,0:T(8,128)(2,1)}) custom-call(s32[4,6]{1,0:T(4,128)} %stack.3.meta.refs_0_, bf16[2,2,48,64,128]{4,3,2,1,0:T(8,128)(2,1)} %own.3, ...), custom_call_target="tpu_custom_call" | custom-call | flops 1638400 | bytes 1638400 | tf_op jit(solution)/shard_map/gru_band0/pallas_call | solution.py:368
  87.5 4.9 %collective-permute-start.5 = (bf16[2,24,64,128]{3,2,1,0:T(8,128)(2,1)}, bf16[2,24,64,128]{3,2,1,0:T(8,128)(2,1)S(1)}, u32[]{:S(2)}, u32[]{:S(2)}) collective-permute-start(bf16[2,24,64,128]{3,2,1,0:T(8,128)(2,1)} %get-tuple-element.33), channel_id=1, source_target_pairs={{1,2},{2,1},{3,4},{4,3},{5,6},{6,5},{7,8},{8,7},{9,10},{10,9},{11,... | collective-permute-start | bytes 2359304 | tf_op jit(solution)/shard_map/ppermute | solution.py:497
  93.3 12.1 %gru_band1.1 = (bf16[4,48,64,128]{3,2,1,0:T(8,128)(2,1)}, bf16[2,24,64,128]{3,2,1,0:T(8,128)(2,1)}, bf16[2,24,64,128]{3,2,1,0:T(8,128)(2,1)}, bf16[2,12,64,128]{3,2,1,0:T(8,128)(2,1)}, bf16[2,12,64,128]{3,2,1,0:T(8,128)(2,1)}) custom-call(s32[4,6]{1,0:T(4,128)} %stack.3.meta.refs_0_, ...), custom_call_target="tpu_custom_call", output_to_operand_aliasing={{0}: (10, {})} | custom-call | flops 1638400 | bytes 1638400 | tf_op jit(solution)/shard_map/gru_band1/pallas_call | solution.py:368
  105.4 3.6 %collective-permute-start.8 = (bf16[2,24,64,128]{3,2,1,0:T(8,128)(2,1)}, bf16[2,24,64,128]{3,2,1,0:T(8,128)(2,1)S(1)}, u32[]{:S(2)}, u32[]{:S(2)}) collective-permute-start(bf16[2,24,64,128]{3,2,1,0:T(8,128)(2,1)} %get-tuple-element.39), channel_id=1, source_target_pairs={{1,2},{2,1},{3,4},{4,3},{5,6},{6,5},{7,8},{8,7},{9,10},{10,9},{11,... | collective-permute-start | bytes 2359304 | tf_op jit(solution)/shard_map/ppermute | solution.py:497
  109.0 0.9 collective-permute-done.5.refs_1_
  112.4 2.9 %aggregate_from0.1.refs_9_ = bf16[2,23,64,128]{3,2,1,0:T(8,128)(2,1)S(1)} custom-call(f32[2]{0:T(128)S(1)} %broadcast_maximum_fusion.counts, bf16[2,24,64,128]{3,2,1,0:T(8,128)(2,1)S(1)} %copy-done.1, bf16[2,24,64,128]{3,2,1,0:T(8,128)(2,1)S(1)} %collective-permute-done.5.refs_1_, bf16[2,12,64,128]{3,2,1,0:T(8,128)(2,1)S(1)} %collective-permute-done.6.refs_2_, ...), custom_call_target="tpu_custom_call" | custom-call | flops 868220928 | bytes 3145728 | tf_op jit(solution)/shard_map/aggregate_from0/pallas_call | solution.py:462
  115.3 3.8 %collective-permute-done.8.refs_5_ = bf16[2,24,64,128]{3,2,1,0:T(8,128)(2,1)S(1)} collective-permute-done((bf16[2,24,64,128]{3,2,1,0:T(8,128)(2,1)}, bf16[2,24,64,128]{3,2,1,0:T(8,128)(2,1)S(1)}, u32[]{:S(2)}, u32[]{:S(2)}) %collective-permute-start.8) | collective-permute-done | bytes 786464 | tf_op jit(solution)/shard_map/ppermute | solution.py:497
  119.1 4.0 %aggregate_from23.1 = bf16[2,48,64,128]{3,2,1,0:T(8,128)(2,1)} custom-call(f32[2]{0:T(128)S(1)} %broadcast_maximum_fusion.counts, bf16[2,24,64,128]{3,2,1,0:T(8,128)(2,1)S(1)} %copy-done.1, bf16[2,24,64,128]{3,2,1,0:T(8,128)(2,1)S(1)} %collective-permute-done.5.refs_1_, bf16[2,12,64,128]{3,2,1,0:T(8,128)(2,1)S(1)} %collective-permute-done.6.refs_2_, ...), custom_call_target="tpu_custom_call" | custom-call | flops 943718400 | bytes 3407872 | tf_op jit(solution)/shard_map/aggregate_from23/pallas_call | solution.py:462
  (44 shorter events, 6.3 us)
Async XLA Ops:
  0.6 13.2 %copy-start = (bf16[81,128]{1,0:T(8,128)(2,1)S(1)}, bf16[81,128]{1,0:T(8,128)(2,1)}, u32[]{:S(2)}) copy-start(bf16[81,128]{1,0:T(8,128)(2,1)} %param.19) | copy-start | bytes 62212
  0.6 13.2 %copy-start.9 = (bf16[5,128,81]{1,2,0:T(8,128)(2,1)S(1)}, bf16[5,128,81]{1,2,0:T(8,128)(2,1)}, u32[]{:S(2)}) copy-start(bf16[5,128,81]{1,2,0:T(8,128)(2,1)} %constant.48.clone) | copy-start | bytes 311044
  0.7 13.4 %copy-start.8 = (bf16[5,128,81]{1,2,0:T(8,128)(2,1)S(1)}, bf16[5,128,81]{1,2,0:T(8,128)(2,1)}, u32[]{:S(2)}) copy-start(bf16[5,128,81]{1,2,0:T(8,128)(2,1)} %constant.49.clone) | copy-start | bytes 311044
  0.7 14.5 %copy-start.4 = (bf16[2,2,48,64,128]{4,3,2,1,0:T(8,128)(2,1)S(1)}, bf16[2,2,48,64,128]{4,3,2,1,0:T(8,128)(2,1)}, u32[]{:S(2)}) copy-start(bf16[2,2,48,64,128]{4,3,2,1,0:T(8,128)(2,1)} %own.3) | copy-start | bytes 9437188
  5.0 10.2 %collective-permute-start = (bf16[2,2,48,64,128]{4,3,2,1,0:T(8,128)(2,1)}, bf16[2,2,48,64,128]{4,3,2,1,0:T(8,128)(2,1)}, u32[]{:S(2)}, u32[]{:S(2)}) collective-permute-start(bf16[2,2,48,64,128]{4,3,2,1,0:T(8,128)(2,1)} %own.3), channel_id=1, source_target_pairs={{0,1},{1,0},{2,3},{3,2},{4,5},{5,4},{6,7},{7,6},{8,9},{9,8},{10,11... | collective-permute-start | bytes 9437192 | tf_op jit(solution)/shard_map/ppermute | solution.py:500
  5.0 30.6 %collective-permute-start.2 = (bf16[48,64,128]{2,1,0:T(8,128)(2,1)}, bf16[48,64,128]{2,1,0:T(8,128)(2,1)}, u32[]{:S(2)}, u32[]{:S(2)}) collective-permute-start(bf16[48,64,128]{2,1,0:T(8,128)(2,1)} %slice_bitcast_fusion.1), channel_id=1, source_target_pairs={{1,2},{2,1},{3,4},{4,3},{5,6},{6,5},{7,8},{8,7},{9,10},{10,9},{11,... | collective-permute-start | bytes 2359304 | tf_op jit(solution)/shard_map/ppermute | solution.py:497
  9.5 34.5 %collective-permute-start.1 = (bf16[48,64,128]{2,1,0:T(8,128)(2,1)}, bf16[48,64,128]{2,1,0:T(8,128)(2,1)}, u32[]{:S(2)}, u32[]{:S(2)}) collective-permute-start(bf16[48,64,128]{2,1,0:T(8,128)(2,1)} %slice_bitcast_fusion.2), channel_id=1, source_target_pairs={{1,2},{2,1},{3,4},{4,3},{5,6},{6,5},{7,8},{8,7},{9,10},{10,9},{11,... | collective-permute-start | bytes 2359304 | tf_op jit(solution)/shard_map/ppermute | solution.py:497
  28.5 29.2 %copy-start.6 = (bf16[2,25,64,128]{3,2,1,0:T(8,128)(2,1)S(1)}, bf16[2,25,64,128]{3,2,1,0:T(8,128)(2,1)}, u32[]{:S(2)}) copy-start(bf16[2,25,64,128]{3,2,1,0:T(8,128)(2,1)} %slice_bitcast_fusion) | copy-start | bytes 2457604
  57.8 16.8 %collective-permute-start.3 = (bf16[2,25,64,128]{3,2,1,0:T(8,128)(2,1)S(1)}, bf16[2,25,64,128]{3,2,1,0:T(8,128)(2,1)S(1)}, u32[]{:S(2)}, u32[]{:S(2)}) collective-permute-start(bf16[2,25,64,128]{3,2,1,0:T(8,128)(2,1)S(1)} %copy-done.6), channel_id=1, source_target_pairs={{1,2},{2,1},{3,4},{4,3},{5,6},{6,5},{7,8},{8,7},{9,10},{10,9},{11,... | collective-permute-start | bytes 2457608 | tf_op jit(solution)/shard_map/ppermute | solution.py:497
  62.1 30.3 %collective-permute-start.4 = (bf16[2,23,64,128]{3,2,1,0:T(8,128)(2,1)}, bf16[2,23,64,128]{3,2,1,0:T(8,128)(2,1)S(1)}, u32[]{:S(2)}, u32[]{:S(2)}) collective-permute-start(bf16[2,23,64,128]{3,2,1,0:T(8,128)(2,1)} %slice_bitcast_fusion.3), channel_id=1, source_target_pairs={{1,2},{2,1},{3,4},{4,3},{5,6},{6,5},{7,8},{8,7},{9,10},{10,9},{11,... | collective-permute-start | bytes 2261000 | tf_op jit(solution)/shard_map/ppermute | solution.py:497
  74.6 0.9 copy-start.5
  87.5 22.4 %collective-permute-start.5 = (bf16[2,24,64,128]{3,2,1,0:T(8,128)(2,1)}, bf16[2,24,64,128]{3,2,1,0:T(8,128)(2,1)S(1)}, u32[]{:S(2)}, u32[]{:S(2)}) collective-permute-start(bf16[2,24,64,128]{3,2,1,0:T(8,128)(2,1)} %get-tuple-element.33), channel_id=1, source_target_pairs={{1,2},{2,1},{3,4},{4,3},{5,6},{6,5},{7,8},{8,7},{9,10},{10,9},{11,... | collective-permute-start | bytes 2359304 | tf_op jit(solution)/shard_map/ppermute | solution.py:497
  92.4 0.9 copy-start.7
  93.3 15.7 %copy-start.10 = (s32[64,2]{0,1:T(2,128)S(1)}, s32[64,2]{0,1:T(2,128)}, u32[]{:S(2)}) copy-start(s32[64,2]{0,1:T(2,128)} %param.17) | copy-start | bytes 1540
  93.3 19.1 %copy-start.1 = (bf16[2,24,64,128]{3,2,1,0:T(8,128)(2,1)S(1)}, bf16[2,24,64,128]{3,2,1,0:T(8,128)(2,1)}, u32[]{:S(2)}) copy-start(bf16[2,24,64,128]{3,2,1,0:T(8,128)(2,1)} %get-tuple-element.32.refs_0_) | copy-start | bytes 2359300
  93.3 19.1 %copy-start.2 = (bf16[1152,128]{1,0:T(8,128)(2,1)S(1)}, bf16[1152,128]{1,0:T(8,128)(2,1)}, u32[]{:S(2)}) copy-start(bf16[1152,128]{1,0:T(8,128)(2,1)} %refs_8_.3) | copy-start | bytes 884740
  105.4 13.7 %copy-start.3 = (bf16[2,24,64,128]{3,2,1,0:T(8,128)(2,1)S(1)}, bf16[2,24,64,128]{3,2,1,0:T(8,128)(2,1)}, u32[]{:S(2)}) copy-start(bf16[2,24,64,128]{3,2,1,0:T(8,128)(2,1)} %get-tuple-element.38.refs_4_) | copy-start | bytes 2359300
  105.4 13.7 %collective-permute-start.8 = (bf16[2,24,64,128]{3,2,1,0:T(8,128)(2,1)}, bf16[2,24,64,128]{3,2,1,0:T(8,128)(2,1)S(1)}, u32[]{:S(2)}, u32[]{:S(2)}) collective-permute-start(bf16[2,24,64,128]{3,2,1,0:T(8,128)(2,1)} %get-tuple-element.39), channel_id=1, source_target_pairs={{1,2},{2,1},{3,4},{4,3},{5,6},{6,5},{7,8},{8,7},{9,10},{10,9},{11,... | collective-permute-start | bytes 2359304 | tf_op jit(solution)/shard_map/ppermute | solution.py:497
  109.9 1.9 %collective-permute-start.6 = (bf16[2,12,64,128]{3,2,1,0:T(8,128)(2,1)}, bf16[2,12,64,128]{3,2,1,0:T(8,128)(2,1)S(1)}, u32[]{:S(2)}, u32[]{:S(2)}) collective-permute-start(bf16[2,12,64,128]{3,2,1,0:T(8,128)(2,1)} %get-tuple-element.36), channel_id=1, source_target_pairs={{0,1},{1,0},{2,3},{3,2},{4,5},{5,4},{6,7},{7,6},{8,9},{9,8},{10,11... | collective-permute-start | bytes 1179656 | tf_op jit(solution)/shard_map/ppermute | solution.py:500
  109.9 2.5 %collective-permute-start.7 = (bf16[2,12,64,128]{3,2,1,0:T(8,128)(2,1)}, bf16[2,12,64,128]{3,2,1,0:T(8,128)(2,1)S(1)}, u32[]{:S(2)}, u32[]{:S(2)}) collective-permute-start(bf16[2,12,64,128]{3,2,1,0:T(8,128)(2,1)} %get-tuple-element.37), channel_id=1, source_target_pairs={{0,1},{1,0},{2,3},{3,2},{4,5},{5,4},{6,7},{7,6},{8,9},{9,8},{10,11... | collective-permute-start | bytes 1179656 | tf_op jit(solution)/shard_map/ppermute | solution.py:500
  110.4 8.7 %collective-permute-start.9 = (bf16[2,12,64,128]{3,2,1,0:T(8,128)(2,1)}, bf16[2,12,64,128]{3,2,1,0:T(8,128)(2,1)S(1)}, u32[]{:S(2)}, u32[]{:S(2)}) collective-permute-start(bf16[2,12,64,128]{3,2,1,0:T(8,128)(2,1)} %get-tuple-element.42), channel_id=1, source_target_pairs={{0,1},{1,0},{2,3},{3,2},{4,5},{5,4},{6,7},{7,6},{8,9},{9,8},{10,11... | collective-permute-start | bytes 1179656 | tf_op jit(solution)/shard_map/ppermute | solution.py:500
  110.4 8.7 %collective-permute-start.10 = (bf16[2,12,64,128]{3,2,1,0:T(8,128)(2,1)}, bf16[2,12,64,128]{3,2,1,0:T(8,128)(2,1)S(1)}, u32[]{:S(2)}, u32[]{:S(2)}) collective-permute-start(bf16[2,12,64,128]{3,2,1,0:T(8,128)(2,1)} %get-tuple-element.43), channel_id=1, source_target_pairs={{0,1},{1,0},{2,3},{3,2},{4,5},{5,4},{6,7},{7,6},{8,9},{9,8},{10,11... | collective-permute-start | bytes 1179656 | tf_op jit(solution)/shard_map/ppermute | solution.py:500

commit v7 on v6

--- a/solution.py
+++ b/solution.py
@@ -15,6 +15,7 @@
 F32 = jnp.float32
 BF16 = jnp.bfloat16
 VMEM_LIMIT = 60 << 20
+MOTION_VMEM_LIMIT = 127 << 19
 
 
 def any_spec():
@@ -97,9 +98,7 @@
     )(state, weights)
 
 
-def motion_kernel(low, frames, meta, own, near, *refs):
-    fars = refs[:frames]
-    flip_ref, mask_ref, base_ref, out_ref, src_buf, raw_buf, tgt_buf, w_buf, sems = refs[frames:]
+def motion_kernel(low, meta, own, near, far, flip_ref, mask_ref, base_ref, out_ref, src_buf, raw_buf, tgt_buf, w_buf, sems):
     step = pl.program_id(0)
     steps = pl.num_programs(0)
     edge = step + low
@@ -110,8 +109,7 @@
 
     def start(e, s):
         def cases(buf, frame):
-            far_cases = [((buf == 1) & (frame == f), far) for f, far in enumerate(fars)]
-            return [(buf == 0, own.at[frame, 0]), (buf == 2, near.at[frame, 0])] + far_cases
+            return ((buf == 0, own.at[frame, 0]), (buf == 1, far.at[frame]), (buf == 2, near.at[frame, 0]))
 
         fetch(cases(meta[e, 0], meta[e, 1]), src_buf.at[s, pl.ds(1, height)], sems.at[0, s])
         fetch(cases(meta[e, 2], meta[e, 3]), raw_buf.at[s], sems.at[1, s])
@@ -194,16 +192,16 @@
     )
 
 
-def motion_of(low, high, meta, own, near, fars, base, earlier):
-    frames, _, height, width, chans = own.shape
+def motion_of(low, high, meta, own, near, far, base, earlier):
+    _, _, height, width, chans = own.shape
     edges = meta.shape[0]
     rows = SPAN + 1
     _, flip, mask = motion_constants(width, chans)
     buffer_rows = height + 4
     target_rows = height + 2 * MARGIN + 2
-    operands = [meta, own, near, *fars, flip, mask, base]
+    operands = [meta, own, near, far, flip, mask, base]
     count = len(operands)
-    body = functools.partial(motion_kernel, low, frames)
+    body = functools.partial(motion_kernel, low)
     if earlier is None:
         kernel, aliases = body, {}
     else:
@@ -214,7 +212,7 @@
         grid_spec=pltpu.PrefetchScalarGridSpec(
             num_scalar_prefetch=1,
             grid=(high - low,),
-            in_specs=[any_spec()] * (2 + frames) + [whole(flip), whole(mask), whole(base)] + [any_spec()] * (len(operands) - count),
+            in_specs=[any_spec()] * 3 + [whole(flip), whole(mask), whole(base)] + [any_spec()] * (len(operands) - count),
             out_specs=pl.BlockSpec((1, buffer_rows, width, chans), lambda e, m: (e + low, 0, 0, 0)),
             scratch_shapes=[
                 pltpu.VMEM((2, buffer_rows, width, chans), BF16),
@@ -226,7 +224,7 @@
         ),
         out_shape=jax.ShapeDtypeStruct((edges, buffer_rows, width, chans), BF16),
         input_output_aliases=aliases,
-        compiler_params=pltpu.CompilerParams(vmem_limit_bytes=VMEM_LIMIT),
+        compiler_params=pltpu.CompilerParams(vmem_limit_bytes=MOTION_VMEM_LIMIT),
         cost_estimate=pl.CostEstimate(
             flops=8 * (high - low) * height * width * chans * rows * width,
             bytes_accessed=6 * (high - low) * height * width * chans,
@@ -499,12 +497,9 @@
     def near_swap(block):
         return lax.ppermute(block, "rows", near_route)
 
-    far_feat, held = [], frame_maps
-    for f in range(frames):
-        feature = held[f, 0]
-        held = lax.optimization_barrier((frame_maps, feature))[0]
-        far_feat.append(far_swap(feature))
-    near = near_swap(held)
+    features = frame_maps[:, 0]
+    far_feat = far_swap(features)
+    near = near_swap(lax.optimization_barrier((frame_maps, features))[0])
 
     my_edges = lax.dynamic_slice_in_dim(edges, me * edge_count, edge_count, 0)
     owner = my_edges // frames

time: 124 us -> 120 us (0.968)
  local copies, waits for them, and re-layouts: 10.3 us -> 6.83 us
    squeeze x2 -> x1, local copies, waits for them, and re-layouts: 4.28 us -> 1.63 us  [per_device(): features = frame_maps[:, 0]]
    unnamed x24 -> x22, local copies, waits for them, and re-layouts: 2.67 us -> 0.24 us
    ppermute x6 -> x5, starting transfers between devices: 21 us -> 19.9 us  [far_swap(): return lax.ppermute(block, 'rows', far_route)]
    ppermute x6 -> x5, waiting for transfers between devices: 23.6 us -> 23.5 us  [far_swap(): return lax.ppermute(block, 'rows', far_route)]
  transfers between devices with their start and end apart: 11 -> 10, of which waited for: 7 -> 6; matrix products, arithmetic and copies ran while one was open for 5% -> 6% of each run, Pallas kernels for 37% -> 38%
where the time goes in v7:
time: 120 us
  Pallas kernels  64.3 us (54%)
  waiting for transfers between devices  25.1 us (21%)
  starting transfers between devices  21 us (18%)
  local copies, waits for them, and re-layouts  6.83 us (6%)
    pallas_call x2, Pallas kernels, gru_of(): pl.pallas_call(kernel, grid_spec=pltpu.PrefetchScalarGridSpec(num_scalar_...  24.1 us
    ppermute x5, waiting for transfers between devices, far_swap(): return lax.ppermute(block, 'rows', far_route)  23.5 us
    pallas_call x2, Pallas kernels, motion_of(): pl.pallas_call(kernel, grid_spec=pltpu.PrefetchScalarGridSpec(num_scalar_...  20.8 us
    ppermute x5, starting transfers between devices, far_swap(): return lax.ppermute(block, 'rows', far_route)  19.9 us
    pallas_call x1, Pallas kernels, gates_of(): pl.pallas_call(gates_kernel, grid=(edges,), in_specs=[pl.BlockSpec((1, he...  11.5 us
    pallas_call x2, Pallas kernels, aggregate_of(): pl.pallas_call(functools.partial(aggregate_kernel, pieces, first, last),...  7.87 us
  transfers between devices with their start and end apart: 10, of which 6 were waited for; matrix products, arithmetic and copies ran while one was open for 6% of the time, Pallas kernels for 38%

profile of v7, /device:TPU:1, one launch (start us, length us, event | category | flops | bytes accessed | tf_op | source)
XLA Modules:
  0.0 119.7 jit_solution(1751782932258959921)
XLA Ops:
  0.7 1.6 %slice_bitcast_fusion = bf16[2,48,64,128]{3,2,1,0:T(8,128)(2,1)S(1)} fusion(bf16[2,2,48,64,128]{4,3,2,1,0:T(8,128)(2,1)} %own.3), kind=kLoop, calls=%fused_computation | loop fusion | bytes 3145728 | tf_op jit(solution)/shard_map/squeeze | solution.py:500
  2.4 4.5 %collective-permute-start.1 = (bf16[2,48,64,128]{3,2,1,0:T(8,128)(2,1)S(1)}, bf16[2,48,64,128]{3,2,1,0:T(8,128)(2,1)}, u32[]{:S(2)}, u32[]{:S(2)}) collective-permute-start(bf16[2,48,64,128]{3,2,1,0:T(8,128)(2,1)S(1)} %slice_bitcast_fusion), channel_id=1, source_target_pairs={{1,2},{2,1},{3,4},{4,3},{5,6},{6,5},{7,8},{8,7},{9,10},{10,9},{11,... | collective-permute-start | bytes 4718600 | tf_op jit(solution)/shard_map/ppermute | solution.py:495
  7.6 0.7 stack.3.meta.refs_0_
  8.5 0.9 pad_maximum_fusion.base_ref.refs_6_
  9.4 2.0 %slice_bitcast_fusion.2 = bf16[2,23,64,128]{3,2,1,0:T(8,128)(2,1)} fusion(bf16[2,2,48,64,128]{4,3,2,1,0:T(8,128)(2,1)} %own.3), kind=kLoop, calls=%fused_computation.2 | loop fusion | bytes 1507328 | tf_op jit(solution)/shard_map/squeeze | solution.py:519
  11.4 2.1 %slice_bitcast_fusion.1 = bf16[2,25,64,128]{3,2,1,0:T(8,128)(2,1)} fusion(bf16[2,2,48,64,128]{4,3,2,1,0:T(8,128)(2,1)} %own.3), kind=kLoop, calls=%fused_computation.1 | loop fusion | bytes 1638400 | tf_op jit(solution)/shard_map/squeeze | solution.py:519
  13.5 11.5 %gates.1.refs_6_ = bf16[4,48,64,256]{3,2,1,0:T(8,128)(2,1)} custom-call(bf16[4,48,64,128]{3,2,1,0:T(8,128)(2,1)} %state.1, bf16[1152,256]{1,0:T(8,128)(2,1)} %weights_ref), custom_call_target="tpu_custom_call" | custom-call | flops 7247757312 | bytes 9437184 | tf_op jit(solution)/shard_map/gates/pallas_call | solution.py:84
  25.0 16.2 %collective-permute-done.1.far.refs_3_ = bf16[2,48,64,128]{3,2,1,0:T(8,128)(2,1)} collective-permute-done((bf16[2,48,64,128]{3,2,1,0:T(8,128)(2,1)S(1)}, bf16[2,48,64,128]{3,2,1,0:T(8,128)(2,1)}, u32[]{:S(2)}, u32[]{:S(2)}) %collective-permute-start.1) | collective-permute-done | bytes 1572896 | tf_op jit(solution)/shard_map/ppermute | solution.py:495
  41.1 13.7 %motion_from0.1.refs_7_ = bf16[4,52,64,128]{3,2,1,0:T(8,128)(2,1)} custom-call(s32[4,6]{1,0:T(4,128)} %stack.3.meta.refs_0_, bf16[2,2,48,64,128]{4,3,2,1,0:T(8,128)(2,1)} %own.3, bf16[2,2,48,64,128]{4,3,2,1,0:T(8,128)(2,1)} %collective-permute-done.near.refs_2_, bf16[2,48,64,128]{3,2,1,0:T(8,128)(2,1)} %collective-permute-done.1.far.refs_3_, ...), custom_call_target="tpu_custom_call" | custom-call | flops 6039797760 | bytes 7077888 | tf_op jit(solution)/shard_map/motion_from0/pallas_call | solution.py:210
  54.8 4.5 %collective-permute-start.2 = (bf16[2,25,64,128]{3,2,1,0:T(8,128)(2,1)}, bf16[2,25,64,128]{3,2,1,0:T(8,128)(2,1)}, u32[]{:S(2)}, u32[]{:S(2)}) collective-permute-start(bf16[2,25,64,128]{3,2,1,0:T(8,128)(2,1)} %slice_bitcast_fusion.1), channel_id=1, source_target_pairs={{1,2},{2,1},{3,4},{4,3},{5,6},{6,5},{7,8},{8,7},{9,10},{10,9},{11,... | collective-permute-start | bytes 2457608 | tf_op jit(solution)/shard_map/ppermute | solution.py:495
  59.3 1.9 %collective-permute-start.3 = (bf16[2,23,64,128]{3,2,1,0:T(8,128)(2,1)}, bf16[2,23,64,128]{3,2,1,0:T(8,128)(2,1)}, u32[]{:S(2)}, u32[]{:S(2)}) collective-permute-start(bf16[2,23,64,128]{3,2,1,0:T(8,128)(2,1)} %slice_bitcast_fusion.2), channel_id=1, source_target_pairs={{1,2},{2,1},{3,4},{4,3},{5,6},{6,5},{7,8},{8,7},{9,10},{10,9},{11,... | collective-permute-start | bytes 2261000 | tf_op jit(solution)/shard_map/ppermute | solution.py:495
  61.2 7.2 %motion_from3.1.refs_5_.motion = bf16[4,52,64,128]{3,2,1,0:T(8,128)(2,1)} custom-call(s32[4,6]{1,0:T(4,128)} %stack.3.meta.refs_0_, bf16[2,2,48,64,128]{4,3,2,1,0:T(8,128)(2,1)} %own.3, bf16[2,2,48,64,128]{4,3,2,1,0:T(8,128)(2,1)} %collective-permute-done.near.refs_2_, ...), custom_call_target="tpu_custom_call", output_to_operand_aliasing={{}: (7, {})} | custom-call | flops 2013265920 | bytes 2359296 | tf_op jit(solution)/shard_map/motion_from3/pallas_call | solution.py:210
  68.4 3.1 %collective-permute-done.2.refs_3_.refs_4_.far_top = bf16[2,25,64,128]{3,2,1,0:T(8,128)(2,1)} collective-permute-done((bf16[2,25,64,128]{3,2,1,0:T(8,128)(2,1)}, bf16[2,25,64,128]{3,2,1,0:T(8,128)(2,1)}, u32[]{:S(2)}, u32[]{:S(2)}) %collective-permute-start.2) | collective-permute-done | bytes 819232 | tf_op jit(solution)/shard_map/ppermute | solution.py:495
  71.5 12.0 %gru_band0.1 = (bf16[4,48,64,128]{3,2,1,0:T(8,128)(2,1)}, bf16[2,24,64,128]{3,2,1,0:T(8,128)(2,1)}, bf16[2,24,64,128]{3,2,1,0:T(8,128)(2,1)}, bf16[2,12,64,128]{3,2,1,0:T(8,128)(2,1)}, bf16[2,12,64,128]{3,2,1,0:T(8,128)(2,1)}) custom-call(s32[4,6]{1,0:T(4,128)} %stack.3.meta.refs_0_, bf16[2,2,48,64,128]{4,3,2,1,0:T(8,128)(2,1)} %own.3, ...), custom_call_target="tpu_custom_call" | custom-call | flops 1638400 | bytes 1638400 | tf_op jit(solution)/shard_map/gru_band0/pallas_call | solution.py:366
  83.5 4.6 %collective-permute-start.4 = (bf16[2,24,64,128]{3,2,1,0:T(8,128)(2,1)}, bf16[2,24,64,128]{3,2,1,0:T(8,128)(2,1)S(1)}, u32[]{:S(2)}, u32[]{:S(2)}) collective-permute-start(bf16[2,24,64,128]{3,2,1,0:T(8,128)(2,1)} %get-tuple-element.31), channel_id=1, source_target_pairs={{1,2},{2,1},{3,4},{4,3},{5,6},{6,5},{7,8},{8,7},{9,10},{10,9},{11,... | collective-permute-start | bytes 2359304 | tf_op jit(solution)/shard_map/ppermute | solution.py:495
  88.1 12.1 %gru_band1.1 = (bf16[4,48,64,128]{3,2,1,0:T(8,128)(2,1)}, bf16[2,24,64,128]{3,2,1,0:T(8,128)(2,1)}, bf16[2,24,64,128]{3,2,1,0:T(8,128)(2,1)}, bf16[2,12,64,128]{3,2,1,0:T(8,128)(2,1)}, bf16[2,12,64,128]{3,2,1,0:T(8,128)(2,1)}) custom-call(s32[4,6]{1,0:T(4,128)} %stack.3.meta.refs_0_, ...), custom_call_target="tpu_custom_call", output_to_operand_aliasing={{0}: (10, {})} | custom-call | flops 1638400 | bytes 1638400 | tf_op jit(solution)/shard_map/gru_band1/pallas_call | solution.py:366
  100.3 4.4 %collective-permute-start.7 = (bf16[2,24,64,128]{3,2,1,0:T(8,128)(2,1)}, bf16[2,24,64,128]{3,2,1,0:T(8,128)(2,1)}, u32[]{:S(2)}, u32[]{:S(2)}) collective-permute-start(bf16[2,24,64,128]{3,2,1,0:T(8,128)(2,1)} %get-tuple-element.37), channel_id=1, source_target_pairs={{1,2},{2,1},{3,4},{4,3},{5,6},{6,5},{7,8},{8,7},{9,10},{10,9},{11,... | collective-permute-start | bytes 2359304 | tf_op jit(solution)/shard_map/ppermute | solution.py:495
  104.7 0.8 collective-permute-done.4.refs_1_
  105.5 0.5 collective-permute-start.6
  106.7 0.5 collective-permute-done.5.refs_2_
  107.2 1.1 collective-permute-done.6.refs_3_
  108.4 2.9 %aggregate_from0.1.refs_9_ = bf16[2,23,64,128]{3,2,1,0:T(8,128)(2,1)S(1)} custom-call(f32[2]{0:T(128)S(1)} %broadcast_maximum_fusion.counts, bf16[2,24,64,128]{3,2,1,0:T(8,128)(2,1)S(1)} %copy-done.1, bf16[2,24,64,128]{3,2,1,0:T(8,128)(2,1)S(1)} %collective-permute-done.4.refs_1_, bf16[2,12,64,128]{3,2,1,0:T(8,128)(2,1)S(1)} %collective-permute-done.5.refs_2_, ...), custom_call_target="tpu_custom_call" | custom-call | flops 868220928 | bytes 3145728 | tf_op jit(solution)/shard_map/aggregate_from0/pallas_call | solution.py:460
  111.3 3.4 %collective-permute-done.7.refs_5_ = bf16[2,24,64,128]{3,2,1,0:T(8,128)(2,1)} collective-permute-done((bf16[2,24,64,128]{3,2,1,0:T(8,128)(2,1)}, bf16[2,24,64,128]{3,2,1,0:T(8,128)(2,1)}, u32[]{:S(2)}, u32[]{:S(2)}) %collective-permute-start.7) | collective-permute-done | bytes 786464 | tf_op jit(solution)/shard_map/ppermute | solution.py:495
  114.7 5.0 %aggregate_from23.1 = bf16[2,48,64,128]{3,2,1,0:T(8,128)(2,1)} custom-call(f32[2]{0:T(128)S(1)} %broadcast_maximum_fusion.counts, bf16[2,24,64,128]{3,2,1,0:T(8,128)(2,1)S(1)} %copy-done.1, bf16[2,24,64,128]{3,2,1,0:T(8,128)(2,1)S(1)} %collective-permute-done.4.refs_1_, bf16[2,12,64,128]{3,2,1,0:T(8,128)(2,1)S(1)} %collective-permute-done.5.refs_2_, ...), custom_call_target="tpu_custom_call" | custom-call | flops 943718400 | bytes 3407872 | tf_op jit(solution)/shard_map/aggregate_from23/pallas_call | solution.py:460
  (39 shorter events, 1.7 us)
Async XLA Ops:
  0.6 6.5 %copy-start = (bf16[81,128]{1,0:T(8,128)(2,1)S(1)}, bf16[81,128]{1,0:T(8,128)(2,1)}, u32[]{:S(2)}) copy-start(bf16[81,128]{1,0:T(8,128)(2,1)} %param.19) | copy-start | bytes 62212
  0.6 6.5 %copy-start.5 = (bf16[5,128,81]{1,2,0:T(8,128)(2,1)S(1)}, bf16[5,128,81]{1,2,0:T(8,128)(2,1)}, u32[]{:S(2)}) copy-start(bf16[5,128,81]{1,2,0:T(8,128)(2,1)} %constant.48.clone) | copy-start | bytes 311044
  0.7 7.6 %copy-start.4 = (bf16[5,128,81]{1,2,0:T(8,128)(2,1)S(1)}, bf16[5,128,81]{1,2,0:T(8,128)(2,1)}, u32[]{:S(2)}) copy-start(bf16[5,128,81]{1,2,0:T(8,128)(2,1)} %constant.49.clone) | copy-start | bytes 311044
  0.7 6.3 %copy-start.7 = (s32[64,2]{0,1:T(2,128)S(1)}, s32[64,2]{0,1:T(2,128)}, u32[]{:S(2)}) copy-start(s32[64,2]{0,1:T(2,128)} %param.17) | copy-start | bytes 1540
  0.7 6.8 %copy-start.6 = (s32[4,2]{0,1:T(2,128)S(1)}, s32[4,2]{0,1:T(2,128)}, u32[]{:S(2)}) copy-start(s32[4,2]{0,1:T(2,128)} %param.18) | copy-start | bytes 100
  2.3 7.1 %collective-permute-start = (bf16[2,2,48,64,128]{4,3,2,1,0:T(8,128)(2,1)}, bf16[2,2,48,64,128]{4,3,2,1,0:T(8,128)(2,1)}, u32[]{:S(2)}, u32[]{:S(2)}) collective-permute-start(bf16[2,2,48,64,128]{4,3,2,1,0:T(8,128)(2,1)} %own.3), channel_id=1, source_target_pairs={{0,1},{1,0},{2,3},{3,2},{4,5},{5,4},{6,7},{7,6},{8,9},{9,8},{10,11... | collective-permute-start | bytes 9437192 | tf_op jit(solution)/shard_map/ppermute | solution.py:498
  2.4 38.7 %collective-permute-start.1 = (bf16[2,48,64,128]{3,2,1,0:T(8,128)(2,1)S(1)}, bf16[2,48,64,128]{3,2,1,0:T(8,128)(2,1)}, u32[]{:S(2)}, u32[]{:S(2)}) collective-permute-start(bf16[2,48,64,128]{3,2,1,0:T(8,128)(2,1)S(1)} %slice_bitcast_fusion), channel_id=1, source_target_pairs={{1,2},{2,1},{3,4},{4,3},{5,6},{6,5},{7,8},{8,7},{9,10},{10,9},{11,... | collective-permute-start | bytes 4718600 | tf_op jit(solution)/shard_map/ppermute | solution.py:495
  54.8 16.7 %collective-permute-start.2 = (bf16[2,25,64,128]{3,2,1,0:T(8,128)(2,1)}, bf16[2,25,64,128]{3,2,1,0:T(8,128)(2,1)}, u32[]{:S(2)}, u32[]{:S(2)}) collective-permute-start(bf16[2,25,64,128]{3,2,1,0:T(8,128)(2,1)} %slice_bitcast_fusion.1), channel_id=1, source_target_pairs={{1,2},{2,1},{3,4},{4,3},{5,6},{6,5},{7,8},{8,7},{9,10},{10,9},{11,... | collective-permute-start | bytes 2457608 | tf_op jit(solution)/shard_map/ppermute | solution.py:495
  59.3 28.7 %collective-permute-start.3 = (bf16[2,23,64,128]{3,2,1,0:T(8,128)(2,1)}, bf16[2,23,64,128]{3,2,1,0:T(8,128)(2,1)}, u32[]{:S(2)}, u32[]{:S(2)}) collective-permute-start(bf16[2,23,64,128]{3,2,1,0:T(8,128)(2,1)} %slice_bitcast_fusion.2), channel_id=1, source_target_pairs={{1,2},{2,1},{3,4},{4,3},{5,6},{6,5},{7,8},{8,7},{9,10},{10,9},{11,... | collective-permute-start | bytes 2261000 | tf_op jit(solution)/shard_map/ppermute | solution.py:495
  83.5 22.0 %collective-permute-start.4 = (bf16[2,24,64,128]{3,2,1,0:T(8,128)(2,1)}, bf16[2,24,64,128]{3,2,1,0:T(8,128)(2,1)S(1)}, u32[]{:S(2)}, u32[]{:S(2)}) collective-permute-start(bf16[2,24,64,128]{3,2,1,0:T(8,128)(2,1)} %get-tuple-element.31), channel_id=1, source_target_pairs={{1,2},{2,1},{3,4},{4,3},{5,6},{6,5},{7,8},{8,7},{9,10},{10,9},{11,... | collective-permute-start | bytes 2359304 | tf_op jit(solution)/shard_map/ppermute | solution.py:495
  88.1 17.5 %copy-start.9 = (bf16[2,12,64,128]{3,2,1,0:T(8,128)(2,1)S(1)}, bf16[2,12,64,128]{3,2,1,0:T(8,128)(2,1)}, u32[]{:S(2)}) copy-start(bf16[2,12,64,128]{3,2,1,0:T(8,128)(2,1)} %get-tuple-element.34) | copy-start | bytes 1179652
  88.1 17.5 %copy-start.8 = (bf16[2,12,64,128]{3,2,1,0:T(8,128)(2,1)S(1)}, bf16[2,12,64,128]{3,2,1,0:T(8,128)(2,1)}, u32[]{:S(2)}) copy-start(bf16[2,12,64,128]{3,2,1,0:T(8,128)(2,1)} %get-tuple-element.35) | copy-start | bytes 1179652
  88.1 20.3 %copy-start.1 = (bf16[2,24,64,128]{3,2,1,0:T(8,128)(2,1)S(1)}, bf16[2,24,64,128]{3,2,1,0:T(8,128)(2,1)}, u32[]{:S(2)}) copy-start(bf16[2,24,64,128]{3,2,1,0:T(8,128)(2,1)} %get-tuple-element.30.refs_0_) | copy-start | bytes 2359300
  88.1 20.3 %copy-start.2 = (bf16[1152,128]{1,0:T(8,128)(2,1)S(1)}, bf16[1152,128]{1,0:T(8,128)(2,1)}, u32[]{:S(2)}) copy-start(bf16[1152,128]{1,0:T(8,128)(2,1)} %refs_8_.3) | copy-start | bytes 884740
  100.3 14.4 %copy-start.3 = (bf16[2,24,64,128]{3,2,1,0:T(8,128)(2,1)S(1)}, bf16[2,24,64,128]{3,2,1,0:T(8,128)(2,1)}, u32[]{:S(2)}) copy-start(bf16[2,24,64,128]{3,2,1,0:T(8,128)(2,1)} %get-tuple-element.36.refs_4_) | copy-start | bytes 2359300
  100.3 14.4 %collective-permute-start.7 = (bf16[2,24,64,128]{3,2,1,0:T(8,128)(2,1)}, bf16[2,24,64,128]{3,2,1,0:T(8,128)(2,1)}, u32[]{:S(2)}, u32[]{:S(2)}) collective-permute-start(bf16[2,24,64,128]{3,2,1,0:T(8,128)(2,1)} %get-tuple-element.37), channel_id=1, source_target_pairs={{1,2},{2,1},{3,4},{4,3},{5,6},{6,5},{7,8},{8,7},{9,10},{10,9},{11,... | collective-permute-start | bytes 2359304 | tf_op jit(solution)/shard_map/ppermute | solution.py:495
  105.5 1.7 %collective-permute-start.5 = (bf16[2,12,64,128]{3,2,1,0:T(8,128)(2,1)S(1)}, bf16[2,12,64,128]{3,2,1,0:T(8,128)(2,1)S(1)}, u32[]{:S(2)}, u32[]{:S(2)}) collective-permute-start(bf16[2,12,64,128]{3,2,1,0:T(8,128)(2,1)S(1)} %copy-done.9), channel_id=1, source_target_pairs={{0,1},{1,0},{2,3},{3,2},{4,5},{5,4},{6,7},{7,6},{8,9},{9,8},{10,11... | collective-permute-start | bytes 1179656 | tf_op jit(solution)/shard_map/ppermute | solution.py:498
  105.5 2.8 %collective-permute-start.6 = (bf16[2,12,64,128]{3,2,1,0:T(8,128)(2,1)S(1)}, bf16[2,12,64,128]{3,2,1,0:T(8,128)(2,1)S(1)}, u32[]{:S(2)}, u32[]{:S(2)}) collective-permute-start(bf16[2,12,64,128]{3,2,1,0:T(8,128)(2,1)S(1)} %copy-done.8), channel_id=1, source_target_pairs={{0,1},{1,0},{2,3},{3,2},{4,5},{5,4},{6,7},{7,6},{8,9},{9,8},{10,11... | collective-permute-start | bytes 1179656 | tf_op jit(solution)/shard_map/ppermute | solution.py:498
  106.0 8.6 %collective-permute-start.8 = (bf16[2,12,64,128]{3,2,1,0:T(8,128)(2,1)}, bf16[2,12,64,128]{3,2,1,0:T(8,128)(2,1)S(1)}, u32[]{:S(2)}, u32[]{:S(2)}) collective-permute-start(bf16[2,12,64,128]{3,2,1,0:T(8,128)(2,1)} %get-tuple-element.40), channel_id=1, source_target_pairs={{0,1},{1,0},{2,3},{3,2},{4,5},{5,4},{6,7},{7,6},{8,9},{9,8},{10,11... | collective-permute-start | bytes 1179656 | tf_op jit(solution)/shard_map/ppermute | solution.py:498
  106.1 8.6 %collective-permute-start.9 = (bf16[2,12,64,128]{3,2,1,0:T(8,128)(2,1)}, bf16[2,12,64,128]{3,2,1,0:T(8,128)(2,1)S(1)}, u32[]{:S(2)}, u32[]{:S(2)}) collective-permute-start(bf16[2,12,64,128]{3,2,1,0:T(8,128)(2,1)} %get-tuple-element.41), channel_id=1, source_target_pairs={{0,1},{1,0},{2,3},{3,2},{4,5},{5,4},{6,7},{7,6},{8,9},{9,8},{10,11... | collective-permute-start | bytes 1179656 | tf_op jit(solution)/shard_map/ppermute | solution.py:498

commit v8 on v7

--- a/solution.py
+++ b/solution.py
@@ -267,7 +267,7 @@
     edges = pl.num_programs(0)
     frames = own.shape[0]
     height, width, chans = own.shape[2:]
-    slot = edge
+    slot = lax.rem(edge, 2)
     top = max(first - 1, 0)
     end = min(last + 1, height)
     rows = end - top
@@ -299,12 +299,15 @@
 
     @pl.when(edge == 0)
     def _():
-        for e in range(state.shape[0]):
-            start(e, e)
+        start(edge, slot)
         edge_row = jnp.zeros((1,) + columns.shape[1:], BF16)
         columns[0:1] = edge_row
         columns[rows + 1 :] = edge_row
         totals[...] = jnp.zeros(totals.shape, F32)
+
+    @pl.when(edge + 1 < edges)
+    def _():
+        start(edge + 1, 1 - slot)
 
     finish(slot)
 
@@ -377,15 +380,15 @@
                 piece_spec,
             ],
             scratch_shapes=[
-                pltpu.VMEM((edges, rows, width, chans), BF16),
-                pltpu.VMEM((edges, rows, width, chans), BF16),
-                pltpu.VMEM((edges, rows, width, 2 * chans), BF16),
-                pltpu.VMEM((edges, rows, width, chans), BF16),
+                pltpu.VMEM((2, rows, width, chans), BF16),
+                pltpu.VMEM((2, rows, width, chans), BF16),
+                pltpu.VMEM((2, rows, width, 2 * chans), BF16),
+                pltpu.VMEM((2, rows, width, chans), BF16),
                 pltpu.VMEM((rows + 2, width, 3 * chans), BF16),
                 pltpu.VMEM((rows, width, chans), F32),
                 pltpu.VMEM((rows, width, chans), F32),
                 pltpu.VMEM((3 * frames, size, width, chans), F32),
-                pltpu.SemaphoreType.DMA((5, edges)),
+                pltpu.SemaphoreType.DMA((5, 2)),
             ],
         ),
         out_shape=[
@@ -425,7 +428,7 @@
             put_columns(columns, at, mean)
             at += piece.shape[1]
             top += piece.shape[1]
-    step = 8
+    step = 8 if (last - first) % 5 else 5
     base = 0
     if len(rest) == 3:
         out_ref[0, :first] = rest[0][0]

time: 120 us -> 120 us (level)
  transfers between devices with their start and end apart: 10 -> 10, of which waited for: 6 -> 7; matrix products, arithmetic and copies ran while one was open for 6% -> 6% of each run, Pallas kernels for 38% -> 38%
where the time goes in v8:
time: 120 us; the launch traced here: 119 us
  Pallas kernels  63.8 us (53%)
  waiting for transfers between devices  25.2 us (21%)
  starting transfers between devices  21.1 us (18%)
  local copies, waits for them, and re-layouts  6.82 us (6%)
    pallas_call x2, Pallas kernels, gru_of(): pl.pallas_call(kernel, grid_spec=pltpu.PrefetchScalarGridSpec(num_scalar_...  23.7 us
    ppermute x5, waiting for transfers between devices, far_swap(): return lax.ppermute(block, 'rows', far_route)  23.6 us
    pallas_call x2, Pallas kernels, motion_of(): pl.pallas_call(kernel, grid_spec=pltpu.PrefetchScalarGridSpec(num_scalar_...  20.9 us
    ppermute x5, starting transfers between devices, far_swap(): return lax.ppermute(block, 'rows', far_route)  19.9 us
    pallas_call x1, Pallas kernels, gates_of(): pl.pallas_call(gates_kernel, grid=(edges,), in_specs=[pl.BlockSpec((1, he...  11.5 us
    pallas_call x2, Pallas kernels, aggregate_of(): pl.pallas_call(functools.partial(aggregate_kernel, pieces, first, last),...  7.78 us
  transfers between devices with their start and end apart: 10, of which 7 were waited for; matrix products, arithmetic and copies ran while one was open for 6% of the time, Pallas kernels for 38%

profile of v8, /device:TPU:1, one launch (start us, length us, event | category | flops | bytes accessed | tf_op | source)
XLA Modules:
  0.0 119.3 jit_solution(7229712535043032339)
XLA Ops:
  0.7 1.6 %slice_bitcast_fusion = bf16[2,48,64,128]{3,2,1,0:T(8,128)(2,1)S(1)} fusion(bf16[2,2,48,64,128]{4,3,2,1,0:T(8,128)(2,1)} %own.3), kind=kLoop, calls=%fused_computation | loop fusion | bytes 3145728 | tf_op jit(solution)/shard_map/squeeze | solution.py:503
  2.4 4.5 %collective-permute-start.1 = (bf16[2,48,64,128]{3,2,1,0:T(8,128)(2,1)S(1)}, bf16[2,48,64,128]{3,2,1,0:T(8,128)(2,1)}, u32[]{:S(2)}, u32[]{:S(2)}) collective-permute-start(bf16[2,48,64,128]{3,2,1,0:T(8,128)(2,1)S(1)} %slice_bitcast_fusion), channel_id=1, source_target_pairs={{1,2},{2,1},{3,4},{4,3},{5,6},{6,5},{7,8},{8,7},{9,10},{10,9},{11,... | collective-permute-start | bytes 4718600 | tf_op jit(solution)/shard_map/ppermute | solution.py:498
  7.6 0.7 stack.3.meta.refs_0_
  8.5 0.9 pad_maximum_fusion.base_ref.refs_6_
  9.4 2.0 %slice_bitcast_fusion.2 = bf16[2,23,64,128]{3,2,1,0:T(8,128)(2,1)} fusion(bf16[2,2,48,64,128]{4,3,2,1,0:T(8,128)(2,1)} %own.3), kind=kLoop, calls=%fused_computation.2 | loop fusion | bytes 1507328 | tf_op jit(solution)/shard_map/squeeze | solution.py:522
  11.4 2.1 %slice_bitcast_fusion.1 = bf16[2,25,64,128]{3,2,1,0:T(8,128)(2,1)} fusion(bf16[2,2,48,64,128]{4,3,2,1,0:T(8,128)(2,1)} %own.3), kind=kLoop, calls=%fused_computation.1 | loop fusion | bytes 1638400 | tf_op jit(solution)/shard_map/squeeze | solution.py:522
  13.5 11.5 %gates.1.refs_6_ = bf16[4,48,64,256]{3,2,1,0:T(8,128)(2,1)} custom-call(bf16[4,48,64,128]{3,2,1,0:T(8,128)(2,1)} %state.1, bf16[1152,256]{1,0:T(8,128)(2,1)} %weights_ref), custom_call_target="tpu_custom_call" | custom-call | flops 7247757312 | bytes 9437184 | tf_op jit(solution)/shard_map/gates/pallas_call | solution.py:84
  25.0 16.2 %collective-permute-done.1.far.refs_3_ = bf16[2,48,64,128]{3,2,1,0:T(8,128)(2,1)} collective-permute-done((bf16[2,48,64,128]{3,2,1,0:T(8,128)(2,1)S(1)}, bf16[2,48,64,128]{3,2,1,0:T(8,128)(2,1)}, u32[]{:S(2)}, u32[]{:S(2)}) %collective-permute-start.1) | collective-permute-done | bytes 1572896 | tf_op jit(solution)/shard_map/ppermute | solution.py:498
  41.1 13.7 %motion_from0.1.refs_7_ = bf16[4,52,64,128]{3,2,1,0:T(8,128)(2,1)} custom-call(s32[4,6]{1,0:T(4,128)} %stack.3.meta.refs_0_, bf16[2,2,48,64,128]{4,3,2,1,0:T(8,128)(2,1)} %own.3, bf16[2,2,48,64,128]{4,3,2,1,0:T(8,128)(2,1)} %collective-permute-done.near.refs_2_, bf16[2,48,64,128]{3,2,1,0:T(8,128)(2,1)} %collective-permute-done.1.far.refs_3_, ...), custom_call_target="tpu_custom_call" | custom-call | flops 6039797760 | bytes 7077888 | tf_op jit(solution)/shard_map/motion_from0/pallas_call | solution.py:210
  54.9 4.4 %collective-permute-start.2 = (bf16[2,25,64,128]{3,2,1,0:T(8,128)(2,1)}, bf16[2,25,64,128]{3,2,1,0:T(8,128)(2,1)}, u32[]{:S(2)}, u32[]{:S(2)}) collective-permute-start(bf16[2,25,64,128]{3,2,1,0:T(8,128)(2,1)} %slice_bitcast_fusion.1), channel_id=1, source_target_pairs={{1,2},{2,1},{3,4},{4,3},{5,6},{6,5},{7,8},{8,7},{9,10},{10,9},{11,... | collective-permute-start | bytes 2457608 | tf_op jit(solution)/shard_map/ppermute | solution.py:498
  59.3 1.9 %collective-permute-start.3 = (bf16[2,23,64,128]{3,2,1,0:T(8,128)(2,1)}, bf16[2,23,64,128]{3,2,1,0:T(8,128)(2,1)}, u32[]{:S(2)}, u32[]{:S(2)}) collective-permute-start(bf16[2,23,64,128]{3,2,1,0:T(8,128)(2,1)} %slice_bitcast_fusion.2), channel_id=1, source_target_pairs={{1,2},{2,1},{3,4},{4,3},{5,6},{6,5},{7,8},{8,7},{9,10},{10,9},{11,... | collective-permute-start | bytes 2261000 | tf_op jit(solution)/shard_map/ppermute | solution.py:498
  61.2 7.2 %motion_from3.1.refs_5_.motion = bf16[4,52,64,128]{3,2,1,0:T(8,128)(2,1)} custom-call(s32[4,6]{1,0:T(4,128)} %stack.3.meta.refs_0_, bf16[2,2,48,64,128]{4,3,2,1,0:T(8,128)(2,1)} %own.3, bf16[2,2,48,64,128]{4,3,2,1,0:T(8,128)(2,1)} %collective-permute-done.near.refs_2_, ...), custom_call_target="tpu_custom_call", output_to_operand_aliasing={{}: (7, {})} | custom-call | flops 2013265920 | bytes 2359296 | tf_op jit(solution)/shard_map/motion_from3/pallas_call | solution.py:210
  68.4 3.1 %collective-permute-done.2.refs_3_.refs_4_.far_top = bf16[2,25,64,128]{3,2,1,0:T(8,128)(2,1)} collective-permute-done((bf16[2,25,64,128]{3,2,1,0:T(8,128)(2,1)}, bf16[2,25,64,128]{3,2,1,0:T(8,128)(2,1)}, u32[]{:S(2)}, u32[]{:S(2)}) %collective-permute-start.2) | collective-permute-done | bytes 819232 | tf_op jit(solution)/shard_map/ppermute | solution.py:498
  71.4 11.8 %gru_band0.1 = (bf16[4,48,64,128]{3,2,1,0:T(8,128)(2,1)}, bf16[2,24,64,128]{3,2,1,0:T(8,128)(2,1)}, bf16[2,24,64,128]{3,2,1,0:T(8,128)(2,1)}, bf16[2,12,64,128]{3,2,1,0:T(8,128)(2,1)}, bf16[2,12,64,128]{3,2,1,0:T(8,128)(2,1)}) custom-call(s32[4,6]{1,0:T(4,128)} %stack.3.meta.refs_0_, bf16[2,2,48,64,128]{4,3,2,1,0:T(8,128)(2,1)} %own.3, ...), custom_call_target="tpu_custom_call" | custom-call | flops 1638400 | bytes 1638400 | tf_op jit(solution)/shard_map/gru_band0/pallas_call | solution.py:369
  83.2 4.6 %collective-permute-start.4 = (bf16[2,24,64,128]{3,2,1,0:T(8,128)(2,1)}, bf16[2,24,64,128]{3,2,1,0:T(8,128)(2,1)S(1)}, u32[]{:S(2)}, u32[]{:S(2)}) collective-permute-start(bf16[2,24,64,128]{3,2,1,0:T(8,128)(2,1)} %get-tuple-element.31), channel_id=1, source_target_pairs={{1,2},{2,1},{3,4},{4,3},{5,6},{6,5},{7,8},{8,7},{9,10},{10,9},{11,... | collective-permute-start | bytes 2359304 | tf_op jit(solution)/shard_map/ppermute | solution.py:498
  87.9 11.9 %gru_band1.1 = (bf16[4,48,64,128]{3,2,1,0:T(8,128)(2,1)}, bf16[2,24,64,128]{3,2,1,0:T(8,128)(2,1)}, bf16[2,24,64,128]{3,2,1,0:T(8,128)(2,1)}, bf16[2,12,64,128]{3,2,1,0:T(8,128)(2,1)}, bf16[2,12,64,128]{3,2,1,0:T(8,128)(2,1)}) custom-call(s32[4,6]{1,0:T(4,128)} %stack.3.meta.refs_0_, ...), custom_call_target="tpu_custom_call", output_to_operand_aliasing={{0}: (10, {})} | custom-call | flops 1638400 | bytes 1638400 | tf_op jit(solution)/shard_map/gru_band1/pallas_call | solution.py:369
  99.9 4.5 %collective-permute-start.7 = (bf16[2,24,64,128]{3,2,1,0:T(8,128)(2,1)}, bf16[2,24,64,128]{3,2,1,0:T(8,128)(2,1)}, u32[]{:S(2)}, u32[]{:S(2)}) collective-permute-start(bf16[2,24,64,128]{3,2,1,0:T(8,128)(2,1)} %get-tuple-element.37), channel_id=1, source_target_pairs={{1,2},{2,1},{3,4},{4,3},{5,6},{6,5},{7,8},{8,7},{9,10},{10,9},{11,... | collective-permute-start | bytes 2359304 | tf_op jit(solution)/shard_map/ppermute | solution.py:498
  104.8 0.5 collective-permute-start.6
  105.4 0.4 collective-permute-start.9
  106.0 0.5 collective-permute-done.5.refs_2_
  106.5 1.1 collective-permute-done.6.refs_3_
  107.7 2.9 %aggregate_from0.1.refs_9_ = bf16[2,23,64,128]{3,2,1,0:T(8,128)(2,1)S(1)} custom-call(f32[2]{0:T(128)S(1)} %broadcast_maximum_fusion.counts, bf16[2,24,64,128]{3,2,1,0:T(8,128)(2,1)S(1)} %copy-done.1, bf16[2,24,64,128]{3,2,1,0:T(8,128)(2,1)S(1)} %collective-permute-done.4.refs_1_, bf16[2,12,64,128]{3,2,1,0:T(8,128)(2,1)S(1)} %collective-permute-done.5.refs_2_, ...), custom_call_target="tpu_custom_call" | custom-call | flops 868220928 | bytes 3145728 | tf_op jit(solution)/shard_map/aggregate_from0/pallas_call | solution.py:463
  110.6 3.9 %collective-permute-done.7.refs_5_ = bf16[2,24,64,128]{3,2,1,0:T(8,128)(2,1)} collective-permute-done((bf16[2,24,64,128]{3,2,1,0:T(8,128)(2,1)}, bf16[2,24,64,128]{3,2,1,0:T(8,128)(2,1)}, u32[]{:S(2)}, u32[]{:S(2)}) %collective-permute-start.7) | collective-permute-done | bytes 786464 | tf_op jit(solution)/shard_map/ppermute | solution.py:498
  114.4 4.9 %aggregate_from23.1 = bf16[2,48,64,128]{3,2,1,0:T(8,128)(2,1)} custom-call(f32[2]{0:T(128)S(1)} %broadcast_maximum_fusion.counts, bf16[2,24,64,128]{3,2,1,0:T(8,128)(2,1)S(1)} %copy-done.1, bf16[2,24,64,128]{3,2,1,0:T(8,128)(2,1)S(1)} %collective-permute-done.4.refs_1_, bf16[2,12,64,128]{3,2,1,0:T(8,128)(2,1)S(1)} %collective-permute-done.5.refs_2_, ...), custom_call_target="tpu_custom_call" | custom-call | flops 943718400 | bytes 3407872 | tf_op jit(solution)/shard_map/aggregate_from23/pallas_call | solution.py:463
  (39 shorter events, 1.7 us)
Async XLA Ops:
  0.6 6.5 %copy-start = (bf16[81,128]{1,0:T(8,128)(2,1)S(1)}, bf16[81,128]{1,0:T(8,128)(2,1)}, u32[]{:S(2)}) copy-start(bf16[81,128]{1,0:T(8,128)(2,1)} %param.19) | copy-start | bytes 62212
  0.6 6.5 %copy-start.5 = (bf16[5,128,81]{1,2,0:T(8,128)(2,1)S(1)}, bf16[5,128,81]{1,2,0:T(8,128)(2,1)}, u32[]{:S(2)}) copy-start(bf16[5,128,81]{1,2,0:T(8,128)(2,1)} %constant.48.clone) | copy-start | bytes 311044
  0.7 7.6 %copy-start.4 = (bf16[5,128,81]{1,2,0:T(8,128)(2,1)S(1)}, bf16[5,128,81]{1,2,0:T(8,128)(2,1)}, u32[]{:S(2)}) copy-start(bf16[5,128,81]{1,2,0:T(8,128)(2,1)} %constant.49.clone) | copy-start | bytes 311044
  0.7 6.3 %copy-start.7 = (s32[64,2]{0,1:T(2,128)S(1)}, s32[64,2]{0,1:T(2,128)}, u32[]{:S(2)}) copy-start(s32[64,2]{0,1:T(2,128)} %param.17) | copy-start | bytes 1540
  0.7 6.8 %copy-start.6 = (s32[4,2]{0,1:T(2,128)S(1)}, s32[4,2]{0,1:T(2,128)}, u32[]{:S(2)}) copy-start(s32[4,2]{0,1:T(2,128)} %param.18) | copy-start | bytes 100
  2.3 7.1 %collective-permute-start = (bf16[2,2,48,64,128]{4,3,2,1,0:T(8,128)(2,1)}, bf16[2,2,48,64,128]{4,3,2,1,0:T(8,128)(2,1)}, u32[]{:S(2)}, u32[]{:S(2)}) collective-permute-start(bf16[2,2,48,64,128]{4,3,2,1,0:T(8,128)(2,1)} %own.3), channel_id=1, source_target_pairs={{0,1},{1,0},{2,3},{3,2},{4,5},{5,4},{6,7},{7,6},{8,9},{9,8},{10,11... | collective-permute-start | bytes 9437192 | tf_op jit(solution)/shard_map/ppermute | solution.py:501
  2.4 38.7 %collective-permute-start.1 = (bf16[2,48,64,128]{3,2,1,0:T(8,128)(2,1)S(1)}, bf16[2,48,64,128]{3,2,1,0:T(8,128)(2,1)}, u32[]{:S(2)}, u32[]{:S(2)}) collective-permute-start(bf16[2,48,64,128]{3,2,1,0:T(8,128)(2,1)S(1)} %slice_bitcast_fusion), channel_id=1, source_target_pairs={{1,2},{2,1},{3,4},{4,3},{5,6},{6,5},{7,8},{8,7},{9,10},{10,9},{11,... | collective-permute-start | bytes 4718600 | tf_op jit(solution)/shard_map/ppermute | solution.py:498
  54.9 16.6 %collective-permute-start.2 = (bf16[2,25,64,128]{3,2,1,0:T(8,128)(2,1)}, bf16[2,25,64,128]{3,2,1,0:T(8,128)(2,1)}, u32[]{:S(2)}, u32[]{:S(2)}) collective-permute-start(bf16[2,25,64,128]{3,2,1,0:T(8,128)(2,1)} %slice_bitcast_fusion.1), channel_id=1, source_target_pairs={{1,2},{2,1},{3,4},{4,3},{5,6},{6,5},{7,8},{8,7},{9,10},{10,9},{11,... | collective-permute-start | bytes 2457608 | tf_op jit(solution)/shard_map/ppermute | solution.py:498
  59.3 28.7 %collective-permute-start.3 = (bf16[2,23,64,128]{3,2,1,0:T(8,128)(2,1)}, bf16[2,23,64,128]{3,2,1,0:T(8,128)(2,1)}, u32[]{:S(2)}, u32[]{:S(2)}) collective-permute-start(bf16[2,23,64,128]{3,2,1,0:T(8,128)(2,1)} %slice_bitcast_fusion.2), channel_id=1, source_target_pairs={{1,2},{2,1},{3,4},{4,3},{5,6},{6,5},{7,8},{8,7},{9,10},{10,9},{11,... | collective-permute-start | bytes 2261000 | tf_op jit(solution)/shard_map/ppermute | solution.py:498
  83.2 21.6 %collective-permute-start.4 = (bf16[2,24,64,128]{3,2,1,0:T(8,128)(2,1)}, bf16[2,24,64,128]{3,2,1,0:T(8,128)(2,1)S(1)}, u32[]{:S(2)}, u32[]{:S(2)}) collective-permute-start(bf16[2,24,64,128]{3,2,1,0:T(8,128)(2,1)} %get-tuple-element.31), channel_id=1, source_target_pairs={{1,2},{2,1},{3,4},{4,3},{5,6},{6,5},{7,8},{8,7},{9,10},{10,9},{11,... | collective-permute-start | bytes 2359304 | tf_op jit(solution)/shard_map/ppermute | solution.py:498
  87.9 16.9 %copy-start.9 = (bf16[2,12,64,128]{3,2,1,0:T(8,128)(2,1)S(1)}, bf16[2,12,64,128]{3,2,1,0:T(8,128)(2,1)}, u32[]{:S(2)}) copy-start(bf16[2,12,64,128]{3,2,1,0:T(8,128)(2,1)} %get-tuple-element.34) | copy-start | bytes 1179652
  87.9 16.9 %copy-start.8 = (bf16[2,12,64,128]{3,2,1,0:T(8,128)(2,1)S(1)}, bf16[2,12,64,128]{3,2,1,0:T(8,128)(2,1)}, u32[]{:S(2)}) copy-start(bf16[2,12,64,128]{3,2,1,0:T(8,128)(2,1)} %get-tuple-element.35) | copy-start | bytes 1179652
  87.9 19.7 %copy-start.1 = (bf16[2,24,64,128]{3,2,1,0:T(8,128)(2,1)S(1)}, bf16[2,24,64,128]{3,2,1,0:T(8,128)(2,1)}, u32[]{:S(2)}) copy-start(bf16[2,24,64,128]{3,2,1,0:T(8,128)(2,1)} %get-tuple-element.30.refs_0_) | copy-start | bytes 2359300
  87.9 19.7 %copy-start.2 = (bf16[1152,128]{1,0:T(8,128)(2,1)S(1)}, bf16[1152,128]{1,0:T(8,128)(2,1)}, u32[]{:S(2)}) copy-start(bf16[1152,128]{1,0:T(8,128)(2,1)} %refs_8_.3) | copy-start | bytes 884740
  99.9 14.5 %copy-start.3 = (bf16[2,24,64,128]{3,2,1,0:T(8,128)(2,1)S(1)}, bf16[2,24,64,128]{3,2,1,0:T(8,128)(2,1)}, u32[]{:S(2)}) copy-start(bf16[2,24,64,128]{3,2,1,0:T(8,128)(2,1)} %get-tuple-element.36.refs_4_) | copy-start | bytes 2359300
  99.9 14.5 %collective-permute-start.7 = (bf16[2,24,64,128]{3,2,1,0:T(8,128)(2,1)}, bf16[2,24,64,128]{3,2,1,0:T(8,128)(2,1)}, u32[]{:S(2)}, u32[]{:S(2)}) collective-permute-start(bf16[2,24,64,128]{3,2,1,0:T(8,128)(2,1)} %get-tuple-element.37), channel_id=1, source_target_pairs={{1,2},{2,1},{3,4},{4,3},{5,6},{6,5},{7,8},{8,7},{9,10},{10,9},{11,... | collective-permute-start | bytes 2359304 | tf_op jit(solution)/shard_map/ppermute | solution.py:498
  104.8 1.7 %collective-permute-start.5 = (bf16[2,12,64,128]{3,2,1,0:T(8,128)(2,1)S(1)}, bf16[2,12,64,128]{3,2,1,0:T(8,128)(2,1)S(1)}, u32[]{:S(2)}, u32[]{:S(2)}) collective-permute-start(bf16[2,12,64,128]{3,2,1,0:T(8,128)(2,1)S(1)} %copy-done.9), channel_id=1, source_target_pairs={{0,1},{1,0},{2,3},{3,2},{4,5},{5,4},{6,7},{7,6},{8,9},{9,8},{10,11... | collective-permute-start | bytes 1179656 | tf_op jit(solution)/shard_map/ppermute | solution.py:501
  104.8 2.8 %collective-permute-start.6 = (bf16[2,12,64,128]{3,2,1,0:T(8,128)(2,1)S(1)}, bf16[2,12,64,128]{3,2,1,0:T(8,128)(2,1)S(1)}, u32[]{:S(2)}, u32[]{:S(2)}) collective-permute-start(bf16[2,12,64,128]{3,2,1,0:T(8,128)(2,1)S(1)} %copy-done.8), channel_id=1, source_target_pairs={{0,1},{1,0},{2,3},{3,2},{4,5},{5,4},{6,7},{7,6},{8,9},{9,8},{10,11... | collective-permute-start | bytes 1179656 | tf_op jit(solution)/shard_map/ppermute | solution.py:501
  105.3 9.1 %collective-permute-start.8 = (bf16[2,12,64,128]{3,2,1,0:T(8,128)(2,1)}, bf16[2,12,64,128]{3,2,1,0:T(8,128)(2,1)S(1)}, u32[]{:S(2)}, u32[]{:S(2)}) collective-permute-start(bf16[2,12,64,128]{3,2,1,0:T(8,128)(2,1)} %get-tuple-element.40), channel_id=1, source_target_pairs={{0,1},{1,0},{2,3},{3,2},{4,5},{5,4},{6,7},{7,6},{8,9},{9,8},{10,11... | collective-permute-start | bytes 1179656 | tf_op jit(solution)/shard_map/ppermute | solution.py:501
  105.4 9.0 %collective-permute-start.9 = (bf16[2,12,64,128]{3,2,1,0:T(8,128)(2,1)}, bf16[2,12,64,128]{3,2,1,0:T(8,128)(2,1)S(1)}, u32[]{:S(2)}, u32[]{:S(2)}) collective-permute-start(bf16[2,12,64,128]{3,2,1,0:T(8,128)(2,1)} %get-tuple-element.41), channel_id=1, source_target_pairs={{0,1},{1,0},{2,3},{3,2},{4,5},{5,4},{6,7},{7,6},{8,9},{9,8},{10,11... | collective-permute-start | bytes 1179656 | tf_op jit(solution)/shard_map/ppermute | solution.py:501
